TPU v7x, 256 devices: a whole 4x4x8 slice. The times are simulated.
256 devices in a mesh: sn: 64 (over z, y, core), rhs: 4 (over x).
Axes of the slice: x: 4, y: 4, z: 8, core: 2. Of those that a mesh axis runs over, the one named last changes fastest.
Arguments:
- right_sides: float32 [4, 4096, 128], P(None, 'sn', 'rhs'), may hold values from -6 to 6
- factor_below: bfloat16 [3, 4096, 4096], P(None, 'sn', 'rhs'), may hold values from -0.09375 to 0.09375
- row_blocks: int32 [3, 32, 32], replicated, may hold values from 0 to 95, as said below
- inverse_top: bfloat16 [4096, 4096], P('sn'), as said below
- inverse_second: bfloat16 [4096, 2048], P('sn'), as said below
- inverse_third: bfloat16 [4096, 1024], P('sn'), as said below
- inverse_fourth: bfloat16 [4096, 512], P('sn'), as said below
Outputs:
- solution: float32 [4, 4096, 128], P(None, 'sn', 'rhs')
Inputs may be any that keep to these rules, and one draw needn't show every extreme that they name: `row_blocks`: each level-l block lists 32 distinct global blocks of the ancestors of its supernode in the binary tree (supernode s of level l has parent s // 2 of level l - 1), in any order, always including all blocks of its parent; all blocks of one supernode list the same; at level 1 they are the 32 root blocks. `inverse_top`: each supernode's block is zero below its diagonal. `inverse_second`: each supernode's block is zero below its diagonal. `inverse_third`: each supernode's block is zero below its diagonal. `inverse_fourth`: each supernode's block is zero below its diagonal.
All inputs are finite; a program needn't handle non-finite values.
Results may differ from a plain program's by a relative error of at most 0.02.
Values may be sent and summed in bfloat16 or wider, within the bound.
No kernel may reach another device: no remote copies, remote signals or barrier semaphores. Data moves between devices by JAX's collectives and lax.ppermute only.
A program may use at most 64 MiB of HBM per device.

v0:
```python
import jax
import jax.numpy as jnp
from jax import lax
from jax.sharding import PartitionSpec as P

BS = 128
NB = 32
LEVELS = 4
RB = 32


def on_device(
    right_sides,
    factor_below,
    row_blocks,
    inverse_top,
    inverse_second,
    inverse_third,
    inverse_fourth,
):
    inverses = (inverse_top, inverse_second, inverse_third, inverse_fourth)
    rows_dev = right_sides.shape[1]
    columns = right_sides.shape[2]
    groups = lax.axis_size("rhs")
    devices = lax.axis_size("sn")
    level_rows = rows_dev * devices
    total_cols = columns * groups
    quarter = RB // groups
    own_index = lax.axis_index("sn")
    column_group = lax.axis_index("rhs")
    solved = []
    outputs = []
    for tier_index in range(LEVELS):
        if tier_index == 0:
            update = right_sides[0]
        else:
            first_block = own_index * rows_dev // BS
            chosen = lax.dynamic_index_in_dim(
                row_blocks[tier_index - 1], first_block, 0, keepdims=False
            )
            my_blocks = lax.dynamic_slice_in_dim(chosen, column_group * quarter, quarter, 0)
            known = jnp.concatenate(solved, axis=0).reshape(tier_index * NB, BS, total_cols)
            picked = jnp.take(known, my_blocks, axis=0).reshape(quarter * BS, total_cols)
            below = factor_below[tier_index - 1]
            summed = lax.psum_scatter(
                lax.dot_general(
                    picked, below, (((0,), (1,)), ((), ())), preferred_element_type=jnp.float32
                ).astype(jnp.bfloat16),
                "rhs",
                scatter_dimension=0,
                tiled=True,
            ).astype(jnp.float32)
            update = right_sides[tier_index] - summed.T
        rounded = update.astype(jnp.bfloat16)
        super_width = level_rows // 2**tier_index
        gathered = lax.all_gather(rounded, "sn", axis=0, tiled=True)
        row_start = own_index * rows_dev // super_width * super_width
        block_rows = lax.dynamic_slice_in_dim(gathered, row_start, super_width, 0)
        result = jnp.dot(inverses[tier_index], block_rows, preferred_element_type=jnp.float32)
        outputs.append(result)
        if tier_index + 1 < LEVELS:
            packed = result.astype(jnp.bfloat16)
            all_columns = lax.all_gather(packed, "rhs", axis=1, tiled=True)
            assembled = lax.all_gather(all_columns, "sn", axis=0, tiled=True)
            solved.append(assembled)
    return jnp.stack(outputs)


def solution(mesh):
    in_specs = (
        P(None, "sn", "rhs"),
        P(None, "sn", "rhs"),
        P(),
        P("sn", None),
        P("sn", None),
        P("sn", None),
        P("sn", None),
    )
    out_specs = P(None, "sn", "rhs")
    return jax.shard_map(
        on_device, mesh=mesh, in_specs=in_specs, out_specs=out_specs, check_vma=False
    )
```

profile of v0, /device:TPU:1, one launch (start us, length us, event | category | flops | bytes accessed | tf_op | source)
XLA Modules:
  0.0 578.2 jit_solution(9210336132383737632)
XLA Ops:
  6.5 0.8 slice.70
  7.3 0.1 copy.29
  7.4 0.0 copy-start.7
  7.4 55.6 %all-gather = bf16[1,4096,32]{2,0,1:T(2,128)(2,1)S(1)} all-gather(bf16[1,64,32]{2,0,1:T(2,128)(2,1)S(1)} %copy.29), channel_id=2, replica_groups=mesh['sn'=64,'rhs'=4] {'sn'}, dimensions={1}, use_global_device_ids=true | all-gather | bytes 266240 | tf_op jit(solution)/shard_map/all_gather | solution.py:56
  63.0 2.1 copy.30
  65.1 0.3 fusion.26
  65.4 9.6 %all_gather.31 = bf16[64,128]{0,1:T(8,128)(2,1)S(1)} all-gather(bf16[64,32]{0,1:T(8,128)(2,1)S(1)} %get-tuple-element.8), channel_id=1, replica_groups=mesh['sn'=64,'rhs'=4] {'rhs'}, dimensions={1}, use_global_device_ids=true | all-gather | bytes 20480 | tf_op jit(solution)/shard_map/all_gather | solution.py:63
  74.9 0.7 copy.31
  75.6 0.0 all-gather.8.cloned.1.call-update
  75.7 0.0 reduce-scatter.4.cloned.1.call-start
  75.8 0.1 fusion.22
  75.9 0.1 compare_and_fusion.2
  75.9 75.8 %all-gather.8.cloned.1.call-done = bf16[4096,128]{1,0:T(8,128)(2,1)} async-done(((bf16[64,128]{1,0:T(8,128)(2,1)}), bf16[4096,128]{1,0:T(8,128)(2,1)}) %all-gather.8.cloned.1.call-update) | async-done | bytes 1048592 | tf_op jit(solution)/shard_map/all_gather | solution.py:64
  151.8 1.9 gather_fusion
  153.7 0.1 broadcast_select_fusion.2
  153.8 1.8 convolution_convert_fusion.2
  155.6 0.0 reduce-scatter.4.cloned.1.call-update
  155.6 0.0 all-gather.10.cloned.1.call-start
  155.7 17.9 %reduce-scatter.4.cloned.1.call-done = bf16[32,64]{1,0:T(8,128)(2,1)} async-done(((bf16[128,64]{1,0:T(8,128)(2,1)}), bf16[32,64]{1,0:T(8,128)(2,1)}) %reduce-scatter.4.cloned.1.call-update) | async-done | bytes 4112 | tf_op jit(solution)/shard_map/reduce_scatter | solution.py:45
  173.5 0.0 copy-done.7
  173.5 0.7 fusion.16
  174.3 53.8 %all-gather.1 = bf16[64,64,32]{1,2,0:T(8,128)(2,1)S(1)} all-gather(bf16[1,64,32]{1,2,0:T(8,128)(2,1)S(1)} %fusion.16), channel_id=1, replica_groups=mesh['sn'=64,'rhs'=4] {'sn'}, dimensions={0}, use_global_device_ids=true | all-gather | bytes 266240 | tf_op jit(solution)/shard_map/all_gather | solution.py:56
  228.1 0.2 copy.32
  228.3 0.5 reshape.249
  228.7 0.0 copy-done.3
  228.7 0.8 bitcast_convert_fusion.1
  229.5 9.0 %all_gather.34 = bf16[64,128]{0,1:T(8,128)(2,1)S(1)} all-gather(bf16[64,32]{0,1:T(8,128)(2,1)S(1)} %get-tuple-element.10), channel_id=1, replica_groups=mesh['sn'=64,'rhs'=4] {'rhs'}, dimensions={1}, use_global_device_ids=true | all-gather | bytes 20480 | tf_op jit(solution)/shard_map/all_gather | solution.py:63
  238.5 0.7 copy.33
  239.2 0.0 all-gather.10.cloned.1.call-update
  239.3 0.0 reduce-scatter.6.cloned.1.call-start
  239.3 0.1 fusion.23
  239.4 0.7 compare_and_fusion
  240.1 75.3 %all-gather.10.cloned.1.call-done = bf16[4096,128]{1,0:T(8,128)(2,1)} async-done(((bf16[64,128]{1,0:T(8,128)(2,1)}), bf16[4096,128]{1,0:T(8,128)(2,1)}) %all-gather.10.cloned.1.call-update) | async-done | bytes 1048592 | tf_op jit(solution)/shard_map/all_gather | solution.py:64
  315.4 0.0 copy-done.1
  315.4 2.7 pad_maximum_fusion.1
  318.1 2.3 gather_fusion.1
  320.4 0.1 broadcast_select_fusion.1
  320.4 1.8 convolution_convert_fusion.1
  322.2 0.0 reduce-scatter.6.cloned.1.call-update
  322.3 0.0 all-gather.12.cloned.1.call-start
  322.3 17.9 %reduce-scatter.6.cloned.1.call-done = bf16[32,64]{1,0:T(8,128)(2,1)} async-done(((bf16[128,64]{1,0:T(8,128)(2,1)}), bf16[32,64]{1,0:T(8,128)(2,1)}) %reduce-scatter.6.cloned.1.call-update) | async-done | bytes 4112 | tf_op jit(solution)/shard_map/reduce_scatter | solution.py:45
  340.2 0.7 fusion.17
  340.9 53.8 %all-gather.2 = bf16[64,64,32]{1,2,0:T(8,128)(2,1)S(1)} all-gather(bf16[1,64,32]{1,2,0:T(8,128)(2,1)S(1)} %fusion.17), channel_id=1, replica_groups=mesh['sn'=64,'rhs'=4] {'sn'}, dimensions={0}, use_global_device_ids=true | all-gather | bytes 266240 | tf_op jit(solution)/shard_map/all_gather | solution.py:56
  394.7 0.2 copy.34
  394.9 0.5 reshape.251
  395.4 0.1 bitcast_convert_fusion
  395.6 9.0 %all_gather.37 = bf16[64,128]{0,1:T(8,128)(2,1)S(1)} all-gather(bf16[64,32]{0,1:T(8,128)(2,1)S(1)} %get-tuple-element.12), channel_id=1, replica_groups=mesh['sn'=64,'rhs'=4] {'rhs'}, dimensions={1}, use_global_device_ids=true | all-gather | bytes 20480 | tf_op jit(solution)/shard_map/all_gather | solution.py:63
  404.6 0.7 copy.35
  405.3 0.0 all-gather.12.cloned.1.call-update
  405.3 0.2 reduce-scatter.8.cloned.1.call-start
  405.5 0.8 fusion.24
  406.3 75.1 %all-gather.12.cloned.1.call-done = bf16[4096,128]{1,0:T(8,128)(2,1)} async-done(((bf16[64,128]{1,0:T(8,128)(2,1)}), bf16[4096,128]{1,0:T(8,128)(2,1)}) %all-gather.12.cloned.1.call-update) | async-done | bytes 1048592 | tf_op jit(solution)/shard_map/all_gather | solution.py:64
  481.4 11.6 %pad_maximum_fusion = bf16[12288,128]{1,0:T(8,128)(2,1)} fusion(bf16[4096,128]{1,0:T(8,128)(2,1)} %all-gather.12.cloned.1.call-done, bf16[4096,128]{1,0:T(8,128)(2,1)S(1)} %copy-done.2, bf16[4096,128]{1,0:T(8,128)(2,1)S(1)} %copy-done.1), kind=kLoop, calls=%fused_computation.3 | loop fusion | flops 9437184 | bytes 6291456 | tf_op jit(solution)/shard_map/concatenate | solution.py:42
  493.0 2.5 gather_fusion.2
  495.5 0.1 broadcast_select_fusion
  495.6 1.8 convolution_convert_fusion
  497.4 0.0 reduce-scatter.8.cloned.1.call-update
  497.5 17.9 %reduce-scatter.8.cloned.1.call-done = bf16[32,64]{1,0:T(8,128)(2,1)} async-done(((bf16[128,64]{1,0:T(8,128)(2,1)}), bf16[32,64]{1,0:T(8,128)(2,1)}) %reduce-scatter.8.cloned.1.call-update) | async-done | bytes 4112 | tf_op jit(solution)/shard_map/reduce_scatter | solution.py:45
  515.4 0.7 fusion.18
  516.1 53.8 %all-gather.3 = bf16[64,64,32]{1,2,0:T(8,128)(2,1)S(1)} all-gather(bf16[1,64,32]{1,2,0:T(8,128)(2,1)S(1)} %fusion.18), channel_id=1, replica_groups=mesh['sn'=64,'rhs'=4] {'sn'}, dimensions={0}, use_global_device_ids=true | all-gather | bytes 266240 | tf_op jit(solution)/shard_map/all_gather | solution.py:56
  569.9 0.2 copy.36
  570.1 0.5 reshape.253
  570.6 0.1 convolution_bitcast_fusion
  570.7 0.6 pad_maximum_fusion.2
  (23 shorter events, 0.1 us)
Async XLA Ops:
  6.5 58.5 %copy-start = (bf16[64,4096]{1,0:T(8,128)(2,1)S(1)}, bf16[64,4096]{1,0:T(8,128)(2,1)}, u32[]{:S(2)}) copy-start(bf16[64,4096]{1,0:T(8,128)(2,1)} %param.10) | copy-start | bytes 1572868
  6.5 69.2 %copy-start.8 = (s32[3,32,32]{2,1,0:T(8,128)S(1)}, s32[3,32,32]{2,1,0:T(8,128)}, u32[]{:S(2)}) copy-start(s32[3,32,32]{2,1,0:T(8,128)} %param.9) | copy-start | bytes 36868
  6.5 145.2 %all-gather.8.cloned.1.call-start = ((), (), s32[]{:S(2)}) async-start(), calls=%async_computation.3 | async-start | bytes 1064960 | tf_op jit(solution)/shard_map/all_gather | solution.py:64
  7.4 166.1 %copy-start.7 = (f32[4,64,32]{1,2,0:T(8,128)S(1)}, f32[4,64,32]{1,2,0:T(8,128)}, u32[]{:S(2)}) copy-start(f32[4,64,32]{1,2,0:T(8,128)} %param.7) | copy-start | bytes 98308
  63.0 165.7 %copy-start.3 = (bf16[64,2048]{1,0:T(8,128)(2,1)S(1)}, bf16[64,2048]{1,0:T(8,128)(2,1)}, u32[]{:S(2)}) copy-start(bf16[64,2048]{1,0:T(8,128)(2,1)} %param.11) | copy-start | bytes 786436
  75.7 97.9 %reduce-scatter.4.cloned.1.call-start = ((), (), s32[]{:S(2)}) async-start(), calls=%async_computation.4 | async-start | bytes 40960 | tf_op jit(solution)/shard_map/reduce_scatter | solution.py:45
  75.8 242.3 %copy-start.9 = (s32[1,32,32]{2,1,0:T(8,128)}, s32[1,32,32]{2,1,0:T(8,128)S(1)}, u32[]{:S(2)}) copy-start(s32[1,32,32]{2,1,0:T(8,128)S(1)} %get-tuple-element.5) | copy-start | bytes 12292
  151.8 163.6 %copy-start.1 = (bf16[4096,128]{1,0:T(8,128)(2,1)S(1)}, bf16[4096,128]{1,0:T(8,128)(2,1)}, u32[]{:S(2)}) copy-start(bf16[4096,128]{1,0:T(8,128)(2,1)} %all-gather.8.cloned.1.call-done) | copy-start | bytes 3145732
  155.6 159.8 %all-gather.10.cloned.1.call-start = ((), (), s32[]{:S(2)}) async-start(), calls=%async_computation.5 | async-start | bytes 1064960 | tf_op jit(solution)/shard_map/all_gather | solution.py:64
  239.3 101.0 %reduce-scatter.6.cloned.1.call-start = ((), (), s32[]{:S(2)}) async-start(), calls=%async_computation.6 | async-start | bytes 40960 | tf_op jit(solution)/shard_map/reduce_scatter | solution.py:45
  240.1 155.3 %copy-start.4 = (bf16[64,1024]{1,0:T(8,128)(2,1)S(1)}, bf16[64,1024]{1,0:T(8,128)(2,1)}, u32[]{:S(2)}) copy-start(bf16[64,1024]{1,0:T(8,128)(2,1)} %param.12) | copy-start | bytes 393220
  318.1 163.3 %copy-start.2 = (bf16[4096,128]{1,0:T(8,128)(2,1)S(1)}, bf16[4096,128]{1,0:T(8,128)(2,1)}, u32[]{:S(2)}) copy-start(bf16[4096,128]{1,0:T(8,128)(2,1)} %all-gather.10.cloned.1.call-done) | copy-start | bytes 3145732
  322.3 159.1 %all-gather.12.cloned.1.call-start = ((), (), s32[]{:S(2)}) async-start(), calls=%async_computation.7 | async-start | bytes 1064960 | tf_op jit(solution)/shard_map/all_gather | solution.py:64
  405.3 110.1 %reduce-scatter.8.cloned.1.call-start = ((), (), s32[]{:S(2)}) async-start(), calls=%async_computation.8 | async-start | bytes 40960 | tf_op jit(solution)/shard_map/reduce_scatter | solution.py:45
  406.3 89.2 %copy-start.10 = (pred[8]{0:T(512)(128)(4,1)S(1)}, pred[8]{0:T(512)(128)(4,1)}, u32[]{:S(2)}) copy-start(pred[8]{0:T(512)(128)(4,1)} %get-tuple-element.14) | copy-start | bytes 28
  493.0 77.6 %copy-start.5 = (bf16[64,512]{1,0:T(8,128)(2,1)S(1)}, bf16[64,512]{1,0:T(8,128)(2,1)}, u32[]{:S(2)}) copy-start(bf16[64,512]{1,0:T(8,128)(2,1)} %param.13) | copy-start | bytes 196612
  493.0 77.8 %copy-start.6 = (f32[32,64]{1,0:T(8,128)S(1)}, f32[32,64]{1,0:T(8,128)}, u32[]{:S(2)}) copy-start(f32[32,64]{1,0:T(8,128)} %get-tuple-element.11) | copy-start | bytes 24580
Sparse Core Ops, SparseCore 0:
  75.8 75.9 all-gather.7
  155.7 17.7 reduce-scatter.3
  239.4 75.9 all-gather.9
  322.4 17.7 reduce-scatter.5
  405.4 75.9 all-gather.11
  497.6 17.7 reduce-scatter.7
where the time goes:
time: 579 us; the launch traced here: 578 us
  waiting for transfers between devices  280 us (48%)
  blocking collectives  245 us (42%)
  other arithmetic  19 us (3%)
  local copies, waits for them, and re-layouts  13.8 us (2%)
  between operations  13.7 us (2%)
  matrix products  6.73 us (1%)
    all_gather x3, waiting for transfers between devices, on_device(): assembled = lax.all_gather(all_columns, 'sn', axis=0, tiled=True)  226 us
    all_gather x4, blocking collectives, on_device(): gathered = lax.all_gather(rounded, 'sn', axis=0, tiled=True)  217 us
    reduce_scatter x3, waiting for transfers between devices, on_device(): lax.psum_scatter(lax.dot_general(picked, below, (((0,), (1,)), ((), ())),...  53.7 us
    all_gather x3, blocking collectives, on_device(): all_columns = lax.all_gather(packed, 'rhs', axis=1, tiled=True)  27.6 us
    concatenate x2, other arithmetic, on_device(): jnp.concatenate(solved, axis=0).reshape(tier_index * NB, BS, total_cols)  14.3 us
  transfers between devices with their start and end apart: 6, of which 6 were waited for; matrix products, arithmetic and copies ran while one was open for 0% of the time, Pallas kernels for 0%

commit v1 on v0

v1 whole, which is shorter than its diff:
```python
import functools

import jax
import jax.numpy as jnp
from jax import lax
from jax.experimental import pallas as pl
from jax.experimental.pallas import tpu as pltpu
from jax.sharding import PartitionSpec as P

BS = 128
NB = 32
LEVELS = 4
RB = 32


def pack(block, copies):
    flipped = block.T
    half = flipped.shape[0] // 2
    packed = jnp.concatenate((flipped[:half], flipped[half:]), axis=1).astype(jnp.bfloat16)
    return jnp.broadcast_to(packed[None], (copies, *packed.shape))


def unpack(gathered, store):
    lanes = gathered.shape[2] // 2
    for b in range(gathered.shape[0] // 2):
        one, two = gathered[2 * b], gathered[2 * b + 1]
        top = jnp.concatenate((one[:, :lanes], two[:, :lanes]), axis=1)
        low = jnp.concatenate((one[:, lanes:], two[:, lanes:]), axis=1)
        store(b, jnp.concatenate((top, low), axis=0))


def dot_lanes(a, b):
    return lax.dot_general(a, b, (((1,), (1,)), ((), ())), preferred_element_type=jnp.float32)


def start_kernel(right_ref, message_ref):
    message_ref[...] = pack(right_ref[0], message_ref.shape[0])


def solve_kernel(gathered_ref, inverse_ref, result_ref, message_ref, flat_ref):
    def store(b, block):
        flat_ref[:, b * BS : (b + 1) * BS] = block

    unpack(gathered_ref, store)
    result = dot_lanes(inverse_ref[...], flat_ref[...])
    result_ref[...] = result
    message_ref[...] = pack(result, message_ref.shape[0])


def final_kernel(gathered_ref, inverse_ref, *refs):
    earlier, (out_ref, flat_ref) = refs[:-2], refs[-2:]

    def store(b, block):
        flat_ref[:, b * BS : (b + 1) * BS] = block

    unpack(gathered_ref, store)
    for l, ref in enumerate(earlier):
        out_ref[l] = ref[...]
    out_ref[len(earlier)] = dot_lanes(inverse_ref[...], flat_ref[...])


def update_kernel(tier, last, index_ref, gathered_ref, below_ref, right_ref, *refs):
    earlier = refs[: tier - 1]
    message_ref = refs[tier - 1]
    flat_ref, known_ref = refs[-2], refs[-1]
    base = 0
    for ref in earlier:
        known_ref[base : base + ref.shape[0]] = ref[...]
        base += ref.shape[0]
    first = base

    def store(b, block):
        known_ref[first + b] = block

    unpack(gathered_ref, store)
    if not last:
        kept_ref = refs[tier]
        kept_ref[...] = known_ref[first:]
    for p in range(RB):
        flat_ref[:, p * BS : (p + 1) * BS] = known_ref[index_ref[0, p]]
    groups, _, width = below_ref.shape
    total = right_ref[tier]
    for q in range(groups):
        total = total - dot_lanes(below_ref[q], flat_ref[:, q * width : (q + 1) * width])
    message_ref[...] = pack(total, message_ref.shape[0])


VMEM = pl.BlockSpec(memory_space=pltpu.VMEM)
SMEM = pl.BlockSpec(memory_space=pltpu.SMEM)


def call(kernel, name, outs, scratch, *args, smem=0):
    return pl.pallas_call(
        kernel,
        out_shape=outs,
        in_specs=[SMEM] * smem + [VMEM] * (len(args) - smem),
        out_specs=[VMEM] * len(outs),
        scratch_shapes=scratch,
        cost_estimate=pl.CostEstimate(flops=20_000_000, bytes_accessed=1_000_000, transcendentals=0),
        compiler_params=pltpu.CompilerParams(vmem_limit_bytes=16 * 2**20),
        name=name,
    )(*args)


def on_device(
    right_sides,
    factor_below,
    row_blocks,
    inverse_top,
    inverse_second,
    inverse_third,
    inverse_fourth,
):
    inverses = (inverse_top, inverse_second, inverse_third, inverse_fourth)
    _, rows, columns = right_sides.shape
    devices = lax.axis_size("sn")
    own = lax.axis_index("sn")
    f32, bf16 = jnp.float32, jnp.bfloat16
    shape = jax.ShapeDtypeStruct
    message = (columns // 2, 2 * rows)
    members = [devices >> l for l in range(LEVELS)]

    def gather(copies):
        n = copies.shape[0]
        groups = None
        if n < devices:
            groups = [list(range(s, s + n)) for s in range(0, devices, n)]
        return lax.all_to_all(copies, "sn", 0, 0, axis_index_groups=groups)

    below = [lax.all_gather(factor_below[t], "rhs") for t in range(LEVELS - 1)]
    chosen = lax.dynamic_index_in_dim(row_blocks, own * rows // BS, 1, keepdims=False)
    places = chosen
    base = NB
    for l in range(1, LEVELS - 1):
        count = NB >> l
        mine = own * rows // BS // count * count
        places = jnp.where(chosen // NB == l, chosen - l * NB - mine + base, places)
        base += count

    (copies,) = call(start_kernel, "start", [shape((members[0], *message), bf16)], [], right_sides)
    known = []
    results = []
    for l in range(LEVELS):
        width = members[l] * rows
        gathered = gather(copies)
        flat = pltpu.VMEM((columns, width), bf16)
        if l == LEVELS - 1:
            (out,) = call(
                final_kernel,
                "final",
                [shape((LEVELS, rows, columns), f32)],
                [flat],
                gathered,
                inverses[l],
                *results,
            )
            return out
        result, copies = call(
            solve_kernel,
            f"solve{l}",
            [shape((rows, columns), f32), shape((members[l], *message), bf16)],
            [flat],
            gathered,
            inverses[l],
        )
        results.append(result)
        gathered = gather(copies)
        tier = l + 1
        last = tier == LEVELS - 1
        blocks = sum(NB >> k for k in range(tier))
        outs = [shape((members[tier], *message), bf16)]
        if not last:
            outs.append(shape((NB >> l, columns, BS), bf16))
        got = call(
            functools.partial(update_kernel, tier, last),
            f"update{tier}",
            outs,
            [pltpu.VMEM((columns, RB * BS), bf16), pltpu.VMEM((blocks, columns, BS), bf16)],
            places[l][None],
            gathered,
            below[l],
            right_sides,
            *known,
            smem=1,
        )
        copies = got[0]
        known.extend(got[1:])


def solution(mesh):
    in_specs = (
        P(None, "sn", "rhs"),
        P(None, "sn", "rhs"),
        P(),
        P("sn", None),
        P("sn", None),
        P("sn", None),
        P("sn", None),
    )
    out_specs = P(None, "sn", "rhs")
    return jax.shard_map(
        on_device, mesh=mesh, in_specs=in_specs, out_specs=out_specs, check_vma=False
    )
```

time: 579 us -> 128 us (0.22)
  waiting for transfers between devices: 280 us -> 14.7 us
  blocking collectives: 245 us -> 71.4 us
  starting transfers between devices: 0.39 us -> 31.4 us
  other arithmetic: 19 us -> 0.01 us
  between operations: 13.7 us -> 0.17 us
  local copies, waits for them, and re-layouts: 13.8 us -> 1.74 us
  Pallas kernels: 0 us -> 7.56 us
  matrix products: 6.73 us -> 0 us
    all_gather x3 -> x0, waiting for transfers between devices: 226 us -> none  [on_device(): assembled = lax.all_gather(all_columns, 'sn', axis=0, tiled=True)]
    all_gather x7 -> x3, blocking collectives: 245 us -> 34 us  [on_device(): below = [lax.all_gather(factor_below[t], 'rhs') for t in range(LEVELS - 1)]]
    reduce_scatter x3 -> x0, waiting for transfers between devices: 53.7 us -> none  [on_device(): lax.psum_scatter(lax.dot_general(picked, below, (((0,), (1,)), ((), ())),...]
    all_to_all x0 -> x3, blocking collectives: none -> 37.4 us  [gather(): return lax.all_to_all(copies, 'sn', 0, 0, axis_index_groups=groups)]
    all_to_all x0 -> x4, starting transfers between devices: none -> 31.4 us  [gather(): return lax.all_to_all(copies, 'sn', 0, 0, axis_index_groups=groups)]
    all_to_all x0 -> x4, waiting for transfers between devices: none -> 14.7 us  [gather(): return lax.all_to_all(copies, 'sn', 0, 0, axis_index_groups=groups)]
    concatenate x2 -> x0, other arithmetic: 14.3 us -> none  [on_device(): jnp.concatenate(solved, axis=0).reshape(tier_index * NB, BS, total_cols)]
    pallas_call x0 -> x8, Pallas kernels: none -> 7.56 us  [call(): pl.pallas_call(kernel, out_shape=outs, in_specs=[SMEM] * smem + [VMEM] *...]
  transfers between devices with their start and end apart: 6 -> 4, of which waited for: 6 -> 2; matrix products, arithmetic and copies ran while one was open for 0% -> 0% of each run, Pallas kernels for 0% -> 0%
where the time goes in v1:
time: 128 us; the launch traced here: 127 us
  blocking collectives  71.4 us (56%)
  starting transfers between devices  31.4 us (25%)
  waiting for transfers between devices  14.7 us (11%)
  Pallas kernels  7.56 us (6%)
  local copies, waits for them, and re-layouts  1.74 us (1%)
    all_to_all x3, blocking collectives, gather(): return lax.all_to_all(copies, 'sn', 0, 0, axis_index_groups=groups)  37.4 us
    all_gather x3, blocking collectives, on_device(): below = [lax.all_gather(factor_below[t], 'rhs') for t in range(LEVELS - 1)]  34 us
    all_to_all x4, starting transfers between devices, gather(): return lax.all_to_all(copies, 'sn', 0, 0, axis_index_groups=groups)  31.4 us
    all_to_all x4, waiting for transfers between devices, gather(): return lax.all_to_all(copies, 'sn', 0, 0, axis_index_groups=groups)  14.7 us
    pallas_call x8, Pallas kernels, call(): pl.pallas_call(kernel, out_shape=outs, in_specs=[SMEM] * smem + [VMEM] *...  7.56 us
  transfers between devices with their start and end apart: 4, of which 2 were waited for; matrix products, arithmetic and copies ran while one was open for 0% of the time, Pallas kernels for 0%

profile of v1, /device:TPU:1, one launch (start us, length us, event | category | flops | bytes accessed | tf_op | source)
XLA Modules:
  0.0 127.0 jit_solution(5954057874577300329)
XLA Ops:
  0.0 0.0 copy-start
  0.0 0.9 copy.18.right_ref
  1.0 0.9 start.1
  1.8 0.0 copy-start.5
  1.8 13.3 %all-to-all-start = ((bf16[64,16,128]{2,1,0:T(8,128)(2,1)}), bf16[64,16,128]{2,1,0:T(8,128)(2,1)S(1)}, u32[]{:S(2)}, u32[]{:S(2)}) async-start(bf16[64,16,128]{2,1,0:T(8,128)(2,1)} %start.1), calls=%async_computation | async-start | bytes 524288 | tf_op jit(solution)/shard_map/all_to_all | solution.py:128
  15.2 0.0 copy-done.5
  15.2 0.0 copy-start.1
  15.2 11.5 %all_gather.9.below_ref = bf16[4,64,1024]{2,1,0:T(8,128)(2,1)S(1)} all-gather(bf16[1,64,1024]{2,1,0:T(8,128)(2,1)S(1)} %get-tuple-element.26), channel_id=1, replica_groups=mesh['sn'=64,'rhs'=4] {'rhs'}, dimensions={0}, use_global_device_ids=true | all-gather | bytes 655360 | tf_op jit(solution)/shard_map/all_gather | solution.py:130
  26.7 1.6 %all-to-all-done.gathered_ref = bf16[64,16,128]{2,1,0:T(8,128)(2,1)S(1)} async-done(((bf16[64,16,128]{2,1,0:T(8,128)(2,1)}), bf16[64,16,128]{2,1,0:T(8,128)(2,1)S(1)}, u32[]{:S(2)}, u32[]{:S(2)}) %all-to-all-start) | async-done | bytes 262176 | tf_op jit(solution)/shard_map/all_to_all | solution.py:128
  28.3 0.0 copy-done.1
  28.3 1.2 solve0.1
  29.5 10.5 %all-to-all-start.1 = ((bf16[64,16,128]{2,1,0:T(8,128)(2,1)}), bf16[64,16,128]{2,1,0:T(8,128)(2,1)S(1)}, u32[]{:S(2)}, u32[]{:S(2)}) async-start(bf16[64,16,128]{2,1,0:T(8,128)(2,1)} %get-tuple-element.15), calls=%async_computation.1 | async-start | bytes 524288 | tf_op jit(solution)/shard_map/all_to_all | solution.py:128
  40.0 0.0 copy-done
  40.1 13.1 %all-to-all-done.1.gathered_ref = bf16[64,16,128]{2,1,0:T(8,128)(2,1)S(1)} async-done(((bf16[64,16,128]{2,1,0:T(8,128)(2,1)}), bf16[64,16,128]{2,1,0:T(8,128)(2,1)S(1)}, u32[]{:S(2)}, u32[]{:S(2)}) %all-to-all-start.1) | async-done | bytes 262176 | tf_op jit(solution)/shard_map/all_to_all | solution.py:128
  53.2 1.1 update1.1
  54.3 0.0 copy-start.2
  54.3 12.8 %all_to_all.35.gathered_ref = bf16[32,16,128]{2,1,0:T(8,128)(2,1)S(1)} all-to-all(bf16[32,16,128]{2,1,0:T(8,128)(2,1)S(1)} %get-tuple-element.16), channel_id=1, replica_groups={{0,4,8,12,16,20,24,28,32,36,40,44,48,52,56,60,64,68,72,76,80,84,88,92,9..., dimensions={0} | all-to-all | bytes 262144 | tf_op jit(solution)/shard_map/all_to_all | solution.py:128
  67.1 0.0 copy-done.2
  67.1 1.1 solve1.1
  68.2 3.9 %all-to-all-start.3 = ((bf16[32,16,128]{2,1,0:T(8,128)(2,1)}), bf16[32,16,128]{2,1,0:T(8,128)(2,1)S(1)}, u32[]{:S(2)}, u32[]{:S(2)}) async-start(bf16[32,16,128]{2,1,0:T(8,128)(2,1)} %get-tuple-element.17), calls=%async_computation.3 | async-start | bytes 262144 | tf_op jit(solution)/shard_map/all_to_all | solution.py:128
  72.1 10.9 %all_gather.10.below_ref = bf16[4,64,1024]{2,1,0:T(8,128)(2,1)S(1)} all-gather(bf16[1,64,1024]{2,1,0:T(8,128)(2,1)S(1)} %get-tuple-element.27), channel_id=1, replica_groups=mesh['sn'=64,'rhs'=4] {'rhs'}, dimensions={0}, use_global_device_ids=true | all-gather | bytes 655360 | tf_op jit(solution)/shard_map/all_gather | solution.py:130
  83.0 0.0 all-to-all-done.3.gathered_ref
  83.0 1.0 update2.1
  84.0 0.0 copy-start.3
  84.0 13.5 %all_to_all.36.gathered_ref = bf16[16,16,128]{2,1,0:T(8,128)(2,1)S(1)} all-to-all(bf16[16,16,128]{2,1,0:T(8,128)(2,1)S(1)} %get-tuple-element.19), channel_id=1, replica_groups={{0,4,8,12,16,20,24,28,32,36,40,44,48,52,56,60},{64,68,72,76,80,84,88,92..., dimensions={0} | all-to-all | bytes 131072 | tf_op jit(solution)/shard_map/all_to_all | solution.py:128
  97.5 0.0 copy-done.3
  97.5 1.0 solve2.1
  98.5 3.7 %all-to-all-start.5 = ((bf16[16,16,128]{2,1,0:T(8,128)(2,1)}), bf16[16,16,128]{2,1,0:T(8,128)(2,1)S(1)}, u32[]{:S(2)}, u32[]{:S(2)}) async-start(bf16[16,16,128]{2,1,0:T(8,128)(2,1)} %get-tuple-element.20), calls=%async_computation.5 | async-start | bytes 131072 | tf_op jit(solution)/shard_map/all_to_all | solution.py:128
  102.3 11.7 %all_gather.11.below_ref = bf16[4,64,1024]{2,1,0:T(8,128)(2,1)S(1)} all-gather(bf16[1,64,1024]{2,1,0:T(8,128)(2,1)S(1)} %get-tuple-element.25), channel_id=1, replica_groups=mesh['sn'=64,'rhs'=4] {'rhs'}, dimensions={0}, use_global_device_ids=true | all-gather | bytes 655360 | tf_op jit(solution)/shard_map/all_gather | solution.py:130
  113.9 0.0 all-to-all-done.5.gathered_ref
  113.9 1.0 update3.1
  114.9 0.0 copy-start.4
  114.9 11.1 %all_to_all.37.gathered_ref = bf16[8,16,128]{2,1,0:T(8,128)(2,1)S(1)} all-to-all(bf16[8,16,128]{2,1,0:T(8,128)(2,1)S(1)} %update3.1), channel_id=1, replica_groups={{0,4,8,12,16,20,24,28},{32,36,40,44,48,52,56,60},{64,68,72,76,80,84,88,..., dimensions={0} | all-to-all | bytes 65536 | tf_op jit(solution)/shard_map/all_to_all | solution.py:128
  126.1 0.0 copy-done.4
  126.1 0.2 final.1
  126.3 0.7 copy.22
  (4 shorter events, 0.1 us)
Async XLA Ops:
  0.0 40.0 %copy-start = (s32[3,32,32]{2,1,0:T(8,128)S(1)}, s32[3,32,32]{2,1,0:T(8,128)}, u32[]{:S(2)}) copy-start(s32[3,32,32]{2,1,0:T(8,128)} %param.9) | copy-start | bytes 36868
  1.8 13.3 %copy-start.5 = (bf16[3,64,1024]{2,1,0:T(8,128)(2,1)S(1)}, bf16[3,64,1024]{2,1,0:T(8,128)(2,1)}, u32[]{:S(2)}) copy-start(bf16[3,64,1024]{2,1,0:T(8,128)(2,1)} %param.8) | copy-start | bytes 1179652
  1.8 26.5 %all-to-all-start = ((bf16[64,16,128]{2,1,0:T(8,128)(2,1)}), bf16[64,16,128]{2,1,0:T(8,128)(2,1)S(1)}, u32[]{:S(2)}, u32[]{:S(2)}) async-start(bf16[64,16,128]{2,1,0:T(8,128)(2,1)} %start.1), calls=%async_computation | async-start | bytes 524288 | tf_op jit(solution)/shard_map/all_to_all | solution.py:128
  15.2 13.1 %copy-start.1 = (bf16[64,4096]{1,0:T(8,128)(2,1)S(1)}, bf16[64,4096]{1,0:T(8,128)(2,1)}, u32[]{:S(2)}) copy-start(bf16[64,4096]{1,0:T(8,128)(2,1)} %inverse_ref.4) | copy-start | bytes 1572868
  29.5 23.7 %all-to-all-start.1 = ((bf16[64,16,128]{2,1,0:T(8,128)(2,1)}), bf16[64,16,128]{2,1,0:T(8,128)(2,1)S(1)}, u32[]{:S(2)}, u32[]{:S(2)}) async-start(bf16[64,16,128]{2,1,0:T(8,128)(2,1)} %get-tuple-element.15), calls=%async_computation.1 | async-start | bytes 524288 | tf_op jit(solution)/shard_map/all_to_all | solution.py:128
  54.3 12.8 %copy-start.2 = (bf16[64,2048]{1,0:T(8,128)(2,1)S(1)}, bf16[64,2048]{1,0:T(8,128)(2,1)}, u32[]{:S(2)}) copy-start(bf16[64,2048]{1,0:T(8,128)(2,1)} %inverse_ref.5) | copy-start | bytes 786436
  68.2 14.8 %all-to-all-start.3 = ((bf16[32,16,128]{2,1,0:T(8,128)(2,1)}), bf16[32,16,128]{2,1,0:T(8,128)(2,1)S(1)}, u32[]{:S(2)}, u32[]{:S(2)}) async-start(bf16[32,16,128]{2,1,0:T(8,128)(2,1)} %get-tuple-element.17), calls=%async_computation.3 | async-start | bytes 262144 | tf_op jit(solution)/shard_map/all_to_all | solution.py:128
  84.0 13.5 %copy-start.3 = (bf16[64,1024]{1,0:T(8,128)(2,1)S(1)}, bf16[64,1024]{1,0:T(8,128)(2,1)}, u32[]{:S(2)}) copy-start(bf16[64,1024]{1,0:T(8,128)(2,1)} %inverse_ref.6) | copy-start | bytes 393220
  98.5 15.4 %all-to-all-start.5 = ((bf16[16,16,128]{2,1,0:T(8,128)(2,1)}), bf16[16,16,128]{2,1,0:T(8,128)(2,1)S(1)}, u32[]{:S(2)}, u32[]{:S(2)}) async-start(bf16[16,16,128]{2,1,0:T(8,128)(2,1)} %get-tuple-element.20), calls=%async_computation.5 | async-start | bytes 131072 | tf_op jit(solution)/shard_map/all_to_all | solution.py:128
  114.9 11.1 %copy-start.4 = (bf16[64,512]{1,0:T(8,128)(2,1)S(1)}, bf16[64,512]{1,0:T(8,128)(2,1)}, u32[]{:S(2)}) copy-start(bf16[64,512]{1,0:T(8,128)(2,1)} %inverse_ref.7) | copy-start | bytes 196612

commit v2 on v1

--- a/solution.py
+++ b/solution.py
@@ -14,9 +14,8 @@
 
 
 def pack(block, copies):
-    flipped = block.T
-    half = flipped.shape[0] // 2
-    packed = jnp.concatenate((flipped[:half], flipped[half:]), axis=1).astype(jnp.bfloat16)
+    half = block.shape[0] // 2
+    packed = jnp.concatenate((block[:half], block[half:]), axis=1).astype(jnp.bfloat16)
     return jnp.broadcast_to(packed[None], (copies, *packed.shape))
 
 
@@ -42,7 +41,7 @@
         flat_ref[:, b * BS : (b + 1) * BS] = block
 
     unpack(gathered_ref, store)
-    result = dot_lanes(inverse_ref[...], flat_ref[...])
+    result = dot_lanes(flat_ref[...], inverse_ref[...])
     result_ref[...] = result
     message_ref[...] = pack(result, message_ref.shape[0])
 
@@ -56,10 +55,21 @@
     unpack(gathered_ref, store)
     for l, ref in enumerate(earlier):
         out_ref[l] = ref[...]
-    out_ref[len(earlier)] = dot_lanes(inverse_ref[...], flat_ref[...])
-
-
-def update_kernel(tier, last, index_ref, gathered_ref, below_ref, right_ref, *refs):
+    out_ref[len(earlier)] = dot_lanes(flat_ref[...], inverse_ref[...])
+
+
+def place(chosen, own_block):
+    found, base = chosen, NB
+    for l in range(1, LEVELS - 1):
+        count = NB >> l
+        mine = own_block // count * count
+        found = jnp.where(chosen // NB == l, chosen - l * NB - mine + base, found)
+        base += count
+    return found
+
+
+def update_kernel(tier, last, parts, index_ref, gathered_ref, right_ref, *refs):
+    below, refs = refs[:parts], refs[parts:]
     earlier = refs[: tier - 1]
     message_ref = refs[tier - 1]
     flat_ref, known_ref = refs[-2], refs[-1]
@@ -76,12 +86,17 @@
     if not last:
         kept_ref = refs[tier]
         kept_ref[...] = known_ref[first:]
-    for p in range(RB):
-        flat_ref[:, p * BS : (p + 1) * BS] = known_ref[index_ref[0, p]]
-    groups, _, width = below_ref.shape
+    quarter = RB // parts
+    listed = index_ref[tier - 1, RB] + RB
+    for k in range(parts):
+        first_listed = lax.rem(listed - k * quarter, RB)
+        for p in range(quarter):
+            at = (k * quarter + p) * BS
+            flat_ref[:, at : at + BS] = known_ref[index_ref[tier - 1, first_listed + p]]
     total = right_ref[tier]
-    for q in range(groups):
-        total = total - dot_lanes(below_ref[q], flat_ref[:, q * width : (q + 1) * width])
+    for q, ref in enumerate(below):
+        width = ref.shape[1]
+        total = total - dot_lanes(flat_ref[:, q * width : (q + 1) * width], ref[...])
     message_ref[...] = pack(total, message_ref.shape[0])
 
 
@@ -113,7 +128,10 @@
 ):
     inverses = (inverse_top, inverse_second, inverse_third, inverse_fourth)
     _, rows, columns = right_sides.shape
+    right_sides = jnp.swapaxes(right_sides, 1, 2)
     devices = lax.axis_size("sn")
+    groups = lax.axis_size("rhs")
+    column_group = lax.axis_index("rhs")
     own = lax.axis_index("sn")
     f32, bf16 = jnp.float32, jnp.bfloat16
     shape = jax.ShapeDtypeStruct
@@ -122,21 +140,26 @@
 
     def gather(copies):
         n = copies.shape[0]
-        groups = None
+        sets = None
         if n < devices:
-            groups = [list(range(s, s + n)) for s in range(0, devices, n)]
-        return lax.all_to_all(copies, "sn", 0, 0, axis_index_groups=groups)
-
-    below = [lax.all_gather(factor_below[t], "rhs") for t in range(LEVELS - 1)]
-    chosen = lax.dynamic_index_in_dim(row_blocks, own * rows // BS, 1, keepdims=False)
-    places = chosen
-    base = NB
-    for l in range(1, LEVELS - 1):
-        count = NB >> l
-        mine = own * rows // BS // count * count
-        places = jnp.where(chosen // NB == l, chosen - l * NB - mine + base, places)
-        base += count
-
+            sets = [list(range(s, s + n)) for s in range(0, devices, n)]
+        return lax.all_to_all(copies, "sn", 0, 0, axis_index_groups=sets)
+
+    def turn(part):
+        got = [part]
+        for step in range(1, groups):
+            pairs = [(i, (i + step) % groups) for i in range(groups)]
+            got.append(lax.ppermute(part, "rhs", pairs))
+        return got
+
+    below_first = turn(factor_below[0])
+    below_rest = turn(factor_below[1:])
+    own_block = own * rows // BS
+    chosen = lax.dynamic_index_in_dim(row_blocks, own_block, 1, keepdims=False)
+    places = place(chosen, own_block)
+    first = jnp.broadcast_to(column_group * (RB // groups), (LEVELS - 1, 1))
+    places = jnp.concatenate((places, first), axis=1)
+    places, right_sides = lax.optimization_barrier((places, right_sides))
     (copies,) = call(start_kernel, "start", [shape((members[0], *message), bf16)], [], right_sides)
     known = []
     results = []
@@ -148,22 +171,26 @@
             (out,) = call(
                 final_kernel,
                 "final",
-                [shape((LEVELS, rows, columns), f32)],
+                [shape((LEVELS, columns, rows), f32)],
                 [flat],
                 gathered,
                 inverses[l],
                 *results,
             )
-            return out
+            return jnp.swapaxes(out, 1, 2)
         result, copies = call(
             solve_kernel,
             f"solve{l}",
-            [shape((rows, columns), f32), shape((members[l], *message), bf16)],
+            [shape((columns, rows), f32), shape((members[l], *message), bf16)],
             [flat],
             gathered,
             inverses[l],
         )
         results.append(result)
+        if l == 0:
+            copies, *below_first = lax.optimization_barrier((copies, *below_first))
+        if l == 1:
+            copies, *below_rest = lax.optimization_barrier((copies, *below_rest))
         gathered = gather(copies)
         tier = l + 1
         last = tier == LEVELS - 1
@@ -172,14 +199,14 @@
         if not last:
             outs.append(shape((NB >> l, columns, BS), bf16))
         got = call(
-            functools.partial(update_kernel, tier, last),
+            functools.partial(update_kernel, tier, last, groups),
             f"update{tier}",
             outs,
             [pltpu.VMEM((columns, RB * BS), bf16), pltpu.VMEM((blocks, columns, BS), bf16)],
-            places[l][None],
+            places,
             gathered,
-            below[l],
             right_sides,
+            *(below_first if l == 0 else [part[l - 1] for part in below_rest]),
             *known,
             smem=1,
         )

time: 128 us -> 107 us (0.84)
  blocking collectives: 71.4 us -> 38 us
  waiting for transfers between devices: 14.7 us -> 29.6 us
    all_gather x3 -> x0, blocking collectives: 34 us -> none  [on_device(): below = [lax.all_gather(factor_below[t], 'rhs') for t in range(LEVELS - 1)]]
    all_to_all x4 -> x3, waiting for transfers between devices: 14.7 us -> 29.6 us  [gather(): return lax.all_to_all(copies, 'sn', 0, 0, axis_index_groups=sets)]
    all_to_all x4 -> x3, starting transfers between devices: 31.4 us -> 25.5 us  [gather(): return lax.all_to_all(copies, 'sn', 0, 0, axis_index_groups=sets)]
    ppermute x0 -> x6, starting transfers between devices: none -> 5.23 us  [turn(): got.append(lax.ppermute(part, 'rhs', pairs))]
    all_to_all x3 -> x4, blocking collectives: 37.4 us -> 38 us  [gather(): return lax.all_to_all(copies, 'sn', 0, 0, axis_index_groups=sets)]
  transfers between devices with their start and end apart: 4 -> 9, of which waited for: 2 -> 3; matrix products, arithmetic and copies ran while one was open for 0% -> 0% of each run, Pallas kernels for 0% -> 3%
where the time goes in v2:
time: 107 us
  blocking collectives  38 us (36%)
  starting transfers between devices  30.7 us (29%)
  waiting for transfers between devices  29.6 us (28%)
  Pallas kernels  7.13 us (7%)
    all_to_all x4, blocking collectives, gather(): return lax.all_to_all(copies, 'sn', 0, 0, axis_index_groups=sets)  38 us
    all_to_all x3, waiting for transfers between devices, gather(): return lax.all_to_all(copies, 'sn', 0, 0, axis_index_groups=sets)  29.6 us
    all_to_all x3, starting transfers between devices, gather(): return lax.all_to_all(copies, 'sn', 0, 0, axis_index_groups=sets)  25.5 us
    pallas_call x8, Pallas kernels, call(): pl.pallas_call(kernel, out_shape=outs, in_specs=[SMEM] * smem + [VMEM] *...  7.13 us
    ppermute x6, starting transfers between devices, turn(): got.append(lax.ppermute(part, 'rhs', pairs))  5.23 us
  transfers between devices with their start and end apart: 9, of which 3 were waited for; matrix products, arithmetic and copies ran while one was open for 0% of the time, Pallas kernels for 3%

profile of v2, /device:TPU:1, one launch (start us, length us, event | category | flops | bytes accessed | tf_op | source)
XLA Modules:
  0.0 106.6 jit_solution(10700560374250130169)
XLA Ops:
  0.0 0.0 copy-start
  0.0 0.0 copy-start.1
  0.0 0.8 copy-done
  0.8 0.0 copy-start.6
  0.8 0.0 copy-done.1
  0.9 0.0 copy-start.2
  0.9 0.8 start.1
  1.7 13.2 %all-to-all-start = ((bf16[64,16,128]{2,1,0:T(8,128)(2,1)}), bf16[64,16,128]{2,1,0:T(8,128)(2,1)S(1)}, u32[]{:S(2)}, u32[]{:S(2)}) async-start(bf16[64,16,128]{2,1,0:T(8,128)(2,1)} %start.1), calls=%async_computation | async-start | bytes 524288 | tf_op jit(solution)/shard_map/all_to_all | solution.py:146
  14.8 0.0 copy-done.6
  14.9 2.6 %collective-permute-start.2 = (bf16[64,1024]{1,0:T(8,128)(2,1)S(1)}, bf16[64,1024]{1,0:T(8,128)(2,1)S(1)}, u32[]{:S(2)}, u32[]{:S(2)}) collective-permute-start(bf16[64,1024]{1,0:T(8,128)(2,1)S(1)} %slice_bitcast_fusion.8.refs_0_), channel_id=1, source_target_pairs={{0,3},{1,0},{2,1},{3,2},{4,7},{5,4},{6,5},{7,6},{8,11},{9,8},{10,9... | collective-permute-start | bytes 393224 | tf_op jit(solution)/shard_map/ppermute | solution.py:152
  17.4 0.5 collective-permute-start.1
  17.9 0.6 collective-permute-start
  18.5 9.5 %all-to-all-done.gathered_ref = bf16[64,16,128]{2,1,0:T(8,128)(2,1)S(1)} async-done(((bf16[64,16,128]{2,1,0:T(8,128)(2,1)}), bf16[64,16,128]{2,1,0:T(8,128)(2,1)S(1)}, u32[]{:S(2)}, u32[]{:S(2)}) %all-to-all-start) | async-done | bytes 262176 | tf_op jit(solution)/shard_map/all_to_all | solution.py:146
  28.0 0.0 copy-done.2
  28.0 1.1 %solve0.1 = (f32[32,64]{1,0:T(8,128)S(1)}, bf16[64,16,128]{2,1,0:T(8,128)(2,1)}) custom-call(bf16[64,16,128]{2,1,0:T(8,128)(2,1)S(1)} %all-to-all-done.gathered_ref, bf16[64,4096]{1,0:T(8,128)(2,1)S(1)} %copy-done.2), custom_call_target="tpu_custom_call" | custom-call | flops 20000000 | bytes 1000000 | tf_op jit(solution)/shard_map/solve0/pallas_call | solution.py:108
  29.1 0.0 collective-permute-done.2.refs_3_
  29.1 0.0 collective-permute-done.1.refs_2_
  29.1 0.0 collective-permute-done.refs_1_
  29.1 8.4 %all-to-all-start.1 = ((bf16[64,16,128]{2,1,0:T(8,128)(2,1)}), bf16[64,16,128]{2,1,0:T(8,128)(2,1)S(1)}, u32[]{:S(2)}, u32[]{:S(2)}) async-start(bf16[64,16,128]{2,1,0:T(8,128)(2,1)} %get-tuple-element.30), calls=%async_computation.1 | async-start | bytes 524288 | tf_op jit(solution)/shard_map/all_to_all | solution.py:146
  37.6 0.4 collective-permute-start.5
  38.0 0.5 collective-permute-start.4
  38.5 0.7 collective-permute-start.3
  39.1 11.6 %all-to-all-done.1.gathered_ref = bf16[64,16,128]{2,1,0:T(8,128)(2,1)S(1)} async-done(((bf16[64,16,128]{2,1,0:T(8,128)(2,1)}), bf16[64,16,128]{2,1,0:T(8,128)(2,1)S(1)}, u32[]{:S(2)}, u32[]{:S(2)}) %all-to-all-start.1) | async-done | bytes 262176 | tf_op jit(solution)/shard_map/all_to_all | solution.py:146
  50.7 1.1 %update1.1 = (bf16[32,16,128]{2,1,0:T(8,128)(2,1)S(1)}, bf16[32,32,128]{2,1,0:T(8,128)(2,1)S(1)}) custom-call(s32[3,33]{1,0:T(4,128)S(1)} %concatenate.3.index_ref, bf16[64,16,128]{2,1,0:T(8,128)(2,1)S(1)} %all-to-all-done.1.gathered_ref, f32[4,32,64]{2,1,0:T(8,128)S(1)} %bitcast.56, bf16[64,1024]{1,0:T(8,128)(2,1)S(1)} %slice_bitcast_fusion.8.refs_0_, ...), custom_call_target="tpu_custom_call" | custom-call | flops 20000000 | bytes 1000000 | tf_op jit(solution)/shard_map/update1/pallas_call | solution.py:108
  51.8 0.0 copy-start.3
  51.8 12.8 %all_to_all.35.gathered_ref = bf16[32,16,128]{2,1,0:T(8,128)(2,1)S(1)} all-to-all(bf16[32,16,128]{2,1,0:T(8,128)(2,1)S(1)} %get-tuple-element.35), channel_id=1, replica_groups={{0,4,8,12,16,20,24,28,32,36,40,44,48,52,56,60,64,68,72,76,80,84,88,92,9..., dimensions={0} | all-to-all | bytes 262144 | tf_op jit(solution)/shard_map/all_to_all | solution.py:146
  64.6 0.0 copy-done.3
  64.6 1.0 solve1.1
  65.6 0.0 collective-permute-done.5
  65.6 0.0 collective-permute-done.4
  65.6 0.0 collective-permute-done.3
  65.6 3.9 %all-to-all-start.3 = ((bf16[32,16,128]{2,1,0:T(8,128)(2,1)}), bf16[32,16,128]{2,1,0:T(8,128)(2,1)S(1)}, u32[]{:S(2)}, u32[]{:S(2)}) async-start(bf16[32,16,128]{2,1,0:T(8,128)(2,1)} %get-tuple-element.37), calls=%async_computation.3 | async-start | bytes 262144 | tf_op jit(solution)/shard_map/all_to_all | solution.py:146
  69.7 8.6 %all-to-all-done.3.gathered_ref = bf16[32,16,128]{2,1,0:T(8,128)(2,1)S(1)} async-done(((bf16[32,16,128]{2,1,0:T(8,128)(2,1)}), bf16[32,16,128]{2,1,0:T(8,128)(2,1)S(1)}, u32[]{:S(2)}, u32[]{:S(2)}) %all-to-all-start.3) | async-done | bytes 131104 | tf_op jit(solution)/shard_map/all_to_all | solution.py:146
  78.2 1.0 update2.1
  79.3 0.0 copy-start.4
  79.3 8.8 %all_to_all.36.gathered_ref = bf16[16,16,128]{2,1,0:T(8,128)(2,1)S(1)} all-to-all(bf16[16,16,128]{2,1,0:T(8,128)(2,1)S(1)} %get-tuple-element.43), channel_id=1, replica_groups={{0,4,8,12,16,20,24,28,32,36,40,44,48,52,56,60},{64,68,72,76,80,84,88,92..., dimensions={0} | all-to-all | bytes 131072 | tf_op jit(solution)/shard_map/all_to_all | solution.py:146
  88.1 0.0 copy-done.4
  88.1 0.3 solve2.1
  88.4 8.7 %all_to_all.37.gathered_ref = bf16[16,16,128]{2,1,0:T(8,128)(2,1)S(1)} all-to-all(bf16[16,16,128]{2,1,0:T(8,128)(2,1)S(1)} %get-tuple-element.44), channel_id=1, replica_groups={{0,4,8,12,16,20,24,28,32,36,40,44,48,52,56,60},{64,68,72,76,80,84,88,92..., dimensions={0} | all-to-all | bytes 131072 | tf_op jit(solution)/shard_map/all_to_all | solution.py:146
  97.1 1.0 update3.1
  98.1 0.0 copy-start.5
  98.1 7.7 %all_to_all.38.gathered_ref = bf16[8,16,128]{2,1,0:T(8,128)(2,1)S(1)} all-to-all(bf16[8,16,128]{2,1,0:T(8,128)(2,1)S(1)} %update3.1), channel_id=1, replica_groups={{0,4,8,12,16,20,24,28},{32,36,40,44,48,52,56,60},{64,68,72,76,80,84,88,..., dimensions={0} | all-to-all | bytes 65536 | tf_op jit(solution)/shard_map/all_to_all | solution.py:146
  105.7 0.0 copy-done.5
  105.7 0.8 final.1
  (7 shorter events, 0.1 us)
Async XLA Ops:
  0.0 0.8 copy-start
  0.0 0.9 copy-start.1
  0.8 14.0 %copy-start.6 = (bf16[3,64,1024]{2,1,0:T(8,128)(2,1)S(1)}, bf16[3,64,1024]{2,1,0:T(8,128)(2,1)}, u32[]{:S(2)}) copy-start(bf16[3,64,1024]{2,1,0:T(8,128)(2,1)} %param.8) | copy-start | bytes 1179652
  0.9 27.1 %copy-start.2 = (bf16[64,4096]{1,0:T(8,128)(2,1)S(1)}, bf16[64,4096]{1,0:T(8,128)(2,1)}, u32[]{:S(2)}) copy-start(bf16[64,4096]{1,0:T(8,128)(2,1)} %inverse_ref.4) | copy-start | bytes 1572868
  1.7 26.3 %all-to-all-start = ((bf16[64,16,128]{2,1,0:T(8,128)(2,1)}), bf16[64,16,128]{2,1,0:T(8,128)(2,1)S(1)}, u32[]{:S(2)}, u32[]{:S(2)}) async-start(bf16[64,16,128]{2,1,0:T(8,128)(2,1)} %start.1), calls=%async_computation | async-start | bytes 524288 | tf_op jit(solution)/shard_map/all_to_all | solution.py:146
  14.9 14.3 %collective-permute-start.2 = (bf16[64,1024]{1,0:T(8,128)(2,1)S(1)}, bf16[64,1024]{1,0:T(8,128)(2,1)S(1)}, u32[]{:S(2)}, u32[]{:S(2)}) collective-permute-start(bf16[64,1024]{1,0:T(8,128)(2,1)S(1)} %slice_bitcast_fusion.8.refs_0_), channel_id=1, source_target_pairs={{0,3},{1,0},{2,1},{3,2},{4,7},{5,4},{6,5},{7,6},{8,11},{9,8},{10,9... | collective-permute-start | bytes 393224 | tf_op jit(solution)/shard_map/ppermute | solution.py:152
  17.4 11.7 %collective-permute-start.1 = (bf16[64,1024]{1,0:T(8,128)(2,1)S(1)}, bf16[64,1024]{1,0:T(8,128)(2,1)S(1)}, u32[]{:S(2)}, u32[]{:S(2)}) collective-permute-start(bf16[64,1024]{1,0:T(8,128)(2,1)S(1)} %slice_bitcast_fusion.8.refs_0_), channel_id=1, source_target_pairs={{0,2},{1,3},{2,0},{3,1},{4,6},{5,7},{6,4},{7,5},{8,10},{9,11},{10,... | collective-permute-start | bytes 393224 | tf_op jit(solution)/shard_map/ppermute | solution.py:152
  17.9 11.2 %collective-permute-start = (bf16[64,1024]{1,0:T(8,128)(2,1)S(1)}, bf16[64,1024]{1,0:T(8,128)(2,1)S(1)}, u32[]{:S(2)}, u32[]{:S(2)}) collective-permute-start(bf16[64,1024]{1,0:T(8,128)(2,1)S(1)} %slice_bitcast_fusion.8.refs_0_), channel_id=1, source_target_pairs={{0,1},{1,2},{2,3},{3,0},{4,5},{5,6},{6,7},{7,4},{8,9},{9,10},{10,1... | collective-permute-start | bytes 393224 | tf_op jit(solution)/shard_map/ppermute | solution.py:152
  29.1 21.6 %all-to-all-start.1 = ((bf16[64,16,128]{2,1,0:T(8,128)(2,1)}), bf16[64,16,128]{2,1,0:T(8,128)(2,1)S(1)}, u32[]{:S(2)}, u32[]{:S(2)}) async-start(bf16[64,16,128]{2,1,0:T(8,128)(2,1)} %get-tuple-element.30), calls=%async_computation.1 | async-start | bytes 524288 | tf_op jit(solution)/shard_map/all_to_all | solution.py:146
  37.6 28.0 %collective-permute-start.5 = (bf16[2,64,1024]{2,1,0:T(8,128)(2,1)S(1)}, bf16[2,64,1024]{2,1,0:T(8,128)(2,1)S(1)}, u32[]{:S(2)}, u32[]{:S(2)}) collective-permute-start(bf16[2,64,1024]{2,1,0:T(8,128)(2,1)S(1)} %slice.31), channel_id=1, source_target_pairs={{0,3},{1,0},{2,1},{3,2},{4,7},{5,4},{6,5},{7,6},{8,11},{9,8},{10,9... | collective-permute-start | bytes 786440 | tf_op jit(solution)/shard_map/ppermute | solution.py:152
  38.0 27.7 %collective-permute-start.4 = (bf16[2,64,1024]{2,1,0:T(8,128)(2,1)S(1)}, bf16[2,64,1024]{2,1,0:T(8,128)(2,1)S(1)}, u32[]{:S(2)}, u32[]{:S(2)}) collective-permute-start(bf16[2,64,1024]{2,1,0:T(8,128)(2,1)S(1)} %slice.31), channel_id=1, source_target_pairs={{0,2},{1,3},{2,0},{3,1},{4,6},{5,7},{6,4},{7,5},{8,10},{9,11},{10,... | collective-permute-start | bytes 786440 | tf_op jit(solution)/shard_map/ppermute | solution.py:152
  38.5 27.2 %collective-permute-start.3 = (bf16[2,64,1024]{2,1,0:T(8,128)(2,1)S(1)}, bf16[2,64,1024]{2,1,0:T(8,128)(2,1)S(1)}, u32[]{:S(2)}, u32[]{:S(2)}) collective-permute-start(bf16[2,64,1024]{2,1,0:T(8,128)(2,1)S(1)} %slice.31), channel_id=1, source_target_pairs={{0,1},{1,2},{2,3},{3,0},{4,5},{5,6},{6,7},{7,4},{8,9},{9,10},{10,1... | collective-permute-start | bytes 786440 | tf_op jit(solution)/shard_map/ppermute | solution.py:152
  51.8 12.8 %copy-start.3 = (bf16[64,2048]{1,0:T(8,128)(2,1)S(1)}, bf16[64,2048]{1,0:T(8,128)(2,1)}, u32[]{:S(2)}) copy-start(bf16[64,2048]{1,0:T(8,128)(2,1)} %inverse_ref.5) | copy-start | bytes 786436
  65.6 12.6 %all-to-all-start.3 = ((bf16[32,16,128]{2,1,0:T(8,128)(2,1)}), bf16[32,16,128]{2,1,0:T(8,128)(2,1)S(1)}, u32[]{:S(2)}, u32[]{:S(2)}) async-start(bf16[32,16,128]{2,1,0:T(8,128)(2,1)} %get-tuple-element.37), calls=%async_computation.3 | async-start | bytes 262144 | tf_op jit(solution)/shard_map/all_to_all | solution.py:146
  79.3 8.8 %copy-start.4 = (bf16[64,1024]{1,0:T(8,128)(2,1)S(1)}, bf16[64,1024]{1,0:T(8,128)(2,1)}, u32[]{:S(2)}) copy-start(bf16[64,1024]{1,0:T(8,128)(2,1)} %inverse_ref.6) | copy-start | bytes 393220
  98.1 7.7 %copy-start.5 = (bf16[64,512]{1,0:T(8,128)(2,1)S(1)}, bf16[64,512]{1,0:T(8,128)(2,1)}, u32[]{:S(2)}) copy-start(bf16[64,512]{1,0:T(8,128)(2,1)} %inverse_ref.7) | copy-start | bytes 196612

commit v3 on v2

v3 whole, which is shorter than its diff:
```python
import functools

import jax
import jax.numpy as jnp
from jax import lax
from jax.experimental import pallas as pl
from jax.experimental.pallas import tpu as pltpu
from jax.sharding import PartitionSpec as P

BS = 128
NB = 32
LEVELS = 4
RB = 32


def pack(block, copies):
    half = block.shape[0] // 2
    packed = jnp.concatenate((block[:half], block[half:]), axis=1).astype(jnp.bfloat16)
    return jnp.broadcast_to(packed[None], (copies, *packed.shape))


def unpack(gathered, store):
    lanes = gathered.shape[2] // 2
    for b in range(gathered.shape[0] // 2):
        one, two = gathered[2 * b], gathered[2 * b + 1]
        top = jnp.concatenate((one[:, :lanes], two[:, :lanes]), axis=1)
        low = jnp.concatenate((one[:, lanes:], two[:, lanes:]), axis=1)
        store(b, jnp.concatenate((top, low), axis=0))


def dot_lanes(a, b):
    return lax.dot_general(a, b, (((1,), (1,)), ((), ())), preferred_element_type=jnp.float32)


def start_kernel(right_ref, message_ref):
    message_ref[...] = pack(right_ref[0], message_ref.shape[0])


def solve_kernel(gathered_ref, inverse_ref, result_ref, message_ref, flat_ref):
    def store(b, block):
        flat_ref[:, b * BS : (b + 1) * BS] = block

    unpack(gathered_ref, store)
    result = dot_lanes(flat_ref[...], inverse_ref[...])
    result_ref[...] = result
    message_ref[...] = pack(result, message_ref.shape[0])


def select_kernel(position_ref, *refs):
    below, out_ref = refs[:-1], refs[-1]
    part = below[0].shape[1] // BS
    for j in range(out_ref.shape[2] // BS):
        at = position_ref[0, j]
        for q, ref in enumerate(below):

            @pl.when(at // part == q)
            def _():
                columns = pl.ds(pl.multiple_of(at % part * BS, BS), BS)
                out_ref[0, :, j * BS : (j + 1) * BS] = ref[:, columns]


def join(mine, other, core):
    first = jnp.where(core == 0, mine, other)
    second = jnp.where(core == 0, other, mine)
    return jnp.concatenate((first, second), axis=1)


def final_kernel(
    pieces, gathered_ref, fourth_ref, first_result_ref, second_result_ref, third_ref, third_other_ref, *refs
):
    parent, parent_other = refs[:pieces], refs[pieces : 2 * pieces]
    out_ref, flat_ref, solved_ref, coupled_ref, last_ref = refs[2 * pieces :]
    own = lax.axis_index("sn")
    core, y, z = own % 2, own // 2 % 4, own // 8 % 2
    half = gathered_ref.shape[1] // 2
    devices, rows = gathered_ref.shape[0], fourth_ref.shape[0]

    def store(b, block):
        flat_ref[:, b * BS : (b + 1) * BS] = block

    def store_last(b, block):
        last_ref[:, b * BS : (b + 1) * BS] = block

    def flat(ref):
        return ref[...].reshape(ref.shape[0] * ref.shape[1], ref.shape[2])

    unpack(gathered_ref[:, :half], store)
    in_plane = pl.ds(pl.multiple_of(z * (devices // 2), devices // 2), devices // 2)
    unpack(gathered_ref[in_plane, half:], store_last)
    mine = dot_lanes(flat_ref[...], flat(third_ref))
    other = dot_lanes(flat_ref[...], flat(third_other_ref))
    out_ref[0] = first_result_ref[...]
    out_ref[1] = second_result_ref[...]
    out_ref[2] = mine[:, :rows]
    for e in range(third_ref.shape[0]):
        block = (z ^ (e // 2 % 2)) * pieces + (y ^ (e % 2 * 2 + e // 4))
        at = slice(e * rows, (e + 1) * rows)
        columns = pl.ds(pl.multiple_of(block * BS, BS), BS)
        solved_ref[:, columns] = join(mine[:, at], other[:, at], core).astype(jnp.bfloat16)
    for e in range(pieces):
        mine = dot_lanes(solved_ref[...], parent[e][0])
        other = dot_lanes(solved_ref[...], parent_other[e][0])
        columns = pl.ds(pl.multiple_of((y ^ e) * BS, BS), BS)
        coupled_ref[:, columns] = join(mine, other, core)
    update = last_ref[...].astype(jnp.float32) - coupled_ref[...]
    out_ref[3] = dot_lanes(update.astype(jnp.bfloat16), fourth_ref[...])


def place(chosen, own_block):
    found, base = chosen, NB
    for l in range(1, LEVELS - 1):
        count = NB >> l
        mine = own_block // count * count
        at = chosen - l * NB - mine + base
        if l == LEVELS - 2:
            at = jnp.full_like(chosen, base)
        found = jnp.where(chosen // NB == l, at, found)
        base += count
    return found


def update_kernel(tiers, kept, parts, index_ref, gathered_ref, right_ref, *refs):
    below = [refs[k * parts : (k + 1) * parts] for k in range(len(tiers))]
    refs = refs[len(tiers) * parts :]
    known_ref, flat_ref = refs[-2], refs[-1]
    base = 0
    if not kept:
        base = refs[0].shape[0]
        known_ref[:base] = refs[0][...]
        refs = refs[1:]
    message_ref = refs[0]

    def store(b, block):
        known_ref[base + b] = block

    unpack(gathered_ref, store)
    if kept:
        refs[1][...] = known_ref[...]
    else:
        known_ref[known_ref.shape[0] - 1] = jnp.zeros(known_ref.shape[1:], known_ref.dtype)
    quarter = RB // parts
    slot = 0
    packed = []
    for tier, group in zip(tiers, below):
        listed = index_ref[tier - 1, RB] + RB
        total = right_ref[tier]
        for k, ref in enumerate(group):
            first_listed = lax.rem(listed - k * quarter, RB)
            for p in range(quarter):
                block = known_ref[index_ref[tier - 1, first_listed + p]]
                flat_ref[slot, :, p * BS : (p + 1) * BS] = block
            total = total - dot_lanes(flat_ref[slot], ref[...])
            slot += 1
        packed.append(pack(total, message_ref.shape[0]))
    message_ref[...] = jnp.concatenate(packed, axis=1)


VMEM = pl.BlockSpec(memory_space=pltpu.VMEM)
SMEM = pl.BlockSpec(memory_space=pltpu.SMEM)


def call(kernel, name, outs, scratch, *args, smem=0):
    return pl.pallas_call(
        kernel,
        out_shape=outs,
        in_specs=[SMEM] * smem + [VMEM] * (len(args) - smem),
        out_specs=[VMEM] * len(outs),
        scratch_shapes=scratch,
        cost_estimate=pl.CostEstimate(flops=20_000_000, bytes_accessed=1_000_000, transcendentals=0),
        compiler_params=pltpu.CompilerParams(vmem_limit_bytes=16 * 2**20),
        name=name,
    )(*args)


def on_device(
    right_sides,
    factor_below,
    row_blocks,
    inverse_top,
    inverse_second,
    inverse_third,
    inverse_fourth,
):
    _, rows, columns = right_sides.shape
    right_sides = jnp.swapaxes(right_sides, 1, 2)
    devices = lax.axis_size("sn")
    groups = lax.axis_size("rhs")
    column_group = lax.axis_index("rhs")
    own = lax.axis_index("sn")
    f32, bf16 = jnp.float32, jnp.bfloat16
    shape = jax.ShapeDtypeStruct
    message = (columns // 2, 2 * rows)
    members = [devices >> l for l in range(LEVELS)]
    barrier = lax.optimization_barrier

    def gather(copies):
        n = copies.shape[0]
        sets = None
        if n < devices:
            sets = [list(range(s, s + n)) for s in range(0, devices, n)]
        return lax.all_to_all(copies, "sn", 0, 0, axis_index_groups=sets)

    def turn(part):
        got = [part]
        for step in range(1, groups):
            pairs = [(i, (i + step) % groups) for i in range(groups)]
            got.append(lax.ppermute(part, "rhs", pairs))
        return got

    def swap(part, bit):
        return lax.ppermute(part, "sn", [(i, i ^ bit) for i in range(devices)])

    core, y_low, y_high, z_low = 1, 2, 4, 8

    def over_y(part):
        return [part] + [swap(part, bits) for bits in (y_low, y_high, y_low + y_high)]

    own_block = own * rows // BS
    chosen = lax.dynamic_index_in_dim(row_blocks, own_block, 1, keepdims=False)
    places = place(chosen, own_block)
    first = jnp.broadcast_to(column_group * (RB // groups), (LEVELS - 1, 1))
    places = jnp.concatenate((places, first), axis=1)
    count = NB >> (LEVELS - 2)
    parent = (LEVELS - 2) * NB + own_block // count * count + jnp.arange(count)
    listed = jnp.arange(RB)
    turned = (column_group + groups - listed // (RB // groups)) % groups * (RB // groups)
    turned = turned + listed % (RB // groups)
    hit = chosen[LEVELS - 2][None, :] == parent[:, None]
    positions = jnp.sum(jnp.where(hit, turned[None, :], 0), axis=1)[None].astype(jnp.int32)
    places, positions, right_sides = barrier((places, positions, right_sides))

    first_below = turn(factor_below[0])
    third = inverse_third[None]
    third_got = swap(third, y_high)

    (copies,) = call(start_kernel, "start", [shape((members[0], *message), bf16)], [], right_sides)
    gathered = gather(copies)
    first_result, copies = call(
        solve_kernel,
        "solve0",
        [shape((columns, rows), f32), shape((members[0], *message), bf16)],
        [pltpu.VMEM((columns, members[0] * rows), bf16)],
        gathered,
        inverse_top,
    )

    copies, third_got, *first_below = barrier((copies, third_got, *first_below))
    third = jnp.concatenate((third, third_got))
    third_got = swap(third, z_low)
    rest_below = turn(factor_below[1:])

    gathered = gather(copies)
    copies, known = call(
        functools.partial(update_kernel, (1,), True, groups),
        "update1",
        [shape((members[1], *message), bf16), shape((NB, columns, BS), bf16)],
        [pltpu.VMEM((NB, columns, BS), bf16), pltpu.VMEM((groups, columns, RB // groups * BS), bf16)],
        places,
        gathered,
        right_sides,
        *first_below,
        smem=1,
    )

    copies, third_got = barrier((copies, third_got))
    third = jnp.concatenate((third, third_got))
    third_got = swap(third, y_low)
    second_below = [part[0] for part in rest_below]
    last_below = [part[1] for part in rest_below]
    (coupled,) = call(
        select_kernel, "select", [shape((1, rows, count * BS), bf16)], [], positions, *last_below, smem=1
    )
    coupled = over_y(coupled)

    gathered = gather(copies)
    second_result, copies = call(
        solve_kernel,
        "solve1",
        [shape((columns, rows), f32), shape((members[1], *message), bf16)],
        [pltpu.VMEM((columns, members[1] * rows), bf16)],
        gathered,
        inverse_second,
    )

    gathered = gather(copies)
    blocks = NB + NB // 2 + 1
    (copies,) = call(
        functools.partial(update_kernel, (2, 3), False, groups),
        "update2",
        [shape((members[2], 2 * message[0], message[1]), bf16)],
        [pltpu.VMEM((blocks, columns, BS), bf16), pltpu.VMEM((2 * groups, columns, RB // groups * BS), bf16)],
        places,
        gathered,
        right_sides,
        *second_below,
        *last_below,
        known,
        smem=1,
    )


    copies, coupled, third_got = barrier((copies, coupled, third_got))
    third = jnp.concatenate((third, third_got))
    third_other = swap(third, core)
    coupled_other = [swap(part, core) for part in coupled]

    gathered = gather(copies)
    (out,) = call(
        functools.partial(final_kernel, len(coupled)),
        "final",
        [shape((LEVELS, columns, rows), f32)],
        [
            pltpu.VMEM((columns, members[2] * rows), bf16),
            pltpu.VMEM((columns, members[2] * rows), bf16),
            pltpu.VMEM((columns, members[3] * rows), f32),
            pltpu.VMEM((columns, members[3] * rows), bf16),
        ],
        gathered,
        inverse_fourth,
        first_result,
        second_result,
        third,
        third_other,
        *coupled,
        *coupled_other,
    )
    return jnp.swapaxes(out, 1, 2)


def solution(mesh):
    in_specs = (
        P(None, "sn", "rhs"),
        P(None, "sn", "rhs"),
        P(),
        P("sn", None),
        P("sn", None),
        P("sn", None),
        P("sn", None),
    )
    out_specs = P(None, "sn", "rhs")
    return jax.shard_map(
        on_device, mesh=mesh, in_specs=in_specs, out_specs=out_specs, check_vma=False
    )
```

time: 107 us -> 99.9 us (0.934)
  blocking collectives: 38 us -> 0 us
  starting transfers between devices: 30.7 us -> 53.1 us
  waiting for transfers between devices: 29.6 us -> 32.6 us
  Pallas kernels: 7.13 us -> 9.4 us
  other arithmetic: 0.01 us -> 2.23 us
    all_to_all x4 -> x0, blocking collectives: 38 us -> none  [gather(): return lax.all_to_all(copies, 'sn', 0, 0, axis_index_groups=sets)]
    ppermute x0 -> x11, starting transfers between devices: none -> 11.7 us  [swap(): return lax.ppermute(part, 'sn', [(i, i ^ bit) for i in range(devices)])]
    all_to_all x3 -> x5, starting transfers between devices: 25.5 us -> 36.1 us  [gather(): return lax.all_to_all(copies, 'sn', 0, 0, axis_index_groups=sets)]
    ppermute x6, waiting for transfers between devices: 0.02 us -> 5.32 us  [turn(): got.append(lax.ppermute(part, 'rhs', pairs))]
    all_to_all x3 -> x5, waiting for transfers between devices: 29.6 us -> 26 us  [gather(): return lax.all_to_all(copies, 'sn', 0, 0, axis_index_groups=sets)]
    pallas_call x8 -> x7, Pallas kernels: 7.13 us -> 9.4 us  [call(): pl.pallas_call(kernel, out_shape=outs, in_specs=[SMEM] * smem + [VMEM] *...]
    concatenate x0 -> x3, other arithmetic: none -> 2.02 us  [on_device(): third = jnp.concatenate((third, third_got))]
    ppermute x0 -> x11, waiting for transfers between devices: none -> 1.29 us  [swap(): return lax.ppermute(part, 'sn', [(i, i ^ bit) for i in range(devices)])]
  transfers between devices with their start and end apart: 9 -> 22, of which waited for: 3 -> 12; matrix products, arithmetic and copies ran while one was open for 0% -> 2% of each run, Pallas kernels for 3% -> 7%
where the time goes in v3:
time: 99.9 us; the launch traced here: 99.3 us
  starting transfers between devices  53.1 us (53%)
  waiting for transfers between devices  32.6 us (33%)
  Pallas kernels  9.4 us (9%)
  other arithmetic  2.23 us (2%)
  local copies, waits for them, and re-layouts  1.91 us (2%)
    all_to_all x5, starting transfers between devices, gather(): return lax.all_to_all(copies, 'sn', 0, 0, axis_index_groups=sets)  36.1 us
    all_to_all x5, waiting for transfers between devices, gather(): return lax.all_to_all(copies, 'sn', 0, 0, axis_index_groups=sets)  26 us
    ppermute x11, starting transfers between devices, swap(): return lax.ppermute(part, 'sn', [(i, i ^ bit) for i in range(devices)])  11.7 us
    pallas_call x7, Pallas kernels, call(): pl.pallas_call(kernel, out_shape=outs, in_specs=[SMEM] * smem + [VMEM] *...  9.4 us
    ppermute x6, waiting for transfers between devices, turn(): got.append(lax.ppermute(part, 'rhs', pairs))  5.32 us
    ppermute x6, starting transfers between devices, turn(): got.append(lax.ppermute(part, 'rhs', pairs))  5.23 us
    concatenate x3, other arithmetic, on_device(): third = jnp.concatenate((third, third_got))  2.02 us
  transfers between devices with their start and end apart: 22, of which 12 were waited for; matrix products, arithmetic and copies ran while one was open for 2% of the time, Pallas kernels for 7%

profile of v3, /device:TPU:1, one launch (start us, length us, event | category | flops | bytes accessed | tf_op | source)
XLA Modules:
  0.0 99.3 jit_solution(3278804766627521825)
XLA Ops:
  0.0 0.0 copy-start
  0.0 0.8 copy-done
  0.9 0.2 select_reduce_fusion
  1.1 0.0 copy-done.1
  1.1 0.0 copy-start.6
  1.1 0.8 start.1
  1.9 13.3 %all-to-all-start = ((bf16[64,16,128]{2,1,0:T(8,128)(2,1)}), bf16[64,16,128]{2,1,0:T(8,128)(2,1)S(1)}, u32[]{:S(2)}, u32[]{:S(2)}) async-start(bf16[64,16,128]{2,1,0:T(8,128)(2,1)} %start.1), calls=%async_computation | async-start | bytes 524288 | tf_op jit(solution)/shard_map/all_to_all | solution.py:201
  15.2 0.0 copy-start.2
  15.2 0.0 copy-done.5
  15.2 3.0 %collective-permute-start = (bf16[1,64,1024]{2,1,0:T(8,128)(2,1)S(1)}, bf16[1,64,1024]{2,1,0:T(8,128)(2,1)S(1)}, u32[]{:S(2)}, u32[]{:S(2)}) collective-permute-start(bf16[1,64,1024]{2,1,0:T(8,128)(2,1)S(1)} %bitcast.56), channel_id=1, source_target_pairs={{0,16},{4,20},{8,24},{12,28},{16,0},{20,4},{24,8},{28,12},{32,48},... | collective-permute-start | bytes 393224 | tf_op jit(solution)/shard_map/ppermute | solution.py:211
  18.2 0.0 copy-done.6
  18.2 2.6 %collective-permute-start.3 = (bf16[64,1024]{1,0:T(8,128)(2,1)S(1)}, bf16[64,1024]{1,0:T(8,128)(2,1)S(1)}, u32[]{:S(2)}, u32[]{:S(2)}) collective-permute-start(bf16[64,1024]{1,0:T(8,128)(2,1)S(1)} %get-tuple-element.32.refs_0_), channel_id=1, source_target_pairs={{0,3},{1,0},{2,1},{3,2},{4,7},{5,4},{6,5},{7,6},{8,11},{9,8},{10,9... | collective-permute-start | bytes 393224 | tf_op jit(solution)/shard_map/ppermute | solution.py:207
  20.8 0.5 collective-permute-start.2
  21.3 0.6 collective-permute-start.1
  21.9 6.4 %all-to-all-done.gathered_ref = bf16[64,16,128]{2,1,0:T(8,128)(2,1)S(1)} async-done(((bf16[64,16,128]{2,1,0:T(8,128)(2,1)}), bf16[64,16,128]{2,1,0:T(8,128)(2,1)S(1)}, u32[]{:S(2)}, u32[]{:S(2)}) %all-to-all-start) | async-done | bytes 262176 | tf_op jit(solution)/shard_map/all_to_all | solution.py:201
  28.3 0.0 copy-done.2
  28.3 1.1 %solve0.1 = (f32[32,64]{1,0:T(8,128)S(1)}, bf16[64,16,128]{2,1,0:T(8,128)(2,1)}) custom-call(bf16[64,16,128]{2,1,0:T(8,128)(2,1)S(1)} %all-to-all-done.gathered_ref, bf16[64,4096]{1,0:T(8,128)(2,1)S(1)} %copy-done.2), custom_call_target="tpu_custom_call" | custom-call | flops 20000000 | bytes 1000000 | tf_op jit(solution)/shard_map/solve0/pallas_call | solution.py:163
  29.5 0.0 collective-permute-done
  29.5 0.0 collective-permute-done.3.refs_3_
  29.5 0.0 collective-permute-done.2.refs_2_
  29.5 0.9 collective-permute-done.1.refs_1_
  30.3 8.6 %all-to-all-start.1 = ((bf16[64,16,128]{2,1,0:T(8,128)(2,1)}), bf16[64,16,128]{2,1,0:T(8,128)(2,1)S(1)}, u32[]{:S(2)}, u32[]{:S(2)}) async-start(bf16[64,16,128]{2,1,0:T(8,128)(2,1)} %get-tuple-element.31), calls=%async_computation.1 | async-start | bytes 524288 | tf_op jit(solution)/shard_map/all_to_all | solution.py:201
  38.9 0.4 collective-permute-start.7
  39.3 1.5 %collective-permute-start.4 = (bf16[2,64,1024]{2,1,0:T(8,128)(2,1)S(1)}, bf16[2,64,1024]{2,1,0:T(8,128)(2,1)S(1)}, u32[]{:S(2)}, u32[]{:S(2)}) collective-permute-start(bf16[2,64,1024]{2,1,0:T(8,128)(2,1)S(1)} %pad_maximum_fusion.2), channel_id=1, source_target_pairs={{0,32},{4,36},{8,40},{12,44},{16,48},{20,52},{24,56},{28,60},{32,0... | collective-permute-start | bytes 786440 | tf_op jit(solution)/shard_map/ppermute | solution.py:211
  40.8 0.5 collective-permute-start.6
  41.3 0.7 collective-permute-start.5
  42.0 4.5 %collective-permute-done.7 = bf16[2,64,1024]{2,1,0:T(8,128)(2,1)S(1)} collective-permute-done((bf16[2,64,1024]{2,1,0:T(8,128)(2,1)S(1)}, bf16[2,64,1024]{2,1,0:T(8,128)(2,1)S(1)}, u32[]{:S(2)}, u32[]{:S(2)}) %collective-permute-start.7) | collective-permute-done | bytes 262176 | tf_op jit(solution)/shard_map/ppermute | solution.py:207
  46.5 5.6 %all-to-all-done.1.gathered_ref = bf16[64,16,128]{2,1,0:T(8,128)(2,1)S(1)} async-done(((bf16[64,16,128]{2,1,0:T(8,128)(2,1)}), bf16[64,16,128]{2,1,0:T(8,128)(2,1)S(1)}, u32[]{:S(2)}, u32[]{:S(2)}) %all-to-all-start.1) | async-done | bytes 262176 | tf_op jit(solution)/shard_map/all_to_all | solution.py:201
  52.1 1.8 %update1.1 = (bf16[32,16,128]{2,1,0:T(8,128)(2,1)}, bf16[32,32,128]{2,1,0:T(8,128)(2,1)S(1)}) custom-call(s32[3,33]{1,0:T(4,128)S(1)} %concatenate.14.index_ref, bf16[64,16,128]{2,1,0:T(8,128)(2,1)S(1)} %all-to-all-done.1.gathered_ref, f32[4,32,64]{2,1,0:T(8,128)S(1)} %bitcast.53, bf16[64,1024]{1,0:T(8,128)(2,1)S(1)} %get-tuple-element.32.refs_0_, ...), custom_call_target="tpu_custom_call" | custom-call | flops 20000000 | bytes 1000000 | tf_op jit(solution)/shard_map/update1/pallas_call | solution.py:163
  53.8 0.0 collective-permute-done.4
  53.8 5.4 %all-to-all-start.2 = ((bf16[32,16,128]{2,1,0:T(8,128)(2,1)}), bf16[32,16,128]{2,1,0:T(8,128)(2,1)S(1)}, u32[]{:S(2)}, u32[]{:S(2)}) async-start(bf16[32,16,128]{2,1,0:T(8,128)(2,1)} %get-tuple-element.38), calls=%async_computation.2 | async-start | bytes 262144 | tf_op jit(solution)/shard_map/all_to_all | solution.py:201
  59.3 0.8 pad_maximum_fusion.1
  60.1 1.4 %collective-permute-start.11 = (bf16[4,64,1024]{2,1,0:T(8,128)(2,1)}, bf16[4,64,1024]{2,1,0:T(8,128)(2,1)}, u32[]{:S(2)}, u32[]{:S(2)}) collective-permute-start(bf16[4,64,1024]{2,1,0:T(8,128)(2,1)} %pad_maximum_fusion.1), channel_id=1, source_target_pairs={{0,8},{4,12},{8,0},{12,4},{16,24},{20,28},{24,16},{28,20},{32,40},... | collective-permute-start | bytes 1572872 | tf_op jit(solution)/shard_map/ppermute | solution.py:211
  61.5 0.0 collective-permute-done.6
  61.5 1.0 slice_bitcast_fusion.1
  62.5 5.3 %all-to-all-done.2.gathered_ref = bf16[32,16,128]{2,1,0:T(8,128)(2,1)S(1)} async-done(((bf16[32,16,128]{2,1,0:T(8,128)(2,1)}), bf16[32,16,128]{2,1,0:T(8,128)(2,1)S(1)}, u32[]{:S(2)}, u32[]{:S(2)}) %all-to-all-start.2) | async-done | bytes 131104 | tf_op jit(solution)/shard_map/all_to_all | solution.py:201
  67.8 1.0 %solve1.1 = (f32[32,64]{1,0:T(8,128)S(1)}, bf16[32,16,128]{2,1,0:T(8,128)(2,1)}) custom-call(bf16[32,16,128]{2,1,0:T(8,128)(2,1)S(1)} %all-to-all-done.2.gathered_ref, bf16[64,2048]{1,0:T(8,128)(2,1)S(1)} %copy-done.3), custom_call_target="tpu_custom_call" | custom-call | flops 20000000 | bytes 1000000 | tf_op jit(solution)/shard_map/solve1/pallas_call | solution.py:163
  68.8 3.9 %all-to-all-start.3 = ((bf16[32,16,128]{2,1,0:T(8,128)(2,1)}), bf16[32,16,128]{2,1,0:T(8,128)(2,1)S(1)}, u32[]{:S(2)}, u32[]{:S(2)}) async-start(bf16[32,16,128]{2,1,0:T(8,128)(2,1)} %get-tuple-element.39), calls=%async_computation.3 | async-start | bytes 262144 | tf_op jit(solution)/shard_map/all_to_all | solution.py:201
  72.7 0.0 collective-permute-done.5
  72.8 0.8 select.36.refs_0_
  73.6 2.7 %collective-permute-start.10 = (bf16[1,64,1024]{2,1,0:T(8,128)(2,1)S(1)}, bf16[1,64,1024]{2,1,0:T(8,128)(2,1)S(1)}, u32[]{:S(2)}, u32[]{:S(2)}) collective-permute-start(bf16[1,64,1024]{2,1,0:T(8,128)(2,1)S(1)} %select.36.refs_0_), channel_id=1, source_target_pairs={{0,24},{4,28},{8,16},{12,20},{16,8},{20,12},{24,0},{28,4},{32,56},... | collective-permute-start | bytes 393224 | tf_op jit(solution)/shard_map/ppermute | solution.py:211
  76.3 0.5 collective-permute-start.9
  76.9 0.1 collective-permute-start.8
  77.0 4.5 %all-to-all-done.3.gathered_ref = bf16[32,16,128]{2,1,0:T(8,128)(2,1)S(1)} async-done(((bf16[32,16,128]{2,1,0:T(8,128)(2,1)}), bf16[32,16,128]{2,1,0:T(8,128)(2,1)S(1)}, u32[]{:S(2)}, u32[]{:S(2)}) %all-to-all-start.3) | async-done | bytes 131104 | tf_op jit(solution)/shard_map/all_to_all | solution.py:201
  81.5 1.8 %update2.1 = bf16[16,32,128]{2,1,0:T(8,128)(2,1)} custom-call(s32[3,33]{1,0:T(4,128)S(1)} %concatenate.14.index_ref, bf16[32,16,128]{2,1,0:T(8,128)(2,1)S(1)} %all-to-all-done.3.gathered_ref, f32[4,32,64]{2,1,0:T(8,128)S(1)} %bitcast.54, bf16[64,1024]{1,0:T(8,128)(2,1)S(1)} %get-tuple-element.52.refs_0_, bf16[64,1024]{1,0:T(8,128)(2,1)S(1)} %get-tuple-element.59.refs_1_, ...), custom_call_target="tpu_custom_call" | custom-call | flops 20000000 | bytes 1000000 | tf_op jit(solution)/shard_map/update2/pallas_call | solution.py:163
  83.3 0.0 collective-permute-done.10.refs_3_
  83.3 0.0 collective-permute-done.9.refs_2_
  83.3 0.2 collective-permute-done.8.refs_1_
  83.6 0.0 collective-permute-done.11
  83.6 1.1 %pad_maximum_fusion.third_ref = bf16[8,64,1024]{2,1,0:T(8,128)(2,1)S(1)} fusion(bf16[4,64,1024]{2,1,0:T(8,128)(2,1)} %collective-permute-done.11, bf16[2,64,1024]{2,1,0:T(8,128)(2,1)S(1)} %collective-permute-done.4, bf16[1,64,1024]{2,1,0:T(8,128)(2,1)S(1)} %collective-permute-done, bf16[1,64,1024]{2,1,0:T(8,128)(2,1)S(1)} %bitcast.59), kind=kLoop, calls=%fused_computation | loop fusion | flops 1572864 | bytes 2097152 | tf_op jit(solution)/shard_map/concatenate | solution.py:303
  84.7 0.0 copy-start.4
  84.7 1.4 %collective-permute-start.12 = (bf16[8,64,1024]{2,1,0:T(8,128)(2,1)S(1)}, bf16[8,64,1024]{2,1,0:T(8,128)(2,1)S(1)}, u32[]{:S(2)}, u32[]{:S(2)}) collective-permute-start(bf16[8,64,1024]{2,1,0:T(8,128)(2,1)S(1)} %pad_maximum_fusion.third_ref), channel_id=1, source_target_pairs={{0,4},{4,0},{8,12},{12,8},{16,20},{20,16},{24,28},{28,24},{32,36},... | collective-permute-start | bytes 3145736 | tf_op jit(solution)/shard_map/ppermute | solution.py:211
  86.2 4.9 %all-to-all-start.4 = ((bf16[16,32,128]{2,1,0:T(8,128)(2,1)}), bf16[16,32,128]{2,1,0:T(8,128)(2,1)S(1)}, u32[]{:S(2)}, u32[]{:S(2)}) async-start(bf16[16,32,128]{2,1,0:T(8,128)(2,1)} %update2.1), calls=%async_computation.4 | async-start | bytes 262144 | tf_op jit(solution)/shard_map/all_to_all | solution.py:201
  91.1 0.2 collective-permute-start.13
  91.3 0.3 collective-permute-start.14
  91.6 0.2 collective-permute-start.15
  91.8 0.3 collective-permute-start.16
  92.1 0.3 collective-permute-done.13.refs_4_
  92.5 0.2 collective-permute-done.14.refs_5_
  92.7 0.3 collective-permute-done.15.refs_6_
  93.0 0.2 collective-permute-done.16.refs_7_
  93.2 4.1 %all-to-all-done.4.gathered_ref = bf16[16,32,128]{2,1,0:T(8,128)(2,1)S(1)} async-done(((bf16[16,32,128]{2,1,0:T(8,128)(2,1)}), bf16[16,32,128]{2,1,0:T(8,128)(2,1)S(1)}, u32[]{:S(2)}, u32[]{:S(2)}) %all-to-all-start.4) | async-done | bytes 131104 | tf_op jit(solution)/shard_map/all_to_all | solution.py:201
  97.3 0.0 collective-permute-done.12.third_other_ref
  97.3 2.1 %final.1 = f32[4,32,64]{2,1,0:T(8,128)} custom-call(bf16[16,32,128]{2,1,0:T(8,128)(2,1)S(1)} %all-to-all-done.4.gathered_ref, bf16[64,512]{1,0:T(8,128)(2,1)S(1)} %copy-done.4, f32[32,64]{1,0:T(8,128)S(1)} %get-tuple-element.44.first_result_ref, f32[32,64]{1,0:T(8,128)S(1)} %get-tuple-element.45.second_result_ref, ...), custom_call_target="tpu_custom_call" | custom-call | flops 20000000 | bytes 1000000 | tf_op jit(solution)/shard_map/final/pallas_call | solution.py:163
  (16 shorter events, 0.2 us)
Async XLA Ops:
  0.0 0.8 copy-start
  0.0 1.1 %copy-start.1 = (f32[4,64,32]{1,2,0:T(8,128)S(1)}, f32[4,64,32]{1,2,0:T(8,128)}, u32[]{:S(2)}) copy-start(f32[4,64,32]{1,2,0:T(8,128)} %param.7) | copy-start | bytes 98308
  1.1 17.1 %copy-start.6 = (bf16[3,64,1024]{2,1,0:T(8,128)(2,1)S(1)}, bf16[3,64,1024]{2,1,0:T(8,128)(2,1)}, u32[]{:S(2)}) copy-start(bf16[3,64,1024]{2,1,0:T(8,128)(2,1)} %param.8) | copy-start | bytes 1179652
  1.9 13.3 %copy-start.5 = (bf16[64,1024]{1,0:T(8,128)(2,1)S(1)}, bf16[64,1024]{1,0:T(8,128)(2,1)}, u32[]{:S(2)}) copy-start(bf16[64,1024]{1,0:T(8,128)(2,1)} %param.12) | copy-start | bytes 393220
  1.9 26.5 %all-to-all-start = ((bf16[64,16,128]{2,1,0:T(8,128)(2,1)}), bf16[64,16,128]{2,1,0:T(8,128)(2,1)S(1)}, u32[]{:S(2)}, u32[]{:S(2)}) async-start(bf16[64,16,128]{2,1,0:T(8,128)(2,1)} %start.1), calls=%async_computation | async-start | bytes 524288 | tf_op jit(solution)/shard_map/all_to_all | solution.py:201
  15.2 13.2 %copy-start.2 = (bf16[64,4096]{1,0:T(8,128)(2,1)S(1)}, bf16[64,4096]{1,0:T(8,128)(2,1)}, u32[]{:S(2)}) copy-start(bf16[64,4096]{1,0:T(8,128)(2,1)} %inverse_ref.2) | copy-start | bytes 1572868
  15.2 14.3 %collective-permute-start = (bf16[1,64,1024]{2,1,0:T(8,128)(2,1)S(1)}, bf16[1,64,1024]{2,1,0:T(8,128)(2,1)S(1)}, u32[]{:S(2)}, u32[]{:S(2)}) collective-permute-start(bf16[1,64,1024]{2,1,0:T(8,128)(2,1)S(1)} %bitcast.56), channel_id=1, source_target_pairs={{0,16},{4,20},{8,24},{12,28},{16,0},{20,4},{24,8},{28,12},{32,48},... | collective-permute-start | bytes 393224 | tf_op jit(solution)/shard_map/ppermute | solution.py:211
  18.2 11.3 %collective-permute-start.3 = (bf16[64,1024]{1,0:T(8,128)(2,1)S(1)}, bf16[64,1024]{1,0:T(8,128)(2,1)S(1)}, u32[]{:S(2)}, u32[]{:S(2)}) collective-permute-start(bf16[64,1024]{1,0:T(8,128)(2,1)S(1)} %get-tuple-element.32.refs_0_), channel_id=1, source_target_pairs={{0,3},{1,0},{2,1},{3,2},{4,7},{5,4},{6,5},{7,6},{8,11},{9,8},{10,9... | collective-permute-start | bytes 393224 | tf_op jit(solution)/shard_map/ppermute | solution.py:207
  20.8 8.7 %collective-permute-start.2 = (bf16[64,1024]{1,0:T(8,128)(2,1)S(1)}, bf16[64,1024]{1,0:T(8,128)(2,1)S(1)}, u32[]{:S(2)}, u32[]{:S(2)}) collective-permute-start(bf16[64,1024]{1,0:T(8,128)(2,1)S(1)} %get-tuple-element.32.refs_0_), channel_id=1, source_target_pairs={{0,2},{1,3},{2,0},{3,1},{4,6},{5,7},{6,4},{7,5},{8,10},{9,11},{10,... | collective-permute-start | bytes 393224 | tf_op jit(solution)/shard_map/ppermute | solution.py:207
  21.3 9.1 %collective-permute-start.1 = (bf16[64,1024]{1,0:T(8,128)(2,1)S(1)}, bf16[64,1024]{1,0:T(8,128)(2,1)S(1)}, u32[]{:S(2)}, u32[]{:S(2)}) collective-permute-start(bf16[64,1024]{1,0:T(8,128)(2,1)S(1)} %get-tuple-element.32.refs_0_), channel_id=1, source_target_pairs={{0,1},{1,2},{2,3},{3,0},{4,5},{5,6},{6,7},{7,4},{8,9},{9,10},{10,1... | collective-permute-start | bytes 393224 | tf_op jit(solution)/shard_map/ppermute | solution.py:207
  30.3 21.7 %all-to-all-start.1 = ((bf16[64,16,128]{2,1,0:T(8,128)(2,1)}), bf16[64,16,128]{2,1,0:T(8,128)(2,1)S(1)}, u32[]{:S(2)}, u32[]{:S(2)}) async-start(bf16[64,16,128]{2,1,0:T(8,128)(2,1)} %get-tuple-element.31), calls=%async_computation.1 | async-start | bytes 524288 | tf_op jit(solution)/shard_map/all_to_all | solution.py:201
  38.9 7.5 %collective-permute-start.7 = (bf16[2,64,1024]{2,1,0:T(8,128)(2,1)S(1)}, bf16[2,64,1024]{2,1,0:T(8,128)(2,1)S(1)}, u32[]{:S(2)}, u32[]{:S(2)}) collective-permute-start(bf16[2,64,1024]{2,1,0:T(8,128)(2,1)S(1)} %slice.39), channel_id=1, source_target_pairs={{0,3},{1,0},{2,1},{3,2},{4,7},{5,4},{6,5},{7,6},{8,11},{9,8},{10,9... | collective-permute-start | bytes 786440 | tf_op jit(solution)/shard_map/ppermute | solution.py:207
  39.3 14.5 %collective-permute-start.4 = (bf16[2,64,1024]{2,1,0:T(8,128)(2,1)S(1)}, bf16[2,64,1024]{2,1,0:T(8,128)(2,1)S(1)}, u32[]{:S(2)}, u32[]{:S(2)}) collective-permute-start(bf16[2,64,1024]{2,1,0:T(8,128)(2,1)S(1)} %pad_maximum_fusion.2), channel_id=1, source_target_pairs={{0,32},{4,36},{8,40},{12,44},{16,48},{20,52},{24,56},{28,60},{32,0... | collective-permute-start | bytes 786440 | tf_op jit(solution)/shard_map/ppermute | solution.py:211
  40.8 20.7 %collective-permute-start.6 = (bf16[2,64,1024]{2,1,0:T(8,128)(2,1)S(1)}, bf16[2,64,1024]{2,1,0:T(8,128)(2,1)}, u32[]{:S(2)}, u32[]{:S(2)}) collective-permute-start(bf16[2,64,1024]{2,1,0:T(8,128)(2,1)S(1)} %slice.39), channel_id=1, source_target_pairs={{0,2},{1,3},{2,0},{3,1},{4,6},{5,7},{6,4},{7,5},{8,10},{9,11},{10,... | collective-permute-start | bytes 786440 | tf_op jit(solution)/shard_map/ppermute | solution.py:207
  41.3 31.4 %collective-permute-start.5 = (bf16[2,64,1024]{2,1,0:T(8,128)(2,1)S(1)}, bf16[2,64,1024]{2,1,0:T(8,128)(2,1)S(1)}, u32[]{:S(2)}, u32[]{:S(2)}) collective-permute-start(bf16[2,64,1024]{2,1,0:T(8,128)(2,1)S(1)} %slice.39), channel_id=1, source_target_pairs={{0,1},{1,2},{2,3},{3,0},{4,5},{5,6},{6,7},{7,4},{8,9},{9,10},{10,1... | collective-permute-start | bytes 786440 | tf_op jit(solution)/shard_map/ppermute | solution.py:207
  53.8 14.0 %all-to-all-start.2 = ((bf16[32,16,128]{2,1,0:T(8,128)(2,1)}), bf16[32,16,128]{2,1,0:T(8,128)(2,1)S(1)}, u32[]{:S(2)}, u32[]{:S(2)}) async-start(bf16[32,16,128]{2,1,0:T(8,128)(2,1)} %get-tuple-element.38), calls=%async_computation.2 | async-start | bytes 262144 | tf_op jit(solution)/shard_map/all_to_all | solution.py:201
  60.1 7.7 %copy-start.3 = (bf16[64,2048]{1,0:T(8,128)(2,1)S(1)}, bf16[64,2048]{1,0:T(8,128)(2,1)}, u32[]{:S(2)}) copy-start(bf16[64,2048]{1,0:T(8,128)(2,1)} %inverse_ref.3) | copy-start | bytes 786436
  60.1 23.4 %collective-permute-start.11 = (bf16[4,64,1024]{2,1,0:T(8,128)(2,1)}, bf16[4,64,1024]{2,1,0:T(8,128)(2,1)}, u32[]{:S(2)}, u32[]{:S(2)}) collective-permute-start(bf16[4,64,1024]{2,1,0:T(8,128)(2,1)} %pad_maximum_fusion.1), channel_id=1, source_target_pairs={{0,8},{4,12},{8,0},{12,4},{16,24},{20,28},{24,16},{28,20},{32,40},... | collective-permute-start | bytes 1572872 | tf_op jit(solution)/shard_map/ppermute | solution.py:211
  68.8 12.6 %all-to-all-start.3 = ((bf16[32,16,128]{2,1,0:T(8,128)(2,1)}), bf16[32,16,128]{2,1,0:T(8,128)(2,1)S(1)}, u32[]{:S(2)}, u32[]{:S(2)}) async-start(bf16[32,16,128]{2,1,0:T(8,128)(2,1)} %get-tuple-element.39), calls=%async_computation.3 | async-start | bytes 262144 | tf_op jit(solution)/shard_map/all_to_all | solution.py:201
  73.6 9.7 %collective-permute-start.10 = (bf16[1,64,1024]{2,1,0:T(8,128)(2,1)S(1)}, bf16[1,64,1024]{2,1,0:T(8,128)(2,1)S(1)}, u32[]{:S(2)}, u32[]{:S(2)}) collective-permute-start(bf16[1,64,1024]{2,1,0:T(8,128)(2,1)S(1)} %select.36.refs_0_), channel_id=1, source_target_pairs={{0,24},{4,28},{8,16},{12,20},{16,8},{20,12},{24,0},{28,4},{32,56},... | collective-permute-start | bytes 393224 | tf_op jit(solution)/shard_map/ppermute | solution.py:211
  76.3 7.0 %collective-permute-start.9 = (bf16[1,64,1024]{2,1,0:T(8,128)(2,1)S(1)}, bf16[1,64,1024]{2,1,0:T(8,128)(2,1)S(1)}, u32[]{:S(2)}, u32[]{:S(2)}) collective-permute-start(bf16[1,64,1024]{2,1,0:T(8,128)(2,1)S(1)} %select.36.refs_0_), channel_id=1, source_target_pairs={{0,16},{4,20},{8,24},{12,28},{16,0},{20,4},{24,8},{28,12},{32,48},... | collective-permute-start | bytes 393224 | tf_op jit(solution)/shard_map/ppermute | solution.py:211
  76.9 6.7 %collective-permute-start.8 = (bf16[1,64,1024]{2,1,0:T(8,128)(2,1)S(1)}, bf16[1,64,1024]{2,1,0:T(8,128)(2,1)S(1)}, u32[]{:S(2)}, u32[]{:S(2)}) collective-permute-start(bf16[1,64,1024]{2,1,0:T(8,128)(2,1)S(1)} %select.36.refs_0_), channel_id=1, source_target_pairs={{0,8},{4,12},{8,0},{12,4},{16,24},{20,28},{24,16},{28,20},{32,40},... | collective-permute-start | bytes 393224 | tf_op jit(solution)/shard_map/ppermute | solution.py:211
  84.7 12.5 %copy-start.4 = (bf16[64,512]{1,0:T(8,128)(2,1)S(1)}, bf16[64,512]{1,0:T(8,128)(2,1)}, u32[]{:S(2)}) copy-start(bf16[64,512]{1,0:T(8,128)(2,1)} %fourth_ref.1) | copy-start | bytes 196612
  84.7 12.5 %collective-permute-start.12 = (bf16[8,64,1024]{2,1,0:T(8,128)(2,1)S(1)}, bf16[8,64,1024]{2,1,0:T(8,128)(2,1)S(1)}, u32[]{:S(2)}, u32[]{:S(2)}) collective-permute-start(bf16[8,64,1024]{2,1,0:T(8,128)(2,1)S(1)} %pad_maximum_fusion.third_ref), channel_id=1, source_target_pairs={{0,4},{4,0},{8,12},{12,8},{16,20},{20,16},{24,28},{28,24},{32,36},... | collective-permute-start | bytes 3145736 | tf_op jit(solution)/shard_map/ppermute | solution.py:211
  86.2 11.1 %all-to-all-start.4 = ((bf16[16,32,128]{2,1,0:T(8,128)(2,1)}), bf16[16,32,128]{2,1,0:T(8,128)(2,1)S(1)}, u32[]{:S(2)}, u32[]{:S(2)}) async-start(bf16[16,32,128]{2,1,0:T(8,128)(2,1)} %update2.1), calls=%async_computation.4 | async-start | bytes 262144 | tf_op jit(solution)/shard_map/all_to_all | solution.py:201
  91.1 1.3 %collective-permute-start.13 = (bf16[1,64,1024]{2,1,0:T(8,128)(2,1)S(1)}, bf16[1,64,1024]{2,1,0:T(8,128)(2,1)S(1)}, u32[]{:S(2)}, u32[]{:S(2)}) collective-permute-start(bf16[1,64,1024]{2,1,0:T(8,128)(2,1)S(1)} %select.36.refs_0_), channel_id=1, source_target_pairs={{0,4},{4,0},{8,12},{12,8},{16,20},{20,16},{24,28},{28,24},{32,36},... | collective-permute-start | bytes 393224 | tf_op jit(solution)/shard_map/ppermute | solution.py:211
  91.3 1.3 %collective-permute-start.14 = (bf16[1,64,1024]{2,1,0:T(8,128)(2,1)S(1)}, bf16[1,64,1024]{2,1,0:T(8,128)(2,1)S(1)}, u32[]{:S(2)}, u32[]{:S(2)}) collective-permute-start(bf16[1,64,1024]{2,1,0:T(8,128)(2,1)S(1)} %collective-permute-done.8.refs_1_), channel_id=1, source_target_pairs={{0,4},{4,0},{8,12},{12,8},{16,20},{20,16},{24,28},{28,24},{32,36},... | collective-permute-start | bytes 393224 | tf_op jit(solution)/shard_map/ppermute | solution.py:211
  91.6 1.3 %collective-permute-start.15 = (bf16[1,64,1024]{2,1,0:T(8,128)(2,1)S(1)}, bf16[1,64,1024]{2,1,0:T(8,128)(2,1)S(1)}, u32[]{:S(2)}, u32[]{:S(2)}) collective-permute-start(bf16[1,64,1024]{2,1,0:T(8,128)(2,1)S(1)} %collective-permute-done.9.refs_2_), channel_id=1, source_target_pairs={{0,4},{4,0},{8,12},{12,8},{16,20},{20,16},{24,28},{28,24},{32,36},... | collective-permute-start | bytes 393224 | tf_op jit(solution)/shard_map/ppermute | solution.py:211
  91.8 1.3 %collective-permute-start.16 = (bf16[1,64,1024]{2,1,0:T(8,128)(2,1)S(1)}, bf16[1,64,1024]{2,1,0:T(8,128)(2,1)S(1)}, u32[]{:S(2)}, u32[]{:S(2)}) collective-permute-start(bf16[1,64,1024]{2,1,0:T(8,128)(2,1)S(1)} %collective-permute-done.10.refs_3_), channel_id=1, source_target_pairs={{0,4},{4,0},{8,12},{12,8},{16,20},{20,16},{24,28},{28,24},{32,36},... | collective-permute-start | bytes 393224 | tf_op jit(solution)/shard_map/ppermute | solution.py:211

commit v4 on v3

v4 whole, which is shorter than its diff:
```python
import functools

import jax
import jax.numpy as jnp
from jax import lax
from jax.experimental import pallas as pl
from jax.experimental.pallas import tpu as pltpu
from jax.sharding import PartitionSpec as P

BS = 128
NB = 32
LEVELS = 4
RB = 32


def pack(block, copies):
    half = block.shape[0] // 2
    packed = jnp.concatenate((block[:half], block[half:]), axis=1).astype(jnp.bfloat16)
    return jnp.broadcast_to(packed[None], (copies, *packed.shape))


def unpack(gathered, store):
    lanes = gathered.shape[2] // 2
    for b in range(gathered.shape[0] // 2):
        one, two = gathered[2 * b], gathered[2 * b + 1]
        top = jnp.concatenate((one[:, :lanes], two[:, :lanes]), axis=1)
        low = jnp.concatenate((one[:, lanes:], two[:, lanes:]), axis=1)
        store(b, jnp.concatenate((top, low), axis=0))


def dot_lanes(a, b):
    return lax.dot_general(a, b, (((1,), (1,)), ((), ())), preferred_element_type=jnp.float32)


def start_kernel(right_ref, message_ref):
    message_ref[...] = pack(right_ref[0], message_ref.shape[0])


def solve_kernel(gathered_ref, inverse_ref, result_ref, message_ref, flat_ref):
    def store(b, block):
        flat_ref[:, b * BS : (b + 1) * BS] = block

    unpack(gathered_ref, store)
    result = dot_lanes(flat_ref[...], inverse_ref[...])
    result_ref[...] = result
    message_ref[...] = pack(result, message_ref.shape[0])


def below_part(near_ref, far_ref, k, tier, tiers):
    ref = near_ref if k < 2 else far_ref
    return ref.at[k % 2 * tiers + tier]


def select_kernel(position_ref, near_ref, far_ref, out_ref):
    positions = position_ref[...]
    part = near_ref.shape[2] // BS
    tiers = near_ref.shape[0] // 2
    for j in range(out_ref.shape[2] // BS):
        at = positions[0, j]
        for k in range(RB // part):

            @pl.when(at // part == k)
            def _():
                columns = pl.ds(pl.multiple_of(at % part * BS, BS), BS)
                block = below_part(near_ref, far_ref, k, tiers - 1, tiers)[:, columns]
                out_ref[0, :, j * BS : (j + 1) * BS] = block


def join(mine, other, core):
    first = jnp.where(core == 0, mine, other)
    second = jnp.where(core == 0, other, mine)
    return jnp.concatenate((first, second), axis=1)


def position():
    own = lax.axis_index("sn")
    return own % 2, own // 2 % 4, own // 8 % 2


def product_kernel(coupled_ref, *refs):
    third, out_ref = refs[:-1], refs[-1]
    core, y, z = position()
    total = None
    for g, ref in enumerate(third):
        picked = []
        for e in range(ref.shape[0]):
            block = (z ^ (e // 2)) * 4 + (y ^ (e % 2 * 2 + g % 2))
            columns = coupled_ref[0, :, pl.ds(pl.multiple_of(block * BS, BS), BS)]
            half = columns.shape[1] // 2
            first = core == g // 2
            picked.append(jnp.where(first, columns[:, :half], columns[:, half:]))
        rows = ref[...].reshape(ref.shape[0] * ref.shape[1], ref.shape[2])
        term = jnp.dot(
            jnp.concatenate(picked, axis=1), rows, preferred_element_type=jnp.float32
        )
        total = term if total is None else total + term
    out_ref[0] = total.astype(out_ref.dtype)


def final_kernel(
    pieces, gathered_ref, third_ref, fourth_ref, first_result_ref, second_result_ref, *refs
):
    parent, parent_other = refs[:pieces], refs[pieces : 2 * pieces]
    out_ref, flat_ref, coupled_ref, last_ref = refs[2 * pieces :]
    core, y, z = position()
    half = gathered_ref.shape[1] // 2
    devices = gathered_ref.shape[0]

    def store(b, block):
        flat_ref[:, b * BS : (b + 1) * BS] = block

    def store_last(b, block):
        last_ref[:, b * BS : (b + 1) * BS] = block

    unpack(gathered_ref[:, :half], store)
    in_plane = pl.ds(pl.multiple_of(z * (devices // 2), devices // 2), devices // 2)
    unpack(gathered_ref[in_plane, half:], store_last)
    out_ref[0] = first_result_ref[...]
    out_ref[1] = second_result_ref[...]
    out_ref[2] = dot_lanes(flat_ref[...], third_ref[...])
    for e in range(pieces):
        mine = dot_lanes(flat_ref[...], parent[e][0])
        other = dot_lanes(flat_ref[...], parent_other[e][0])
        columns = pl.ds(pl.multiple_of((y ^ e) * BS, BS), BS)
        coupled_ref[:, columns] = join(mine, other, core)
    update = last_ref[...].astype(jnp.float32) - coupled_ref[...]
    out_ref[3] = dot_lanes(update.astype(jnp.bfloat16), fourth_ref[...])


def place(chosen, own_block):
    found, base = chosen, NB
    for l in range(1, LEVELS - 1):
        count = NB >> l
        mine = own_block // count * count
        at = chosen - l * NB - mine + base
        if l == LEVELS - 2:
            at = jnp.full_like(chosen, base)
        found = jnp.where(chosen // NB == l, at, found)
        base += count
    return found


def update_kernel(tiers, kept, index_ref, gathered_ref, right_ref, near_ref, far_ref, *refs):
    known_ref, flat_ref = refs[-2], refs[-1]
    base = 0
    if not kept:
        base = refs[0].shape[0]
        known_ref[:base] = refs[0][...]
        refs = refs[1:]
    message_ref = refs[0]

    def store(b, block):
        known_ref[base + b] = block

    unpack(gathered_ref, store)
    if kept:
        refs[1][...] = known_ref[...]
    else:
        known_ref[known_ref.shape[0] - 1] = jnp.zeros(known_ref.shape[1:], known_ref.dtype)
    places = index_ref[...]
    quarter = near_ref.shape[2] // BS
    parts = RB // quarter
    slot = 0
    packed = []
    for t, tier in enumerate(tiers):
        total = right_ref[tier]
        for k in range(parts):
            ref = below_part(near_ref, far_ref, k, t, len(tiers))
            for p in range(quarter):
                block = known_ref[places[tier - 1, k * quarter + p]]
                flat_ref[slot, :, p * BS : (p + 1) * BS] = block
            total = total - dot_lanes(flat_ref[slot], ref[...])
            slot += 1
        packed.append(pack(total, message_ref.shape[0]))
    message_ref[...] = jnp.concatenate(packed, axis=1)


VMEM = pl.BlockSpec(memory_space=pltpu.VMEM)


def held(*arrays):
    return [pltpu.with_memory_space_constraint(array, pltpu.HBM) for array in arrays]


def call(kernel, name, outs, scratch, *args):
    return pl.pallas_call(
        kernel,
        out_shape=outs,
        in_specs=[VMEM] * len(args),
        out_specs=[VMEM] * len(outs),
        scratch_shapes=scratch,
        cost_estimate=pl.CostEstimate(flops=20_000_000, bytes_accessed=1_000_000, transcendentals=0),
        compiler_params=pltpu.CompilerParams(vmem_limit_bytes=16 * 2**20),
        name=name,
    )(*args)


def on_device(
    right_sides,
    factor_below,
    row_blocks,
    inverse_top,
    inverse_second,
    inverse_third,
    inverse_fourth,
):
    _, rows, columns = right_sides.shape
    right_sides = jnp.swapaxes(right_sides, 1, 2)
    devices = lax.axis_size("sn")
    groups = lax.axis_size("rhs")
    column_group = lax.axis_index("rhs")
    own = lax.axis_index("sn")
    f32, bf16 = jnp.float32, jnp.bfloat16
    shape = jax.ShapeDtypeStruct
    message = (columns // 2, 2 * rows)
    members = [devices >> l for l in range(LEVELS)]
    barrier = lax.optimization_barrier

    def gather(copies):
        n = copies.shape[0]
        sets = None
        if n < devices:
            sets = [list(range(s, s + n)) for s in range(0, devices, n)]
        return lax.all_to_all(copies, "sn", 0, 0, axis_index_groups=sets)

    def swap_group(part, bit):
        return lax.ppermute(part, "rhs", [(i, i ^ bit) for i in range(groups)])

    def swap(part, bit):
        return lax.ppermute(part, "sn", [(i, i ^ bit) for i in range(devices)])

    core, y_low, y_high, z_low = 1, 2, 4, 8

    def over_y(part):
        return [part] + [swap(part, bits) for bits in (y_low, y_high, y_low + y_high)]

    own_block = own * rows // BS
    chosen = lax.dynamic_index_in_dim(row_blocks, own_block, 1, keepdims=False)
    places = place(chosen, own_block)
    quarter = RB // groups
    part = jnp.arange(groups)
    source = (column_group ^ part)[:, None] == part[None, :]
    listed = places.reshape(LEVELS - 1, 1, groups, quarter)
    places = jnp.sum(jnp.where(source[None, :, :, None], listed, 0), axis=2)
    places = places.reshape(LEVELS - 1, RB)
    count = NB >> (LEVELS - 2)
    parent = (LEVELS - 2) * NB + own_block // count * count + jnp.arange(count)
    listed = jnp.arange(RB)
    turned = (column_group ^ listed // quarter) * quarter + listed % quarter
    hit = chosen[LEVELS - 2][None, :] == parent[:, None]
    positions = jnp.sum(jnp.where(hit, turned[None, :], 0), axis=1)[None].astype(jnp.int32)
    places, positions, right_sides = barrier((places, positions, right_sides))

    below = factor_below
    below_got = swap_group(below, 1)
    third = inverse_third[None]
    third_got = [swap(third, bits) for bits in (y_high, z_low, y_high + z_low)]

    (copies,) = call(start_kernel, "start", [shape((members[0], *message), bf16)], [], right_sides)
    gathered = gather(copies)
    first_result, copies = call(
        solve_kernel,
        "solve0",
        [shape((columns, rows), f32), shape((members[0], *message), bf16)],
        [pltpu.VMEM((columns, members[0] * rows), bf16)],
        gathered,
        inverse_top,
    )

    copies, third_got, below_got = barrier((copies, third_got, below_got))
    first_below = jnp.stack((below[0], below_got[0]))
    first_far = swap_group(first_below, 2)
    rest_below = jnp.concatenate((below[1:], below_got[1:]))
    rest_far = swap_group(rest_below, 2)
    third = jnp.concatenate((third, *third_got))
    third_got = swap(third, y_low)

    gathered = gather(copies)
    copies, known = call(
        functools.partial(update_kernel, (1,), True),
        "update1",
        [shape((members[1], *message), bf16), shape((NB, columns, BS), bf16)],
        [pltpu.VMEM((NB, columns, BS), bf16), pltpu.VMEM((groups, columns, RB // groups * BS), bf16)],
        places,
        gathered,
        right_sides,
        first_below,
        first_far,
    )

    copies, third_got = barrier((copies, third_got))
    third = [third, third_got]
    third = third + [swap(part, core) for part in third]
    (coupled,) = call(
        select_kernel, "select", [shape((1, rows, count * BS), bf16)], [], positions, rest_below, rest_far
    )

    gathered = gather(copies)
    second_result, copies = call(
        solve_kernel,
        "solve1",
        [shape((columns, rows), f32), shape((members[1], *message), bf16)],
        [pltpu.VMEM((columns, members[1] * rows), bf16)],
        gathered,
        inverse_second,
    )

    copies, coupled, third = barrier((copies, coupled, third))
    (coupled,) = call(
        product_kernel, "product", [shape(coupled.shape, bf16)], [], coupled, *held(*third)
    )
    coupled = over_y(coupled)

    gathered = gather(copies)
    blocks = NB + NB // 2 + 1
    (copies,) = call(
        functools.partial(update_kernel, (2, 3), False),
        "update2",
        [shape((members[2], 2 * message[0], message[1]), bf16)],
        [pltpu.VMEM((blocks, columns, BS), bf16), pltpu.VMEM((2 * groups, columns, RB // groups * BS), bf16)],
        places,
        gathered,
        right_sides,
        rest_below,
        rest_far,
        known,
    )

    coupled_other = [swap(part, core) for part in coupled]

    gathered = gather(copies)
    (out,) = call(
        functools.partial(final_kernel, len(coupled)),
        "final",
        [shape((LEVELS, columns, rows), f32)],
        [
            pltpu.VMEM((columns, members[2] * rows), bf16),
            pltpu.VMEM((columns, members[3] * rows), f32),
            pltpu.VMEM((columns, members[3] * rows), bf16),
        ],
        gathered,
        inverse_third,
        inverse_fourth,
        first_result,
        second_result,
        *coupled,
        *coupled_other,
    )
    return jnp.swapaxes(out, 1, 2)


def solution(mesh):
    in_specs = (
        P(None, "sn", "rhs"),
        P(None, "sn", "rhs"),
        P(),
        P("sn", None),
        P("sn", None),
        P("sn", None),
        P("sn", None),
    )
    out_specs = P(None, "sn", "rhs")
    return jax.shard_map(
        on_device, mesh=mesh, in_specs=in_specs, out_specs=out_specs, check_vma=False
    )
```

time: 99.9 us -> 97.6 us (0.977)
  other arithmetic: 2.23 us -> 0.53 us
  waiting for transfers between devices: 32.6 us -> 31 us
    all_to_all x5, waiting for transfers between devices: 26 us -> 23.7 us  [gather(): return lax.all_to_all(copies, 'sn', 0, 0, axis_index_groups=sets)]
    concatenate x3 -> x2, other arithmetic: 2.02 us -> 0.12 us  [the longest x1 0.07 us: on_device(): third = jnp.concatenate((third, *third_got))]
    ppermute x11 -> x13, waiting for transfers between devices: 1.29 us -> 2.43 us  [swap(): return lax.ppermute(part, 'sn', [(i, i ^ bit) for i in range(devices)])]
    ppermute x6 -> x3, waiting for transfers between devices: 5.32 us -> 4.85 us  [swap_group(): return lax.ppermute(part, 'rhs', [(i, i ^ bit) for i in range(groups)])]
    pallas_call x7 -> x8, Pallas kernels: 9.4 us -> 9.85 us  [call(): pl.pallas_call(kernel, out_shape=outs, in_specs=[VMEM] * len(args), out_s...]
    ppermute x11 -> x13, starting transfers between devices: 11.7 us -> 11.3 us  [swap(): return lax.ppermute(part, 'sn', [(i, i ^ bit) for i in range(devices)])]
    ppermute x6 -> x3, starting transfers between devices: 5.23 us -> 5.08 us  [swap_group(): return lax.ppermute(part, 'rhs', [(i, i ^ bit) for i in range(groups)])]
  transfers between devices with their start and end apart: 22 -> 21, of which waited for: 12 -> 10; matrix products, arithmetic and copies ran while one was open for 2% -> 1% of each run, Pallas kernels for 7% -> 8%
where the time goes in v4:
time: 97.6 us; the launch traced here: 97.1 us
  starting transfers between devices  52.9 us (54%)
  waiting for transfers between devices  31 us (32%)
  Pallas kernels  9.85 us (10%)
  local copies, waits for them, and re-layouts  2.58 us (3%)
    all_to_all x5, starting transfers between devices, gather(): return lax.all_to_all(copies, 'sn', 0, 0, axis_index_groups=sets)  36.5 us
    all_to_all x5, waiting for transfers between devices, gather(): return lax.all_to_all(copies, 'sn', 0, 0, axis_index_groups=sets)  23.7 us
    ppermute x13, starting transfers between devices, swap(): return lax.ppermute(part, 'sn', [(i, i ^ bit) for i in range(devices)])  11.3 us
    pallas_call x8, Pallas kernels, call(): pl.pallas_call(kernel, out_shape=outs, in_specs=[VMEM] * len(args), out_s...  9.85 us
    ppermute x3, starting transfers between devices, swap_group(): return lax.ppermute(part, 'rhs', [(i, i ^ bit) for i in range(groups)])  5.08 us
    ppermute x3, waiting for transfers between devices, swap_group(): return lax.ppermute(part, 'rhs', [(i, i ^ bit) for i in range(groups)])  4.85 us
    ppermute x13, waiting for transfers between devices, swap(): return lax.ppermute(part, 'sn', [(i, i ^ bit) for i in range(devices)])  2.43 us
  transfers between devices with their start and end apart: 21, of which 10 were waited for; matrix products, arithmetic and copies ran while one was open for 1% of the time, Pallas kernels for 8%

profile of v4, /device:TPU:1, one launch (start us, length us, event | category | flops | bytes accessed | tf_op | source)
XLA Modules:
  0.0 97.1 jit_solution(96992055245488512)
XLA Ops:
  0.0 0.0 copy-start
  0.1 0.7 copy-done
  0.9 0.1 squeeze.4
  0.9 0.1 iota_compare_fusion
  1.0 0.1 select_reduce_fusion
  1.1 0.1 reshape.100.index_ref
  1.2 0.2 select_reduce_fusion.1
  1.4 0.8 start.1
  2.2 13.3 %all-to-all-start = ((bf16[64,16,128]{2,1,0:T(8,128)(2,1)}), bf16[64,16,128]{2,1,0:T(8,128)(2,1)S(1)}, u32[]{:S(2)}, u32[]{:S(2)}) async-start(bf16[64,16,128]{2,1,0:T(8,128)(2,1)} %start.1), calls=%async_computation | async-start | bytes 524288 | tf_op jit(solution)/shard_map/all_to_all | solution.py:224
  15.5 1.3 %collective-permute-start.3 = (bf16[3,64,1024]{2,1,0:T(8,128)(2,1)}, bf16[3,64,1024]{2,1,0:T(8,128)(2,1)S(1)}, u32[]{:S(2)}, u32[]{:S(2)}) collective-permute-start(bf16[3,64,1024]{2,1,0:T(8,128)(2,1)} %param.8), channel_id=1, source_target_pairs={{0,1},{1,0},{2,3},{3,2},{4,5},{5,4},{6,7},{7,6},{8,9},{9,8},{10,11... | collective-permute-start | bytes 1179656 | tf_op jit(solution)/shard_map/ppermute | solution.py:227
  16.8 2.9 %collective-permute-start = (bf16[1,64,1024]{2,1,0:T(8,128)(2,1)S(1)}, bf16[1,64,1024]{2,1,0:T(8,128)(2,1)S(1)}, u32[]{:S(2)}, u32[]{:S(2)}) collective-permute-start(bf16[1,64,1024]{2,1,0:T(8,128)(2,1)S(1)} %bitcast.9), channel_id=1, source_target_pairs={{0,16},{4,20},{8,24},{12,28},{16,0},{20,4},{24,8},{28,12},{32,48},... | collective-permute-start | bytes 393224 | tf_op jit(solution)/shard_map/ppermute | solution.py:230
  19.7 1.2 %collective-permute-start.1 = (bf16[1,64,1024]{2,1,0:T(8,128)(2,1)S(1)}, bf16[1,64,1024]{2,1,0:T(8,128)(2,1)S(1)}, u32[]{:S(2)}, u32[]{:S(2)}) collective-permute-start(bf16[1,64,1024]{2,1,0:T(8,128)(2,1)S(1)} %bitcast.10), channel_id=1, source_target_pairs={{0,32},{4,36},{8,40},{12,44},{16,48},{20,52},{24,56},{28,60},{32,0... | collective-permute-start | bytes 393224 | tf_op jit(solution)/shard_map/ppermute | solution.py:230
  20.9 0.1 collective-permute-start.2
  21.0 7.7 %all-to-all-done.gathered_ref = bf16[64,16,128]{2,1,0:T(8,128)(2,1)S(1)} async-done(((bf16[64,16,128]{2,1,0:T(8,128)(2,1)}), bf16[64,16,128]{2,1,0:T(8,128)(2,1)S(1)}, u32[]{:S(2)}, u32[]{:S(2)}) %all-to-all-start) | async-done | bytes 262176 | tf_op jit(solution)/shard_map/all_to_all | solution.py:224
  28.7 1.1 %solve0.1 = (f32[32,64]{1,0:T(8,128)S(1)}, bf16[64,16,128]{2,1,0:T(8,128)(2,1)}) custom-call(bf16[64,16,128]{2,1,0:T(8,128)(2,1)S(1)} %all-to-all-done.gathered_ref, bf16[64,4096]{1,0:T(8,128)(2,1)S(1)} %copy-done.2), custom_call_target="tpu_custom_call" | custom-call | flops 20000000 | bytes 1000000 | tf_op jit(solution)/shard_map/solve0/pallas_call | solution.py:186
  29.8 0.0 collective-permute-done
  29.8 0.0 collective-permute-done.1
  29.8 1.3 %collective-permute-done.2 = bf16[1,64,1024]{2,1,0:T(8,128)(2,1)S(1)} collective-permute-done((bf16[1,64,1024]{2,1,0:T(8,128)(2,1)S(1)}, bf16[1,64,1024]{2,1,0:T(8,128)(2,1)S(1)}, u32[]{:S(2)}, u32[]{:S(2)}) %collective-permute-start.2) | collective-permute-done | bytes 131104 | tf_op jit(solution)/shard_map/ppermute | solution.py:230
  31.1 0.0 collective-permute-done.3
  31.1 0.1 pad_maximum_fusion.refs_0_
  31.2 0.7 copy-done.9
  31.9 0.3 collective-permute-start.5
  32.2 9.1 %all-to-all-start.1 = ((bf16[64,16,128]{2,1,0:T(8,128)(2,1)}), bf16[64,16,128]{2,1,0:T(8,128)(2,1)S(1)}, u32[]{:S(2)}, u32[]{:S(2)}) async-start(bf16[64,16,128]{2,1,0:T(8,128)(2,1)} %get-tuple-element.30), calls=%async_computation.1 | async-start | bytes 524288 | tf_op jit(solution)/shard_map/all_to_all | solution.py:224
  41.3 0.0 copy-done.8
  41.3 0.9 slice.18
  42.3 2.8 %collective-permute-start.4 = (bf16[2,64,1024]{2,1,0:T(8,128)(2,1)S(1)}, bf16[2,64,1024]{2,1,0:T(8,128)(2,1)S(1)}, u32[]{:S(2)}, u32[]{:S(2)}) collective-permute-start(bf16[2,64,1024]{2,1,0:T(8,128)(2,1)S(1)} %pad_maximum_fusion.2.near_ref), channel_id=1, source_target_pairs={{0,2},{1,3},{2,0},{3,1},{4,6},{5,7},{6,4},{7,5},{8,10},{9,11},{10,... | collective-permute-start | bytes 786440 | tf_op jit(solution)/shard_map/ppermute | solution.py:227
  45.2 0.0 copy-done.10
  45.2 0.9 collective-permute-start.6
  46.2 0.7 collective-permute-start.7
  46.9 4.4 %collective-permute-done.4.far_ref = bf16[2,64,1024]{2,1,0:T(8,128)(2,1)S(1)} collective-permute-done((bf16[2,64,1024]{2,1,0:T(8,128)(2,1)S(1)}, bf16[2,64,1024]{2,1,0:T(8,128)(2,1)S(1)}, u32[]{:S(2)}, u32[]{:S(2)}) %collective-permute-start.4) | collective-permute-done | bytes 262176 | tf_op jit(solution)/shard_map/ppermute | solution.py:227
  51.3 3.2 %all-to-all-done.1.gathered_ref = bf16[64,16,128]{2,1,0:T(8,128)(2,1)S(1)} async-done(((bf16[64,16,128]{2,1,0:T(8,128)(2,1)}), bf16[64,16,128]{2,1,0:T(8,128)(2,1)S(1)}, u32[]{:S(2)}, u32[]{:S(2)}) %all-to-all-start.1) | async-done | bytes 262176 | tf_op jit(solution)/shard_map/all_to_all | solution.py:224
  54.5 1.2 %update1.1 = (bf16[32,16,128]{2,1,0:T(8,128)(2,1)}, bf16[32,32,128]{2,1,0:T(8,128)(2,1)S(1)}) custom-call(s32[3,32]{1,0:T(4,128)S(1)} %reshape.100.index_ref, bf16[64,16,128]{2,1,0:T(8,128)(2,1)S(1)} %all-to-all-done.1.gathered_ref, f32[4,32,64]{2,1,0:T(8,128)S(1)} %bitcast.7, bf16[2,64,1024]{2,1,0:T(8,128)(2,1)S(1)} %pad_maximum_fusion.2.near_ref, ...), custom_call_target="tpu_custom_call" | custom-call | flops 20000000 | bytes 1000000 | tf_op jit(solution)/shard_map/update1/pallas_call | solution.py:186
  55.6 0.0 collective-permute-done.5.refs_1_
  55.7 0.3 collective-permute-start.8
  55.9 6.2 %all-to-all-start.2 = ((bf16[32,16,128]{2,1,0:T(8,128)(2,1)}), bf16[32,16,128]{2,1,0:T(8,128)(2,1)S(1)}, u32[]{:S(2)}, u32[]{:S(2)}) async-start(bf16[32,16,128]{2,1,0:T(8,128)(2,1)} %get-tuple-element.36), calls=%async_computation.2 | async-start | bytes 262144 | tf_op jit(solution)/shard_map/all_to_all | solution.py:224
  62.1 0.0 copy-start.4
  62.1 0.5 collective-permute-done.6.far_ref
  62.6 1.0 %select.40.coupled_ref = bf16[1,64,1024]{2,1,0:T(8,128)(2,1)S(1)} custom-call(s32[1,8]{1,0:T(1,128)S(1)} %bitcast.13, bf16[4,64,1024]{2,1,0:T(8,128)(2,1)S(1)} %pad_maximum_fusion.1.near_ref, bf16[4,64,1024]{2,1,0:T(8,128)(2,1)S(1)} %collective-permute-done.6.far_ref), custom_call_target="tpu_custom_call" | custom-call | flops 20000000 | bytes 1000000 | tf_op jit(solution)/shard_map/select/pallas_call | solution.py:186
  63.6 0.0 copy-done.7
  63.6 7.1 %all-to-all-done.2.gathered_ref = bf16[32,16,128]{2,1,0:T(8,128)(2,1)S(1)} async-done(((bf16[32,16,128]{2,1,0:T(8,128)(2,1)}), bf16[32,16,128]{2,1,0:T(8,128)(2,1)S(1)}, u32[]{:S(2)}, u32[]{:S(2)}) %all-to-all-start.2) | async-done | bytes 131104 | tf_op jit(solution)/shard_map/all_to_all | solution.py:224
  70.6 1.0 %solve1.1 = (f32[32,64]{1,0:T(8,128)S(1)}, bf16[32,16,128]{2,1,0:T(8,128)(2,1)}) custom-call(bf16[32,16,128]{2,1,0:T(8,128)(2,1)S(1)} %all-to-all-done.2.gathered_ref, bf16[64,2048]{1,0:T(8,128)(2,1)S(1)} %copy-done.4), custom_call_target="tpu_custom_call" | custom-call | flops 20000000 | bytes 1000000 | tf_op jit(solution)/shard_map/solve1/pallas_call | solution.py:186
  71.6 0.0 collective-permute-done.7.refs_2_
  71.6 0.0 collective-permute-done.8.refs_3_
  71.6 3.9 %all-to-all-start.3 = ((bf16[32,16,128]{2,1,0:T(8,128)(2,1)}), bf16[32,16,128]{2,1,0:T(8,128)(2,1)S(1)}, u32[]{:S(2)}, u32[]{:S(2)}) async-start(bf16[32,16,128]{2,1,0:T(8,128)(2,1)} %get-tuple-element.40), calls=%async_computation.3 | async-start | bytes 262144 | tf_op jit(solution)/shard_map/all_to_all | solution.py:224
  75.5 2.1 %product.1.refs_0_ = bf16[1,64,1024]{2,1,0:T(8,128)(2,1)S(1)} custom-call(bf16[1,64,1024]{2,1,0:T(8,128)(2,1)S(1)} %select.40.coupled_ref, bf16[4,64,1024]{2,1,0:T(8,128)(2,1)} %copy-done.6, bf16[4,64,1024]{2,1,0:T(8,128)(2,1)} %copy-done.7, bf16[4,64,1024]{2,1,0:T(8,128)(2,1)} %collective-permute-done.7.refs_2_, ...), custom_call_target="tpu_custom_call" | custom-call | flops 20000000 | bytes 1000000 | tf_op jit(solution)/shard_map/product/pallas_call | solution.py:186
  77.7 1.5 %collective-permute-start.9 = (bf16[1,64,1024]{2,1,0:T(8,128)(2,1)S(1)}, bf16[1,64,1024]{2,1,0:T(8,128)(2,1)S(1)}, u32[]{:S(2)}, u32[]{:S(2)}) collective-permute-start(bf16[1,64,1024]{2,1,0:T(8,128)(2,1)S(1)} %product.1.refs_0_), channel_id=1, source_target_pairs={{0,8},{4,12},{8,0},{12,4},{16,24},{20,28},{24,16},{28,20},{32,40},... | collective-permute-start | bytes 393224 | tf_op jit(solution)/shard_map/ppermute | solution.py:230
  79.1 2.4 %collective-permute-start.10 = (bf16[1,64,1024]{2,1,0:T(8,128)(2,1)S(1)}, bf16[1,64,1024]{2,1,0:T(8,128)(2,1)S(1)}, u32[]{:S(2)}, u32[]{:S(2)}) collective-permute-start(bf16[1,64,1024]{2,1,0:T(8,128)(2,1)S(1)} %product.1.refs_0_), channel_id=1, source_target_pairs={{0,16},{4,20},{8,24},{12,28},{16,0},{20,4},{24,8},{28,12},{32,48},... | collective-permute-start | bytes 393224 | tf_op jit(solution)/shard_map/ppermute | solution.py:230
  81.6 0.1 collective-permute-start.11
  81.6 2.5 %all-to-all-done.3.gathered_ref = bf16[32,16,128]{2,1,0:T(8,128)(2,1)S(1)} async-done(((bf16[32,16,128]{2,1,0:T(8,128)(2,1)}), bf16[32,16,128]{2,1,0:T(8,128)(2,1)S(1)}, u32[]{:S(2)}, u32[]{:S(2)}) %all-to-all-start.3) | async-done | bytes 131104 | tf_op jit(solution)/shard_map/all_to_all | solution.py:224
  84.2 1.3 %update2.1 = bf16[16,32,128]{2,1,0:T(8,128)(2,1)} custom-call(s32[3,32]{1,0:T(4,128)S(1)} %reshape.100.index_ref, bf16[32,16,128]{2,1,0:T(8,128)(2,1)S(1)} %all-to-all-done.3.gathered_ref, f32[4,32,64]{2,1,0:T(8,128)S(1)} %bitcast.8, bf16[4,64,1024]{2,1,0:T(8,128)(2,1)S(1)} %pad_maximum_fusion.1.near_ref, ...), custom_call_target="tpu_custom_call" | custom-call | flops 20000000 | bytes 1000000 | tf_op jit(solution)/shard_map/update2/pallas_call | solution.py:186
  85.5 4.0 %all-to-all-start.4 = ((bf16[16,32,128]{2,1,0:T(8,128)(2,1)}), bf16[16,32,128]{2,1,0:T(8,128)(2,1)S(1)}, u32[]{:S(2)}, u32[]{:S(2)}) async-start(bf16[16,32,128]{2,1,0:T(8,128)(2,1)} %update2.1), calls=%async_computation.4 | async-start | bytes 262144 | tf_op jit(solution)/shard_map/all_to_all | solution.py:224
  89.5 0.3 collective-permute-start.12
  89.8 0.0 collective-permute-done.9.refs_1_
  89.8 0.2 collective-permute-start.13
  90.0 0.0 collective-permute-done.10.refs_2_
  90.0 0.3 collective-permute-start.14
  90.3 0.1 collective-permute-done.11.refs_3_
  90.4 1.1 %collective-permute-start.15 = (bf16[1,64,1024]{2,1,0:T(8,128)(2,1)S(1)}, bf16[1,64,1024]{2,1,0:T(8,128)(2,1)S(1)}, u32[]{:S(2)}, u32[]{:S(2)}) collective-permute-start(bf16[1,64,1024]{2,1,0:T(8,128)(2,1)S(1)} %collective-permute-done.11.refs_3_), channel_id=1, source_target_pairs={{0,4},{4,0},{8,12},{12,8},{16,20},{20,16},{24,28},{28,24},{32,36},... | collective-permute-start | bytes 393224 | tf_op jit(solution)/shard_map/ppermute | solution.py:230
  91.5 0.0 collective-permute-done.12.refs_4_
  91.5 0.0 collective-permute-done.13.refs_5_
  91.5 0.0 collective-permute-done.14.refs_6_
  91.5 1.0 %collective-permute-done.15.refs_7_ = bf16[1,64,1024]{2,1,0:T(8,128)(2,1)S(1)} collective-permute-done((bf16[1,64,1024]{2,1,0:T(8,128)(2,1)S(1)}, bf16[1,64,1024]{2,1,0:T(8,128)(2,1)S(1)}, u32[]{:S(2)}, u32[]{:S(2)}) %collective-permute-start.15) | collective-permute-done | bytes 131104 | tf_op jit(solution)/shard_map/ppermute | solution.py:230
  92.5 3.2 %all-to-all-done.4.gathered_ref = bf16[16,32,128]{2,1,0:T(8,128)(2,1)S(1)} async-done(((bf16[16,32,128]{2,1,0:T(8,128)(2,1)}), bf16[16,32,128]{2,1,0:T(8,128)(2,1)S(1)}, u32[]{:S(2)}, u32[]{:S(2)}) %all-to-all-start.4) | async-done | bytes 131104 | tf_op jit(solution)/shard_map/all_to_all | solution.py:224
  95.7 1.4 %final.1 = f32[4,32,64]{2,1,0:T(8,128)} custom-call(bf16[16,32,128]{2,1,0:T(8,128)(2,1)S(1)} %all-to-all-done.4.gathered_ref, bf16[64,1024]{1,0:T(8,128)(2,1)S(1)} %copy-done.3, bf16[64,512]{1,0:T(8,128)(2,1)S(1)} %copy-done.5, f32[32,64]{1,0:T(8,128)S(1)} %get-tuple-element.42.first_result_ref, f32[32,64]{1,0:T(8,128)S(1)} %get-tuple-element.43.second_result_ref, ...), custom_call_target="tpu_custom_call" | custom-call | flops 20000000 | bytes 1000000 | tf_op jit(solution)/shard_map/final/pallas_call | solution.py:186
  (26 shorter events, 0.2 us)
Async XLA Ops:
  0.0 0.8 copy-start
  0.0 1.4 %copy-start.1 = (f32[4,64,32]{1,2,0:T(8,128)S(1)}, f32[4,64,32]{1,2,0:T(8,128)}, u32[]{:S(2)}) copy-start(f32[4,64,32]{1,2,0:T(8,128)} %param.7) | copy-start | bytes 98308
  0.0 28.7 %copy-start.2 = (bf16[64,4096]{1,0:T(8,128)(2,1)S(1)}, bf16[64,4096]{1,0:T(8,128)(2,1)}, u32[]{:S(2)}) copy-start(bf16[64,4096]{1,0:T(8,128)(2,1)} %inverse_ref.2) | copy-start | bytes 1572868
  2.2 14.6 %copy-start.3 = (bf16[64,1024]{1,0:T(8,128)(2,1)S(1)}, bf16[64,1024]{1,0:T(8,128)(2,1)}, u32[]{:S(2)}) copy-start(bf16[64,1024]{1,0:T(8,128)(2,1)} %third_ref.1) | copy-start | bytes 393220
  2.2 26.5 %all-to-all-start = ((bf16[64,16,128]{2,1,0:T(8,128)(2,1)}), bf16[64,16,128]{2,1,0:T(8,128)(2,1)S(1)}, u32[]{:S(2)}, u32[]{:S(2)}) async-start(bf16[64,16,128]{2,1,0:T(8,128)(2,1)} %start.1), calls=%async_computation | async-start | bytes 524288 | tf_op jit(solution)/shard_map/all_to_all | solution.py:224
  15.5 15.6 %collective-permute-start.3 = (bf16[3,64,1024]{2,1,0:T(8,128)(2,1)}, bf16[3,64,1024]{2,1,0:T(8,128)(2,1)S(1)}, u32[]{:S(2)}, u32[]{:S(2)}) collective-permute-start(bf16[3,64,1024]{2,1,0:T(8,128)(2,1)} %param.8), channel_id=1, source_target_pairs={{0,1},{1,0},{2,3},{3,2},{4,5},{5,4},{6,7},{7,6},{8,9},{9,8},{10,11... | collective-permute-start | bytes 1179656 | tf_op jit(solution)/shard_map/ppermute | solution.py:227
  16.8 13.0 %collective-permute-start = (bf16[1,64,1024]{2,1,0:T(8,128)(2,1)S(1)}, bf16[1,64,1024]{2,1,0:T(8,128)(2,1)S(1)}, u32[]{:S(2)}, u32[]{:S(2)}) collective-permute-start(bf16[1,64,1024]{2,1,0:T(8,128)(2,1)S(1)} %bitcast.9), channel_id=1, source_target_pairs={{0,16},{4,20},{8,24},{12,28},{16,0},{20,4},{24,8},{28,12},{32,48},... | collective-permute-start | bytes 393224 | tf_op jit(solution)/shard_map/ppermute | solution.py:230
  19.7 10.1 %collective-permute-start.1 = (bf16[1,64,1024]{2,1,0:T(8,128)(2,1)S(1)}, bf16[1,64,1024]{2,1,0:T(8,128)(2,1)S(1)}, u32[]{:S(2)}, u32[]{:S(2)}) collective-permute-start(bf16[1,64,1024]{2,1,0:T(8,128)(2,1)S(1)} %bitcast.10), channel_id=1, source_target_pairs={{0,32},{4,36},{8,40},{12,44},{16,48},{20,52},{24,56},{28,60},{32,0... | collective-permute-start | bytes 393224 | tf_op jit(solution)/shard_map/ppermute | solution.py:230
  20.9 10.3 %collective-permute-start.2 = (bf16[1,64,1024]{2,1,0:T(8,128)(2,1)S(1)}, bf16[1,64,1024]{2,1,0:T(8,128)(2,1)S(1)}, u32[]{:S(2)}, u32[]{:S(2)}) collective-permute-start(bf16[1,64,1024]{2,1,0:T(8,128)(2,1)S(1)} %bitcast.11), channel_id=1, source_target_pairs={{0,48},{4,52},{8,56},{12,60},{16,32},{20,36},{24,40},{28,44},{32,1... | collective-permute-start | bytes 393224 | tf_op jit(solution)/shard_map/ppermute | solution.py:230
  31.1 0.7 copy-start.9
  31.9 14.3 %copy-start.6 = (bf16[4,64,1024]{2,1,0:T(8,128)(2,1)}, bf16[4,64,1024]{2,1,0:T(8,128)(2,1)S(1)}, u32[]{:S(2)}) copy-start(bf16[4,64,1024]{2,1,0:T(8,128)(2,1)S(1)} %pad_maximum_fusion.refs_0_) | copy-start | bytes 1572868
  31.9 9.4 %copy-start.8 = (bf16[3,64,1024]{2,1,0:T(8,128)(2,1)S(1)}, bf16[3,64,1024]{2,1,0:T(8,128)(2,1)}, u32[]{:S(2)}) copy-start(bf16[3,64,1024]{2,1,0:T(8,128)(2,1)} %param.8) | copy-start | bytes 1179652
  31.9 23.8 %collective-permute-start.5 = (bf16[4,64,1024]{2,1,0:T(8,128)(2,1)S(1)}, bf16[4,64,1024]{2,1,0:T(8,128)(2,1)S(1)}, u32[]{:S(2)}, u32[]{:S(2)}) collective-permute-start(bf16[4,64,1024]{2,1,0:T(8,128)(2,1)S(1)} %pad_maximum_fusion.refs_0_), channel_id=1, source_target_pairs={{0,8},{4,12},{8,0},{12,4},{16,24},{20,28},{24,16},{28,20},{32,40},... | collective-permute-start | bytes 1572872 | tf_op jit(solution)/shard_map/ppermute | solution.py:230
  32.2 22.3 %all-to-all-start.1 = ((bf16[64,16,128]{2,1,0:T(8,128)(2,1)}), bf16[64,16,128]{2,1,0:T(8,128)(2,1)S(1)}, u32[]{:S(2)}, u32[]{:S(2)}) async-start(bf16[64,16,128]{2,1,0:T(8,128)(2,1)} %get-tuple-element.30), calls=%async_computation.1 | async-start | bytes 524288 | tf_op jit(solution)/shard_map/all_to_all | solution.py:224
  42.3 2.9 %copy-start.10 = (bf16[3,64,1024]{2,1,0:T(8,128)(2,1)S(1)}, bf16[3,64,1024]{2,1,0:T(8,128)(2,1)}, u32[]{:S(2)}) copy-start(bf16[3,64,1024]{2,1,0:T(8,128)(2,1)} %copy-done.9) | copy-start | bytes 1179652
  42.3 9.0 %collective-permute-start.4 = (bf16[2,64,1024]{2,1,0:T(8,128)(2,1)S(1)}, bf16[2,64,1024]{2,1,0:T(8,128)(2,1)S(1)}, u32[]{:S(2)}, u32[]{:S(2)}) collective-permute-start(bf16[2,64,1024]{2,1,0:T(8,128)(2,1)S(1)} %pad_maximum_fusion.2.near_ref), channel_id=1, source_target_pairs={{0,2},{1,3},{2,0},{3,1},{4,6},{5,7},{6,4},{7,5},{8,10},{9,11},{10,... | collective-permute-start | bytes 786440 | tf_op jit(solution)/shard_map/ppermute | solution.py:227
  45.2 17.3 %collective-permute-start.6 = (bf16[4,64,1024]{2,1,0:T(8,128)(2,1)S(1)}, bf16[4,64,1024]{2,1,0:T(8,128)(2,1)S(1)}, u32[]{:S(2)}, u32[]{:S(2)}) collective-permute-start(bf16[4,64,1024]{2,1,0:T(8,128)(2,1)S(1)} %pad_maximum_fusion.1.near_ref), channel_id=1, source_target_pairs={{0,2},{1,3},{2,0},{3,1},{4,6},{5,7},{6,4},{7,5},{8,10},{9,11},{10,... | collective-permute-start | bytes 1572872 | tf_op jit(solution)/shard_map/ppermute | solution.py:227
  46.2 25.4 %collective-permute-start.7 = (bf16[4,64,1024]{2,1,0:T(8,128)(2,1)S(1)}, bf16[4,64,1024]{2,1,0:T(8,128)(2,1)}, u32[]{:S(2)}, u32[]{:S(2)}) collective-permute-start(bf16[4,64,1024]{2,1,0:T(8,128)(2,1)S(1)} %pad_maximum_fusion.refs_0_), channel_id=1, source_target_pairs={{0,4},{4,0},{8,12},{12,8},{16,20},{20,16},{24,28},{28,24},{32,36},... | collective-permute-start | bytes 1572872 | tf_op jit(solution)/shard_map/ppermute | solution.py:230
  55.7 7.9 %copy-start.7 = (bf16[4,64,1024]{2,1,0:T(8,128)(2,1)}, bf16[4,64,1024]{2,1,0:T(8,128)(2,1)S(1)}, u32[]{:S(2)}) copy-start(bf16[4,64,1024]{2,1,0:T(8,128)(2,1)S(1)} %collective-permute-done.5.refs_1_) | copy-start | bytes 1572868
  55.7 16.0 %collective-permute-start.8 = (bf16[4,64,1024]{2,1,0:T(8,128)(2,1)S(1)}, bf16[4,64,1024]{2,1,0:T(8,128)(2,1)}, u32[]{:S(2)}, u32[]{:S(2)}) collective-permute-start(bf16[4,64,1024]{2,1,0:T(8,128)(2,1)S(1)} %collective-permute-done.5.refs_1_), channel_id=1, source_target_pairs={{0,4},{4,0},{8,12},{12,8},{16,20},{20,16},{24,28},{28,24},{32,36},... | collective-permute-start | bytes 1572872 | tf_op jit(solution)/shard_map/ppermute | solution.py:230
  55.9 14.7 %all-to-all-start.2 = ((bf16[32,16,128]{2,1,0:T(8,128)(2,1)}), bf16[32,16,128]{2,1,0:T(8,128)(2,1)S(1)}, u32[]{:S(2)}, u32[]{:S(2)}) async-start(bf16[32,16,128]{2,1,0:T(8,128)(2,1)} %get-tuple-element.36), calls=%async_computation.2 | async-start | bytes 262144 | tf_op jit(solution)/shard_map/all_to_all | solution.py:224
  62.1 8.5 %copy-start.4 = (bf16[64,2048]{1,0:T(8,128)(2,1)S(1)}, bf16[64,2048]{1,0:T(8,128)(2,1)}, u32[]{:S(2)}) copy-start(bf16[64,2048]{1,0:T(8,128)(2,1)} %inverse_ref.3) | copy-start | bytes 786436
  71.6 12.6 %all-to-all-start.3 = ((bf16[32,16,128]{2,1,0:T(8,128)(2,1)}), bf16[32,16,128]{2,1,0:T(8,128)(2,1)S(1)}, u32[]{:S(2)}, u32[]{:S(2)}) async-start(bf16[32,16,128]{2,1,0:T(8,128)(2,1)} %get-tuple-element.40), calls=%async_computation.3 | async-start | bytes 262144 | tf_op jit(solution)/shard_map/all_to_all | solution.py:224
  77.7 12.1 %collective-permute-start.9 = (bf16[1,64,1024]{2,1,0:T(8,128)(2,1)S(1)}, bf16[1,64,1024]{2,1,0:T(8,128)(2,1)S(1)}, u32[]{:S(2)}, u32[]{:S(2)}) collective-permute-start(bf16[1,64,1024]{2,1,0:T(8,128)(2,1)S(1)} %product.1.refs_0_), channel_id=1, source_target_pairs={{0,8},{4,12},{8,0},{12,4},{16,24},{20,28},{24,16},{28,20},{32,40},... | collective-permute-start | bytes 393224 | tf_op jit(solution)/shard_map/ppermute | solution.py:230
  79.1 10.8 %collective-permute-start.10 = (bf16[1,64,1024]{2,1,0:T(8,128)(2,1)S(1)}, bf16[1,64,1024]{2,1,0:T(8,128)(2,1)S(1)}, u32[]{:S(2)}, u32[]{:S(2)}) collective-permute-start(bf16[1,64,1024]{2,1,0:T(8,128)(2,1)S(1)} %product.1.refs_0_), channel_id=1, source_target_pairs={{0,16},{4,20},{8,24},{12,28},{16,0},{20,4},{24,8},{28,12},{32,48},... | collective-permute-start | bytes 393224 | tf_op jit(solution)/shard_map/ppermute | solution.py:230
  81.6 8.8 %collective-permute-start.11 = (bf16[1,64,1024]{2,1,0:T(8,128)(2,1)S(1)}, bf16[1,64,1024]{2,1,0:T(8,128)(2,1)S(1)}, u32[]{:S(2)}, u32[]{:S(2)}) collective-permute-start(bf16[1,64,1024]{2,1,0:T(8,128)(2,1)S(1)} %product.1.refs_0_), channel_id=1, source_target_pairs={{0,24},{4,28},{8,16},{12,20},{16,8},{20,12},{24,0},{28,4},{32,56},... | collective-permute-start | bytes 393224 | tf_op jit(solution)/shard_map/ppermute | solution.py:230
  85.5 10.2 %copy-start.5 = (bf16[64,512]{1,0:T(8,128)(2,1)S(1)}, bf16[64,512]{1,0:T(8,128)(2,1)}, u32[]{:S(2)}) copy-start(bf16[64,512]{1,0:T(8,128)(2,1)} %fourth_ref.1) | copy-start | bytes 196612
  85.5 10.2 %all-to-all-start.4 = ((bf16[16,32,128]{2,1,0:T(8,128)(2,1)}), bf16[16,32,128]{2,1,0:T(8,128)(2,1)S(1)}, u32[]{:S(2)}, u32[]{:S(2)}) async-start(bf16[16,32,128]{2,1,0:T(8,128)(2,1)} %update2.1), calls=%async_computation.4 | async-start | bytes 262144 | tf_op jit(solution)/shard_map/all_to_all | solution.py:224
  89.5 2.0 %collective-permute-start.12 = (bf16[1,64,1024]{2,1,0:T(8,128)(2,1)S(1)}, bf16[1,64,1024]{2,1,0:T(8,128)(2,1)S(1)}, u32[]{:S(2)}, u32[]{:S(2)}) collective-permute-start(bf16[1,64,1024]{2,1,0:T(8,128)(2,1)S(1)} %product.1.refs_0_), channel_id=1, source_target_pairs={{0,4},{4,0},{8,12},{12,8},{16,20},{20,16},{24,28},{28,24},{32,36},... | collective-permute-start | bytes 393224 | tf_op jit(solution)/shard_map/ppermute | solution.py:230
  89.8 1.7 %collective-permute-start.13 = (bf16[1,64,1024]{2,1,0:T(8,128)(2,1)S(1)}, bf16[1,64,1024]{2,1,0:T(8,128)(2,1)S(1)}, u32[]{:S(2)}, u32[]{:S(2)}) collective-permute-start(bf16[1,64,1024]{2,1,0:T(8,128)(2,1)S(1)} %collective-permute-done.9.refs_1_), channel_id=1, source_target_pairs={{0,4},{4,0},{8,12},{12,8},{16,20},{20,16},{24,28},{28,24},{32,36},... | collective-permute-start | bytes 393224 | tf_op jit(solution)/shard_map/ppermute | solution.py:230
  90.0 1.5 %collective-permute-start.14 = (bf16[1,64,1024]{2,1,0:T(8,128)(2,1)S(1)}, bf16[1,64,1024]{2,1,0:T(8,128)(2,1)S(1)}, u32[]{:S(2)}, u32[]{:S(2)}) collective-permute-start(bf16[1,64,1024]{2,1,0:T(8,128)(2,1)S(1)} %collective-permute-done.10.refs_2_), channel_id=1, source_target_pairs={{0,4},{4,0},{8,12},{12,8},{16,20},{20,16},{24,28},{28,24},{32,36},... | collective-permute-start | bytes 393224 | tf_op jit(solution)/shard_map/ppermute | solution.py:230
  90.4 2.1 %collective-permute-start.15 = (bf16[1,64,1024]{2,1,0:T(8,128)(2,1)S(1)}, bf16[1,64,1024]{2,1,0:T(8,128)(2,1)S(1)}, u32[]{:S(2)}, u32[]{:S(2)}) collective-permute-start(bf16[1,64,1024]{2,1,0:T(8,128)(2,1)S(1)} %collective-permute-done.11.refs_3_), channel_id=1, source_target_pairs={{0,4},{4,0},{8,12},{12,8},{16,20},{20,16},{24,28},{28,24},{32,36},... | collective-permute-start | bytes 393224 | tf_op jit(solution)/shard_map/ppermute | solution.py:230

commit v5 on v4

--- a/solution.py
+++ b/solution.py
@@ -81,9 +81,10 @@
     third, out_ref = refs[:-1], refs[-1]
     core, y, z = position()
     total = None
-    for g, ref in enumerate(third):
+    for n, ref in enumerate(third):
+        g = n % 4
         picked = []
-        for e in range(ref.shape[0]):
+        for e in range(ref.shape[0]) if n < 4 else (3,):
             block = (z ^ (e // 2)) * 4 + (y ^ (e % 2 * 2 + g % 2))
             columns = coupled_ref[0, :, pl.ds(pl.multiple_of(block * BS, BS), BS)]
             half = columns.shape[1] // 2
@@ -254,7 +255,7 @@
     below = factor_below
     below_got = swap_group(below, 1)
     third = inverse_third[None]
-    third_got = [swap(third, bits) for bits in (y_high, z_low, y_high + z_low)]
+    far, near = swap(third, y_high), swap(third, z_low)
 
     (copies,) = call(start_kernel, "start", [shape((members[0], *message), bf16)], [], right_sides)
     gathered = gather(copies)
@@ -267,13 +268,14 @@
         inverse_top,
     )
 
-    copies, third_got, below_got = barrier((copies, third_got, below_got))
+    copies, (far, near), below_got = barrier((copies, (far, near), below_got))
     first_below = jnp.stack((below[0], below_got[0]))
     first_far = swap_group(first_below, 2)
     rest_below = jnp.concatenate((below[1:], below_got[1:]))
     rest_far = swap_group(rest_below, 2)
-    third = jnp.concatenate((third, *third_got))
+    third = jnp.concatenate((third, far, near))
     third_got = swap(third, y_low)
+    corner = swap(far, z_low)
 
     gathered = gather(copies)
     copies, known = call(
@@ -288,9 +290,11 @@
         first_far,
     )
 
-    copies, third_got = barrier((copies, third_got))
+    copies, third_got, corner = barrier((copies, third_got, corner))
+    corner = [corner, swap(corner, y_low)]
     third = [third, third_got]
     third = third + [swap(part, core) for part in third]
+    corner = corner + [swap(part, core) for part in corner]
     (coupled,) = call(
         select_kernel, "select", [shape((1, rows, count * BS), bf16)], [], positions, rest_below, rest_far
     )
@@ -306,8 +310,9 @@
     )
 
     copies, coupled, third = barrier((copies, coupled, third))
+    third = third + corner
     (coupled,) = call(
-        product_kernel, "product", [shape(coupled.shape, bf16)], [], coupled, *held(*third)
+        product_kernel, "product", [shape(coupled.shape, bf16)], [], coupled, *held(*third[:4]), *third[4:]
     )
     coupled = over_y(coupled)
 

time: 97.6 us -> 95.6 us (0.980)
  waiting for transfers between devices: 31 us -> 25.5 us
  starting transfers between devices: 52.9 us -> 57.9 us
  local copies, waits for them, and re-layouts: 2.58 us -> 1.05 us
    ppermute x13 -> x16, starting transfers between devices: 11.3 us -> 16.1 us  [swap(): return lax.ppermute(part, 'sn', [(i, i ^ bit) for i in range(devices)])]
    all_to_all x5, waiting for transfers between devices: 23.7 us -> 20.3 us  [gather(): return lax.all_to_all(copies, 'sn', 0, 0, axis_index_groups=sets)]
    ppermute x3, waiting for transfers between devices: 4.85 us -> 2.52 us  [swap_group(): return lax.ppermute(part, 'rhs', [(i, i ^ bit) for i in range(groups)])]
    ppermute x13 -> x16, waiting for transfers between devices: 2.43 us -> 2.67 us  [swap(): return lax.ppermute(part, 'sn', [(i, i ^ bit) for i in range(devices)])]
  transfers between devices with their start and end apart: 21 -> 24, of which waited for: 10 -> 10; matrix products, arithmetic and copies ran while one was open for 1% -> 0% of each run, Pallas kernels for 8% -> 8%
where the time goes in v5:
time: 95.6 us; the launch traced here: 95 us
  starting transfers between devices  57.9 us (61%)
  waiting for transfers between devices  25.5 us (27%)
  Pallas kernels  9.82 us (10%)
  local copies, waits for them, and re-layouts  1.05 us (1%)
    all_to_all x5, starting transfers between devices, gather(): return lax.all_to_all(copies, 'sn', 0, 0, axis_index_groups=sets)  36.7 us
    all_to_all x5, waiting for transfers between devices, gather(): return lax.all_to_all(copies, 'sn', 0, 0, axis_index_groups=sets)  20.3 us
    ppermute x16, starting transfers between devices, swap(): return lax.ppermute(part, 'sn', [(i, i ^ bit) for i in range(devices)])  16.1 us
    pallas_call x8, Pallas kernels, call(): pl.pallas_call(kernel, out_shape=outs, in_specs=[VMEM] * len(args), out_s...  9.82 us
    ppermute x3, starting transfers between devices, swap_group(): return lax.ppermute(part, 'rhs', [(i, i ^ bit) for i in range(groups)])  5.08 us
    ppermute x16, waiting for transfers between devices, swap(): return lax.ppermute(part, 'sn', [(i, i ^ bit) for i in range(devices)])  2.67 us
    ppermute x3, waiting for transfers between devices, swap_group(): return lax.ppermute(part, 'rhs', [(i, i ^ bit) for i in range(groups)])  2.52 us
  transfers between devices with their start and end apart: 24, of which 10 were waited for; matrix products, arithmetic and copies ran while one was open for 0% of the time, Pallas kernels for 8%

profile of v5, /device:TPU:1, one launch (start us, length us, event | category | flops | bytes accessed | tf_op | source)
XLA Modules:
  0.0 95.0 jit_solution(11991196385460193859)
XLA Ops:
  0.1 0.7 copy-done
  0.8 0.1 squeeze.4
  0.9 0.1 iota_compare_fusion
  1.0 0.1 select_reduce_fusion
  1.1 0.1 reshape.100.index_ref
  1.2 0.2 select_reduce_fusion.1
  1.4 0.8 start.1
  2.2 13.3 %all-to-all-start = ((bf16[64,16,128]{2,1,0:T(8,128)(2,1)}), bf16[64,16,128]{2,1,0:T(8,128)(2,1)S(1)}, u32[]{:S(2)}, u32[]{:S(2)}) async-start(bf16[64,16,128]{2,1,0:T(8,128)(2,1)} %start.1), calls=%async_computation | async-start | bytes 524288 | tf_op jit(solution)/shard_map/all_to_all | solution.py:225
  15.5 1.3 %collective-permute-start.2 = (bf16[3,64,1024]{2,1,0:T(8,128)(2,1)}, bf16[3,64,1024]{2,1,0:T(8,128)(2,1)S(1)}, u32[]{:S(2)}, u32[]{:S(2)}) collective-permute-start(bf16[3,64,1024]{2,1,0:T(8,128)(2,1)} %param.8), channel_id=1, source_target_pairs={{0,1},{1,0},{2,3},{3,2},{4,5},{5,4},{6,7},{7,6},{8,9},{9,8},{10,11... | collective-permute-start | bytes 1179656 | tf_op jit(solution)/shard_map/ppermute | solution.py:228
  16.8 2.9 %collective-permute-start = (bf16[1,64,1024]{2,1,0:T(8,128)(2,1)S(1)}, bf16[1,64,1024]{2,1,0:T(8,128)(2,1)S(1)}, u32[]{:S(2)}, u32[]{:S(2)}) collective-permute-start(bf16[1,64,1024]{2,1,0:T(8,128)(2,1)S(1)} %bitcast.9), channel_id=1, source_target_pairs={{0,16},{4,20},{8,24},{12,28},{16,0},{20,4},{24,8},{28,12},{32,48},... | collective-permute-start | bytes 393224 | tf_op jit(solution)/shard_map/ppermute | solution.py:231
  19.7 1.2 %collective-permute-start.1 = (bf16[1,64,1024]{2,1,0:T(8,128)(2,1)S(1)}, bf16[1,64,1024]{2,1,0:T(8,128)(2,1)S(1)}, u32[]{:S(2)}, u32[]{:S(2)}) collective-permute-start(bf16[1,64,1024]{2,1,0:T(8,128)(2,1)S(1)} %bitcast.10), channel_id=1, source_target_pairs={{0,32},{4,36},{8,40},{12,44},{16,48},{20,52},{24,56},{28,60},{32,0... | collective-permute-start | bytes 393224 | tf_op jit(solution)/shard_map/ppermute | solution.py:231
  20.8 7.8 %all-to-all-done.gathered_ref = bf16[64,16,128]{2,1,0:T(8,128)(2,1)S(1)} async-done(((bf16[64,16,128]{2,1,0:T(8,128)(2,1)}), bf16[64,16,128]{2,1,0:T(8,128)(2,1)S(1)}, u32[]{:S(2)}, u32[]{:S(2)}) %all-to-all-start) | async-done | bytes 262176 | tf_op jit(solution)/shard_map/all_to_all | solution.py:225
  28.6 1.1 %solve0.1 = (f32[32,64]{1,0:T(8,128)S(1)}, bf16[64,16,128]{2,1,0:T(8,128)(2,1)}) custom-call(bf16[64,16,128]{2,1,0:T(8,128)(2,1)S(1)} %all-to-all-done.gathered_ref, bf16[64,4096]{1,0:T(8,128)(2,1)S(1)} %copy-done.2), custom_call_target="tpu_custom_call" | custom-call | flops 20000000 | bytes 1000000 | tf_op jit(solution)/shard_map/solve0/pallas_call | solution.py:187
  29.8 0.0 collective-permute-done
  29.8 0.0 collective-permute-done.1
  29.8 0.0 collective-permute-done.2
  29.8 7.4 %all-to-all-start.1 = ((bf16[64,16,128]{2,1,0:T(8,128)(2,1)}), bf16[64,16,128]{2,1,0:T(8,128)(2,1)S(1)}, u32[]{:S(2)}, u32[]{:S(2)}) async-start(bf16[64,16,128]{2,1,0:T(8,128)(2,1)} %get-tuple-element.30), calls=%async_computation.1 | async-start | bytes 524288 | tf_op jit(solution)/shard_map/all_to_all | solution.py:225
  37.2 0.0 copy-start.8
  37.3 1.5 %collective-permute-start.4 = (bf16[3,64,1024]{2,1,0:T(8,128)(2,1)S(1)}, bf16[3,64,1024]{2,1,0:T(8,128)(2,1)S(1)}, u32[]{:S(2)}, u32[]{:S(2)}) collective-permute-start(bf16[3,64,1024]{2,1,0:T(8,128)(2,1)S(1)} %pad_maximum_fusion.1.refs_0_), channel_id=1, source_target_pairs={{0,8},{4,12},{8,0},{12,4},{16,24},{20,28},{24,16},{28,20},{32,40},... | collective-permute-start | bytes 1179656 | tf_op jit(solution)/shard_map/ppermute | solution.py:231
  38.9 2.8 %collective-permute-start.3 = (bf16[2,64,1024]{2,1,0:T(8,128)(2,1)S(1)}, bf16[2,64,1024]{2,1,0:T(8,128)(2,1)S(1)}, u32[]{:S(2)}, u32[]{:S(2)}) collective-permute-start(bf16[2,64,1024]{2,1,0:T(8,128)(2,1)S(1)} %pad_maximum_fusion.2.near_ref), channel_id=1, source_target_pairs={{0,2},{1,3},{2,0},{3,1},{4,6},{5,7},{6,4},{7,5},{8,10},{9,11},{10,... | collective-permute-start | bytes 786440 | tf_op jit(solution)/shard_map/ppermute | solution.py:228
  41.8 0.9 collective-permute-start.6
  42.8 1.2 %collective-permute-start.5 = (bf16[1,64,1024]{2,1,0:T(8,128)(2,1)S(1)}, bf16[1,64,1024]{2,1,0:T(8,128)(2,1)S(1)}, u32[]{:S(2)}, u32[]{:S(2)}) collective-permute-start(bf16[1,64,1024]{2,1,0:T(8,128)(2,1)S(1)} %collective-permute-done), channel_id=1, source_target_pairs={{0,32},{4,36},{8,40},{12,44},{16,48},{20,52},{24,56},{28,60},{32,0... | collective-permute-start | bytes 393224 | tf_op jit(solution)/shard_map/ppermute | solution.py:231
  44.0 1.2 %collective-permute-start.7 = (bf16[3,64,1024]{2,1,0:T(8,128)(2,1)S(1)}, bf16[3,64,1024]{2,1,0:T(8,128)(2,1)}, u32[]{:S(2)}, u32[]{:S(2)}) collective-permute-start(bf16[3,64,1024]{2,1,0:T(8,128)(2,1)S(1)} %pad_maximum_fusion.1.refs_0_), channel_id=1, source_target_pairs={{0,4},{4,0},{8,12},{12,8},{16,20},{20,16},{24,28},{28,24},{32,36},... | collective-permute-start | bytes 1179656 | tf_op jit(solution)/shard_map/ppermute | solution.py:231
  45.2 2.5 %collective-permute-done.3.far_ref = bf16[2,64,1024]{2,1,0:T(8,128)(2,1)S(1)} collective-permute-done((bf16[2,64,1024]{2,1,0:T(8,128)(2,1)S(1)}, bf16[2,64,1024]{2,1,0:T(8,128)(2,1)S(1)}, u32[]{:S(2)}, u32[]{:S(2)}) %collective-permute-start.3) | collective-permute-done | bytes 262176 | tf_op jit(solution)/shard_map/ppermute | solution.py:228
  47.7 2.7 %all-to-all-done.1.gathered_ref = bf16[64,16,128]{2,1,0:T(8,128)(2,1)S(1)} async-done(((bf16[64,16,128]{2,1,0:T(8,128)(2,1)}), bf16[64,16,128]{2,1,0:T(8,128)(2,1)S(1)}, u32[]{:S(2)}, u32[]{:S(2)}) %all-to-all-start.1) | async-done | bytes 262176 | tf_op jit(solution)/shard_map/all_to_all | solution.py:225
  50.4 1.2 %update1.1 = (bf16[32,16,128]{2,1,0:T(8,128)(2,1)}, bf16[32,32,128]{2,1,0:T(8,128)(2,1)S(1)}) custom-call(s32[3,32]{1,0:T(4,128)S(1)} %reshape.100.index_ref, bf16[64,16,128]{2,1,0:T(8,128)(2,1)S(1)} %all-to-all-done.1.gathered_ref, f32[4,32,64]{2,1,0:T(8,128)S(1)} %bitcast.7, bf16[2,64,1024]{2,1,0:T(8,128)(2,1)S(1)} %pad_maximum_fusion.2.near_ref, ...), custom_call_target="tpu_custom_call" | custom-call | flops 20000000 | bytes 1000000 | tf_op jit(solution)/shard_map/update1/pallas_call | solution.py:187
  51.6 0.0 collective-permute-done.5.refs_4_
  51.6 0.0 collective-permute-done.4.refs_1_
  51.6 0.3 collective-permute-start.8
  52.0 6.6 %all-to-all-start.2 = ((bf16[32,16,128]{2,1,0:T(8,128)(2,1)}), bf16[32,16,128]{2,1,0:T(8,128)(2,1)S(1)}, u32[]{:S(2)}, u32[]{:S(2)}) async-start(bf16[32,16,128]{2,1,0:T(8,128)(2,1)} %get-tuple-element.35), calls=%async_computation.2 | async-start | bytes 262144 | tf_op jit(solution)/shard_map/all_to_all | solution.py:225
  58.6 0.0 copy-start.4
  58.6 1.5 %collective-permute-start.9 = (bf16[1,64,1024]{2,1,0:T(8,128)(2,1)S(1)}, bf16[1,64,1024]{2,1,0:T(8,128)(2,1)S(1)}, u32[]{:S(2)}, u32[]{:S(2)}) collective-permute-start(bf16[1,64,1024]{2,1,0:T(8,128)(2,1)S(1)} %collective-permute-done.5.refs_4_), channel_id=1, source_target_pairs={{0,8},{4,12},{8,0},{12,4},{16,24},{20,28},{24,16},{28,20},{32,40},... | collective-permute-start | bytes 393224 | tf_op jit(solution)/shard_map/ppermute | solution.py:231
  60.1 0.0 collective-permute-done.6.far_ref
  60.1 1.0 %select.40.coupled_ref = bf16[1,64,1024]{2,1,0:T(8,128)(2,1)S(1)} custom-call(s32[1,8]{1,0:T(1,128)S(1)} %bitcast.12, bf16[4,64,1024]{2,1,0:T(8,128)(2,1)S(1)} %pad_maximum_fusion.near_ref, bf16[4,64,1024]{2,1,0:T(8,128)(2,1)S(1)} %collective-permute-done.6.far_ref), custom_call_target="tpu_custom_call" | custom-call | flops 20000000 | bytes 1000000 | tf_op jit(solution)/shard_map/select/pallas_call | solution.py:187
  61.1 6.1 %all-to-all-done.2.gathered_ref = bf16[32,16,128]{2,1,0:T(8,128)(2,1)S(1)} async-done(((bf16[32,16,128]{2,1,0:T(8,128)(2,1)}), bf16[32,16,128]{2,1,0:T(8,128)(2,1)S(1)}, u32[]{:S(2)}, u32[]{:S(2)}) %all-to-all-start.2) | async-done | bytes 131104 | tf_op jit(solution)/shard_map/all_to_all | solution.py:225
  67.2 1.0 %solve1.1 = (f32[32,64]{1,0:T(8,128)S(1)}, bf16[32,16,128]{2,1,0:T(8,128)(2,1)}) custom-call(bf16[32,16,128]{2,1,0:T(8,128)(2,1)S(1)} %all-to-all-done.2.gathered_ref, bf16[64,2048]{1,0:T(8,128)(2,1)S(1)} %copy-done.4), custom_call_target="tpu_custom_call" | custom-call | flops 20000000 | bytes 1000000 | tf_op jit(solution)/shard_map/solve1/pallas_call | solution.py:187
  68.2 0.0 collective-permute-done.7.refs_2_
  68.2 0.0 collective-permute-done.8.refs_3_
  68.2 3.9 %all-to-all-start.3 = ((bf16[32,16,128]{2,1,0:T(8,128)(2,1)}), bf16[32,16,128]{2,1,0:T(8,128)(2,1)S(1)}, u32[]{:S(2)}, u32[]{:S(2)}) async-start(bf16[32,16,128]{2,1,0:T(8,128)(2,1)} %get-tuple-element.39), calls=%async_computation.3 | async-start | bytes 262144 | tf_op jit(solution)/shard_map/all_to_all | solution.py:225
  72.1 0.4 collective-permute-start.10
  72.5 0.0 collective-permute-done.9.refs_5_
  72.5 0.2 collective-permute-start.11
  72.7 0.8 collective-permute-done.10.refs_6_
  73.5 0.4 collective-permute-done.11.refs_7_
  73.9 2.1 %product.1.refs_0_ = bf16[1,64,1024]{2,1,0:T(8,128)(2,1)S(1)} custom-call(bf16[1,64,1024]{2,1,0:T(8,128)(2,1)S(1)} %select.40.coupled_ref, bf16[3,64,1024]{2,1,0:T(8,128)(2,1)} %copy-done.6, bf16[3,64,1024]{2,1,0:T(8,128)(2,1)} %copy-done.7, bf16[3,64,1024]{2,1,0:T(8,128)(2,1)} %collective-permute-done.7.refs_2_, ...), custom_call_target="tpu_custom_call" | custom-call | flops 20000000 | bytes 1000000 | tf_op jit(solution)/shard_map/product/pallas_call | solution.py:187
  76.0 1.5 %collective-permute-start.12 = (bf16[1,64,1024]{2,1,0:T(8,128)(2,1)S(1)}, bf16[1,64,1024]{2,1,0:T(8,128)(2,1)S(1)}, u32[]{:S(2)}, u32[]{:S(2)}) collective-permute-start(bf16[1,64,1024]{2,1,0:T(8,128)(2,1)S(1)} %product.1.refs_0_), channel_id=1, source_target_pairs={{0,8},{4,12},{8,0},{12,4},{16,24},{20,28},{24,16},{28,20},{32,40},... | collective-permute-start | bytes 393224 | tf_op jit(solution)/shard_map/ppermute | solution.py:231
  77.4 2.4 %collective-permute-start.13 = (bf16[1,64,1024]{2,1,0:T(8,128)(2,1)S(1)}, bf16[1,64,1024]{2,1,0:T(8,128)(2,1)S(1)}, u32[]{:S(2)}, u32[]{:S(2)}) collective-permute-start(bf16[1,64,1024]{2,1,0:T(8,128)(2,1)S(1)} %product.1.refs_0_), channel_id=1, source_target_pairs={{0,16},{4,20},{8,24},{12,28},{16,0},{20,4},{24,8},{28,12},{32,48},... | collective-permute-start | bytes 393224 | tf_op jit(solution)/shard_map/ppermute | solution.py:231
  79.9 0.3 collective-permute-start.14
  80.1 0.6 all-to-all-done.3.gathered_ref
  80.8 1.3 %update2.1 = bf16[16,32,128]{2,1,0:T(8,128)(2,1)} custom-call(s32[3,32]{1,0:T(4,128)S(1)} %reshape.100.index_ref, bf16[32,16,128]{2,1,0:T(8,128)(2,1)S(1)} %all-to-all-done.3.gathered_ref, f32[4,32,64]{2,1,0:T(8,128)S(1)} %bitcast.8, bf16[4,64,1024]{2,1,0:T(8,128)(2,1)S(1)} %pad_maximum_fusion.near_ref, ...), custom_call_target="tpu_custom_call" | custom-call | flops 20000000 | bytes 1000000 | tf_op jit(solution)/shard_map/update2/pallas_call | solution.py:187
  82.0 5.5 %all-to-all-start.4 = ((bf16[16,32,128]{2,1,0:T(8,128)(2,1)}), bf16[16,32,128]{2,1,0:T(8,128)(2,1)S(1)}, u32[]{:S(2)}, u32[]{:S(2)}) async-start(bf16[16,32,128]{2,1,0:T(8,128)(2,1)} %update2.1), calls=%async_computation.4 | async-start | bytes 262144 | tf_op jit(solution)/shard_map/all_to_all | solution.py:225
  87.5 0.2 collective-permute-start.15
  87.7 0.0 collective-permute-done.12.refs_1_
  87.7 0.3 collective-permute-start.16
  88.0 0.0 collective-permute-done.13.refs_2_
  88.0 0.2 collective-permute-start.17
  88.2 0.5 collective-permute-done.14.refs_3_
  88.7 0.9 collective-permute-start.18
  89.6 0.0 collective-permute-done.15.refs_4_
  89.6 0.0 collective-permute-done.16.refs_5_
  89.6 0.0 collective-permute-done.17.refs_6_
  89.6 1.0 %collective-permute-done.18.refs_7_ = bf16[1,64,1024]{2,1,0:T(8,128)(2,1)S(1)} collective-permute-done((bf16[1,64,1024]{2,1,0:T(8,128)(2,1)S(1)}, bf16[1,64,1024]{2,1,0:T(8,128)(2,1)S(1)}, u32[]{:S(2)}, u32[]{:S(2)}) %collective-permute-start.18) | collective-permute-done | bytes 131104 | tf_op jit(solution)/shard_map/ppermute | solution.py:231
  90.6 3.1 %all-to-all-done.4.gathered_ref = bf16[16,32,128]{2,1,0:T(8,128)(2,1)S(1)} async-done(((bf16[16,32,128]{2,1,0:T(8,128)(2,1)}), bf16[16,32,128]{2,1,0:T(8,128)(2,1)S(1)}, u32[]{:S(2)}, u32[]{:S(2)}) %all-to-all-start.4) | async-done | bytes 131104 | tf_op jit(solution)/shard_map/all_to_all | solution.py:225
  93.7 1.4 %final.1 = f32[4,32,64]{2,1,0:T(8,128)} custom-call(bf16[16,32,128]{2,1,0:T(8,128)(2,1)S(1)} %all-to-all-done.4.gathered_ref, bf16[64,1024]{1,0:T(8,128)(2,1)S(1)} %copy-done.3, bf16[64,512]{1,0:T(8,128)(2,1)S(1)} %copy-done.5, f32[32,64]{1,0:T(8,128)S(1)} %get-tuple-element.41.first_result_ref, f32[32,64]{1,0:T(8,128)S(1)} %get-tuple-element.42.second_result_ref, ...), custom_call_target="tpu_custom_call" | custom-call | flops 20000000 | bytes 1000000 | tf_op jit(solution)/shard_map/final/pallas_call | solution.py:187
  (32 shorter events, 0.3 us)
Async XLA Ops:
  0.0 0.8 copy-start
  0.0 1.4 %copy-start.1 = (f32[4,64,32]{1,2,0:T(8,128)S(1)}, f32[4,64,32]{1,2,0:T(8,128)}, u32[]{:S(2)}) copy-start(f32[4,64,32]{1,2,0:T(8,128)} %param.7) | copy-start | bytes 98308
  0.0 28.6 %copy-start.2 = (bf16[64,4096]{1,0:T(8,128)(2,1)S(1)}, bf16[64,4096]{1,0:T(8,128)(2,1)}, u32[]{:S(2)}) copy-start(bf16[64,4096]{1,0:T(8,128)(2,1)} %inverse_ref.2) | copy-start | bytes 1572868
  2.2 14.6 %copy-start.3 = (bf16[64,1024]{1,0:T(8,128)(2,1)S(1)}, bf16[64,1024]{1,0:T(8,128)(2,1)}, u32[]{:S(2)}) copy-start(bf16[64,1024]{1,0:T(8,128)(2,1)} %third_ref.1) | copy-start | bytes 393220
  2.2 26.5 %all-to-all-start = ((bf16[64,16,128]{2,1,0:T(8,128)(2,1)}), bf16[64,16,128]{2,1,0:T(8,128)(2,1)S(1)}, u32[]{:S(2)}, u32[]{:S(2)}) async-start(bf16[64,16,128]{2,1,0:T(8,128)(2,1)} %start.1), calls=%async_computation | async-start | bytes 524288 | tf_op jit(solution)/shard_map/all_to_all | solution.py:225
  15.5 14.3 %collective-permute-start.2 = (bf16[3,64,1024]{2,1,0:T(8,128)(2,1)}, bf16[3,64,1024]{2,1,0:T(8,128)(2,1)S(1)}, u32[]{:S(2)}, u32[]{:S(2)}) collective-permute-start(bf16[3,64,1024]{2,1,0:T(8,128)(2,1)} %param.8), channel_id=1, source_target_pairs={{0,1},{1,0},{2,3},{3,2},{4,5},{5,4},{6,7},{7,6},{8,9},{9,8},{10,11... | collective-permute-start | bytes 1179656 | tf_op jit(solution)/shard_map/ppermute | solution.py:228
  16.8 13.0 %collective-permute-start = (bf16[1,64,1024]{2,1,0:T(8,128)(2,1)S(1)}, bf16[1,64,1024]{2,1,0:T(8,128)(2,1)S(1)}, u32[]{:S(2)}, u32[]{:S(2)}) collective-permute-start(bf16[1,64,1024]{2,1,0:T(8,128)(2,1)S(1)} %bitcast.9), channel_id=1, source_target_pairs={{0,16},{4,20},{8,24},{12,28},{16,0},{20,4},{24,8},{28,12},{32,48},... | collective-permute-start | bytes 393224 | tf_op jit(solution)/shard_map/ppermute | solution.py:231
  19.7 10.1 %collective-permute-start.1 = (bf16[1,64,1024]{2,1,0:T(8,128)(2,1)S(1)}, bf16[1,64,1024]{2,1,0:T(8,128)(2,1)S(1)}, u32[]{:S(2)}, u32[]{:S(2)}) collective-permute-start(bf16[1,64,1024]{2,1,0:T(8,128)(2,1)S(1)} %bitcast.10), channel_id=1, source_target_pairs={{0,32},{4,36},{8,40},{12,44},{16,48},{20,52},{24,56},{28,60},{32,0... | collective-permute-start | bytes 393224 | tf_op jit(solution)/shard_map/ppermute | solution.py:231
  29.8 9.0 %copy-start.9 = (bf16[3,64,1024]{2,1,0:T(8,128)(2,1)}, bf16[3,64,1024]{2,1,0:T(8,128)(2,1)S(1)}, u32[]{:S(2)}) copy-start(bf16[3,64,1024]{2,1,0:T(8,128)(2,1)S(1)} %collective-permute-done.2) | copy-start | bytes 1179652
  29.8 20.6 %all-to-all-start.1 = ((bf16[64,16,128]{2,1,0:T(8,128)(2,1)}), bf16[64,16,128]{2,1,0:T(8,128)(2,1)S(1)}, u32[]{:S(2)}, u32[]{:S(2)}) async-start(bf16[64,16,128]{2,1,0:T(8,128)(2,1)} %get-tuple-element.30), calls=%async_computation.1 | async-start | bytes 524288 | tf_op jit(solution)/shard_map/all_to_all | solution.py:225
  37.2 1.6 %copy-start.8 = (bf16[3,64,1024]{2,1,0:T(8,128)(2,1)S(1)}, bf16[3,64,1024]{2,1,0:T(8,128)(2,1)}, u32[]{:S(2)}) copy-start(bf16[3,64,1024]{2,1,0:T(8,128)(2,1)} %param.8) | copy-start | bytes 1179652
  37.3 6.7 %copy-start.6 = (bf16[3,64,1024]{2,1,0:T(8,128)(2,1)}, bf16[3,64,1024]{2,1,0:T(8,128)(2,1)S(1)}, u32[]{:S(2)}) copy-start(bf16[3,64,1024]{2,1,0:T(8,128)(2,1)S(1)} %pad_maximum_fusion.1.refs_0_) | copy-start | bytes 1179652
  37.3 14.3 %collective-permute-start.4 = (bf16[3,64,1024]{2,1,0:T(8,128)(2,1)S(1)}, bf16[3,64,1024]{2,1,0:T(8,128)(2,1)S(1)}, u32[]{:S(2)}, u32[]{:S(2)}) collective-permute-start(bf16[3,64,1024]{2,1,0:T(8,128)(2,1)S(1)} %pad_maximum_fusion.1.refs_0_), channel_id=1, source_target_pairs={{0,8},{4,12},{8,0},{12,4},{16,24},{20,28},{24,16},{28,20},{32,40},... | collective-permute-start | bytes 1179656 | tf_op jit(solution)/shard_map/ppermute | solution.py:231
  38.9 2.9 %copy-start.10 = (bf16[3,64,1024]{2,1,0:T(8,128)(2,1)S(1)}, bf16[3,64,1024]{2,1,0:T(8,128)(2,1)}, u32[]{:S(2)}) copy-start(bf16[3,64,1024]{2,1,0:T(8,128)(2,1)} %copy-done.9) | copy-start | bytes 1179652
  38.9 8.8 %collective-permute-start.3 = (bf16[2,64,1024]{2,1,0:T(8,128)(2,1)S(1)}, bf16[2,64,1024]{2,1,0:T(8,128)(2,1)S(1)}, u32[]{:S(2)}, u32[]{:S(2)}) collective-permute-start(bf16[2,64,1024]{2,1,0:T(8,128)(2,1)S(1)} %pad_maximum_fusion.2.near_ref), channel_id=1, source_target_pairs={{0,2},{1,3},{2,0},{3,1},{4,6},{5,7},{6,4},{7,5},{8,10},{9,11},{10,... | collective-permute-start | bytes 786440 | tf_op jit(solution)/shard_map/ppermute | solution.py:228
  41.8 18.3 %collective-permute-start.6 = (bf16[4,64,1024]{2,1,0:T(8,128)(2,1)S(1)}, bf16[4,64,1024]{2,1,0:T(8,128)(2,1)S(1)}, u32[]{:S(2)}, u32[]{:S(2)}) collective-permute-start(bf16[4,64,1024]{2,1,0:T(8,128)(2,1)S(1)} %pad_maximum_fusion.near_ref), channel_id=1, source_target_pairs={{0,2},{1,3},{2,0},{3,1},{4,6},{5,7},{6,4},{7,5},{8,10},{9,11},{10,... | collective-permute-start | bytes 1572872 | tf_op jit(solution)/shard_map/ppermute | solution.py:228
  42.8 8.8 %collective-permute-start.5 = (bf16[1,64,1024]{2,1,0:T(8,128)(2,1)S(1)}, bf16[1,64,1024]{2,1,0:T(8,128)(2,1)S(1)}, u32[]{:S(2)}, u32[]{:S(2)}) collective-permute-start(bf16[1,64,1024]{2,1,0:T(8,128)(2,1)S(1)} %collective-permute-done), channel_id=1, source_target_pairs={{0,32},{4,36},{8,40},{12,44},{16,48},{20,52},{24,56},{28,60},{32,0... | collective-permute-start | bytes 393224 | tf_op jit(solution)/shard_map/ppermute | solution.py:231
  44.0 24.2 %collective-permute-start.7 = (bf16[3,64,1024]{2,1,0:T(8,128)(2,1)S(1)}, bf16[3,64,1024]{2,1,0:T(8,128)(2,1)}, u32[]{:S(2)}, u32[]{:S(2)}) collective-permute-start(bf16[3,64,1024]{2,1,0:T(8,128)(2,1)S(1)} %pad_maximum_fusion.1.refs_0_), channel_id=1, source_target_pairs={{0,4},{4,0},{8,12},{12,8},{16,20},{20,16},{24,28},{28,24},{32,36},... | collective-permute-start | bytes 1179656 | tf_op jit(solution)/shard_map/ppermute | solution.py:231
  51.6 9.5 %copy-start.7 = (bf16[3,64,1024]{2,1,0:T(8,128)(2,1)}, bf16[3,64,1024]{2,1,0:T(8,128)(2,1)S(1)}, u32[]{:S(2)}) copy-start(bf16[3,64,1024]{2,1,0:T(8,128)(2,1)S(1)} %collective-permute-done.4.refs_1_) | copy-start | bytes 1179652
  51.6 16.6 %collective-permute-start.8 = (bf16[3,64,1024]{2,1,0:T(8,128)(2,1)S(1)}, bf16[3,64,1024]{2,1,0:T(8,128)(2,1)}, u32[]{:S(2)}, u32[]{:S(2)}) collective-permute-start(bf16[3,64,1024]{2,1,0:T(8,128)(2,1)S(1)} %collective-permute-done.4.refs_1_), channel_id=1, source_target_pairs={{0,4},{4,0},{8,12},{12,8},{16,20},{20,16},{24,28},{28,24},{32,36},... | collective-permute-start | bytes 1179656 | tf_op jit(solution)/shard_map/ppermute | solution.py:231
  52.0 15.2 %all-to-all-start.2 = ((bf16[32,16,128]{2,1,0:T(8,128)(2,1)}), bf16[32,16,128]{2,1,0:T(8,128)(2,1)S(1)}, u32[]{:S(2)}, u32[]{:S(2)}) async-start(bf16[32,16,128]{2,1,0:T(8,128)(2,1)} %get-tuple-element.35), calls=%async_computation.2 | async-start | bytes 262144 | tf_op jit(solution)/shard_map/all_to_all | solution.py:225
  58.6 8.6 %copy-start.4 = (bf16[64,2048]{1,0:T(8,128)(2,1)S(1)}, bf16[64,2048]{1,0:T(8,128)(2,1)}, u32[]{:S(2)}) copy-start(bf16[64,2048]{1,0:T(8,128)(2,1)} %inverse_ref.3) | copy-start | bytes 786436
  58.6 13.9 %collective-permute-start.9 = (bf16[1,64,1024]{2,1,0:T(8,128)(2,1)S(1)}, bf16[1,64,1024]{2,1,0:T(8,128)(2,1)S(1)}, u32[]{:S(2)}, u32[]{:S(2)}) collective-permute-start(bf16[1,64,1024]{2,1,0:T(8,128)(2,1)S(1)} %collective-permute-done.5.refs_4_), channel_id=1, source_target_pairs={{0,8},{4,12},{8,0},{12,4},{16,24},{20,28},{24,16},{28,20},{32,40},... | collective-permute-start | bytes 393224 | tf_op jit(solution)/shard_map/ppermute | solution.py:231
  68.2 12.6 %all-to-all-start.3 = ((bf16[32,16,128]{2,1,0:T(8,128)(2,1)}), bf16[32,16,128]{2,1,0:T(8,128)(2,1)S(1)}, u32[]{:S(2)}, u32[]{:S(2)}) async-start(bf16[32,16,128]{2,1,0:T(8,128)(2,1)} %get-tuple-element.39), calls=%async_computation.3 | async-start | bytes 262144 | tf_op jit(solution)/shard_map/all_to_all | solution.py:225
  72.1 1.4 %collective-permute-start.10 = (bf16[1,64,1024]{2,1,0:T(8,128)(2,1)S(1)}, bf16[1,64,1024]{2,1,0:T(8,128)(2,1)S(1)}, u32[]{:S(2)}, u32[]{:S(2)}) collective-permute-start(bf16[1,64,1024]{2,1,0:T(8,128)(2,1)S(1)} %collective-permute-done.5.refs_4_), channel_id=1, source_target_pairs={{0,4},{4,0},{8,12},{12,8},{16,20},{20,16},{24,28},{28,24},{32,36},... | collective-permute-start | bytes 393224 | tf_op jit(solution)/shard_map/ppermute | solution.py:231
  72.5 1.3 %collective-permute-start.11 = (bf16[1,64,1024]{2,1,0:T(8,128)(2,1)S(1)}, bf16[1,64,1024]{2,1,0:T(8,128)(2,1)S(1)}, u32[]{:S(2)}, u32[]{:S(2)}) collective-permute-start(bf16[1,64,1024]{2,1,0:T(8,128)(2,1)S(1)} %collective-permute-done.9.refs_5_), channel_id=1, source_target_pairs={{0,4},{4,0},{8,12},{12,8},{16,20},{20,16},{24,28},{28,24},{32,36},... | collective-permute-start | bytes 393224 | tf_op jit(solution)/shard_map/ppermute | solution.py:231
  76.0 11.7 %collective-permute-start.12 = (bf16[1,64,1024]{2,1,0:T(8,128)(2,1)S(1)}, bf16[1,64,1024]{2,1,0:T(8,128)(2,1)S(1)}, u32[]{:S(2)}, u32[]{:S(2)}) collective-permute-start(bf16[1,64,1024]{2,1,0:T(8,128)(2,1)S(1)} %product.1.refs_0_), channel_id=1, source_target_pairs={{0,8},{4,12},{8,0},{12,4},{16,24},{20,28},{24,16},{28,20},{32,40},... | collective-permute-start | bytes 393224 | tf_op jit(solution)/shard_map/ppermute | solution.py:231
  77.4 10.6 %collective-permute-start.13 = (bf16[1,64,1024]{2,1,0:T(8,128)(2,1)S(1)}, bf16[1,64,1024]{2,1,0:T(8,128)(2,1)S(1)}, u32[]{:S(2)}, u32[]{:S(2)}) collective-permute-start(bf16[1,64,1024]{2,1,0:T(8,128)(2,1)S(1)} %product.1.refs_0_), channel_id=1, source_target_pairs={{0,16},{4,20},{8,24},{12,28},{16,0},{20,4},{24,8},{28,12},{32,48},... | collective-permute-start | bytes 393224 | tf_op jit(solution)/shard_map/ppermute | solution.py:231
  79.9 8.8 %collective-permute-start.14 = (bf16[1,64,1024]{2,1,0:T(8,128)(2,1)S(1)}, bf16[1,64,1024]{2,1,0:T(8,128)(2,1)S(1)}, u32[]{:S(2)}, u32[]{:S(2)}) collective-permute-start(bf16[1,64,1024]{2,1,0:T(8,128)(2,1)S(1)} %product.1.refs_0_), channel_id=1, source_target_pairs={{0,24},{4,28},{8,16},{12,20},{16,8},{20,12},{24,0},{28,4},{32,56},... | collective-permute-start | bytes 393224 | tf_op jit(solution)/shard_map/ppermute | solution.py:231
  82.0 11.6 %copy-start.5 = (bf16[64,512]{1,0:T(8,128)(2,1)S(1)}, bf16[64,512]{1,0:T(8,128)(2,1)}, u32[]{:S(2)}) copy-start(bf16[64,512]{1,0:T(8,128)(2,1)} %fourth_ref.1) | copy-start | bytes 196612
  82.0 11.6 %all-to-all-start.4 = ((bf16[16,32,128]{2,1,0:T(8,128)(2,1)}), bf16[16,32,128]{2,1,0:T(8,128)(2,1)S(1)}, u32[]{:S(2)}, u32[]{:S(2)}) async-start(bf16[16,32,128]{2,1,0:T(8,128)(2,1)} %update2.1), calls=%async_computation.4 | async-start | bytes 262144 | tf_op jit(solution)/shard_map/all_to_all | solution.py:225
  87.5 2.1 %collective-permute-start.15 = (bf16[1,64,1024]{2,1,0:T(8,128)(2,1)S(1)}, bf16[1,64,1024]{2,1,0:T(8,128)(2,1)S(1)}, u32[]{:S(2)}, u32[]{:S(2)}) collective-permute-start(bf16[1,64,1024]{2,1,0:T(8,128)(2,1)S(1)} %product.1.refs_0_), channel_id=1, source_target_pairs={{0,4},{4,0},{8,12},{12,8},{16,20},{20,16},{24,28},{28,24},{32,36},... | collective-permute-start | bytes 393224 | tf_op jit(solution)/shard_map/ppermute | solution.py:231
  87.7 1.9 %collective-permute-start.16 = (bf16[1,64,1024]{2,1,0:T(8,128)(2,1)S(1)}, bf16[1,64,1024]{2,1,0:T(8,128)(2,1)S(1)}, u32[]{:S(2)}, u32[]{:S(2)}) collective-permute-start(bf16[1,64,1024]{2,1,0:T(8,128)(2,1)S(1)} %collective-permute-done.12.refs_1_), channel_id=1, source_target_pairs={{0,4},{4,0},{8,12},{12,8},{16,20},{20,16},{24,28},{28,24},{32,36},... | collective-permute-start | bytes 393224 | tf_op jit(solution)/shard_map/ppermute | solution.py:231
  88.0 1.6 %collective-permute-start.17 = (bf16[1,64,1024]{2,1,0:T(8,128)(2,1)S(1)}, bf16[1,64,1024]{2,1,0:T(8,128)(2,1)S(1)}, u32[]{:S(2)}, u32[]{:S(2)}) collective-permute-start(bf16[1,64,1024]{2,1,0:T(8,128)(2,1)S(1)} %collective-permute-done.13.refs_2_), channel_id=1, source_target_pairs={{0,4},{4,0},{8,12},{12,8},{16,20},{20,16},{24,28},{28,24},{32,36},... | collective-permute-start | bytes 393224 | tf_op jit(solution)/shard_map/ppermute | solution.py:231
  88.7 1.9 %collective-permute-start.18 = (bf16[1,64,1024]{2,1,0:T(8,128)(2,1)S(1)}, bf16[1,64,1024]{2,1,0:T(8,128)(2,1)S(1)}, u32[]{:S(2)}, u32[]{:S(2)}) collective-permute-start(bf16[1,64,1024]{2,1,0:T(8,128)(2,1)S(1)} %collective-permute-done.14.refs_3_), channel_id=1, source_target_pairs={{0,4},{4,0},{8,12},{12,8},{16,20},{20,16},{24,28},{28,24},{32,36},... | collective-permute-start | bytes 393224 | tf_op jit(solution)/shard_map/ppermute | solution.py:231

commit v6 on v5

--- a/solution.py
+++ b/solution.py
@@ -77,23 +77,21 @@
     return own % 2, own // 2 % 4, own // 8 % 2
 
 
-def product_kernel(coupled_ref, *refs):
-    third, out_ref = refs[:-1], refs[-1]
+def product_kernel(corner, coupled_ref, *refs):
+    third, out_ref = refs[:4], refs[-1]
     core, y, z = position()
-    total = None
-    for n, ref in enumerate(third):
-        g = n % 4
+    total = refs[4][0] if corner else None
+    for g, ref in enumerate(third):
         picked = []
-        for e in range(ref.shape[0]) if n < 4 else (3,):
+        for e in (3,) if corner else range(ref.shape[0]):
             block = (z ^ (e // 2)) * 4 + (y ^ (e % 2 * 2 + g % 2))
             columns = coupled_ref[0, :, pl.ds(pl.multiple_of(block * BS, BS), BS)]
             half = columns.shape[1] // 2
             first = core == g // 2
             picked.append(jnp.where(first, columns[:, :half], columns[:, half:]))
         rows = ref[...].reshape(ref.shape[0] * ref.shape[1], ref.shape[2])
-        term = jnp.dot(
-            jnp.concatenate(picked, axis=1), rows, preferred_element_type=jnp.float32
-        )
+        picked = picked[0] if corner else jnp.concatenate(picked, axis=1)
+        term = jnp.dot(picked, rows, preferred_element_type=jnp.float32)
         total = term if total is None else total + term
     out_ref[0] = total.astype(out_ref.dtype)
 
@@ -299,7 +297,16 @@
         select_kernel, "select", [shape((1, rows, count * BS), bf16)], [], positions, rest_below, rest_far
     )
 
-    gathered = gather(copies)
+    (partial,) = call(
+        functools.partial(product_kernel, False),
+        "product",
+        [shape(coupled.shape, f32)],
+        [],
+        coupled,
+        *held(*third),
+    )
+    gathered = gather(copies)
+    gathered, coupled, partial = barrier((gathered, coupled, partial))
     second_result, copies = call(
         solve_kernel,
         "solve1",
@@ -309,10 +316,14 @@
         inverse_second,
     )
 
-    copies, coupled, third = barrier((copies, coupled, third))
-    third = third + corner
     (coupled,) = call(
-        product_kernel, "product", [shape(coupled.shape, bf16)], [], coupled, *held(*third[:4]), *third[4:]
+        functools.partial(product_kernel, True),
+        "corner",
+        [shape(coupled.shape, bf16)],
+        [],
+        coupled,
+        *corner,
+        partial,
     )
     coupled = over_y(coupled)
 

time: 95.6 us -> 95.2 us (level)
  waiting for transfers between devices: 25.5 us -> 23.6 us
    all_to_all x5, waiting for transfers between devices: 20.3 us -> 18 us  [gather(): return lax.all_to_all(copies, 'sn', 0, 0, axis_index_groups=sets)]
    ppermute x16, starting transfers between devices: 16.1 us -> 17.1 us  [swap(): return lax.ppermute(part, 'sn', [(i, i ^ bit) for i in range(devices)])]
    pallas_call x8 -> x9, Pallas kernels: 9.82 us -> 10 us  [call(): pl.pallas_call(kernel, out_shape=outs, in_specs=[VMEM] * len(args), out_s...]
  transfers between devices with their start and end apart: 24 -> 24, of which waited for: 10 -> 10; matrix products, arithmetic and copies ran while one was open for 0% -> 1% of each run, Pallas kernels for 8% -> 8%
where the time goes in v6:
time: 95.2 us; the launch traced here: 94.6 us
  starting transfers between devices  57.5 us (60%)
  waiting for transfers between devices  23.6 us (25%)
  Pallas kernels  10 us (11%)
  local copies, waits for them, and re-layouts  1.75 us (2%)
  other arithmetic  1.46 us (2%)
    all_to_all x5, starting transfers between devices, gather(): return lax.all_to_all(copies, 'sn', 0, 0, axis_index_groups=sets)  36 us
    all_to_all x5, waiting for transfers between devices, gather(): return lax.all_to_all(copies, 'sn', 0, 0, axis_index_groups=sets)  18 us
    ppermute x16, starting transfers between devices, swap(): return lax.ppermute(part, 'sn', [(i, i ^ bit) for i in range(devices)])  17.1 us
    pallas_call x9, Pallas kernels, call(): pl.pallas_call(kernel, out_shape=outs, in_specs=[VMEM] * len(args), out_s...  10 us
    ppermute x3, starting transfers between devices, swap_group(): return lax.ppermute(part, 'rhs', [(i, i ^ bit) for i in range(groups)])  4.44 us
    ppermute x3, waiting for transfers between devices, swap_group(): return lax.ppermute(part, 'rhs', [(i, i ^ bit) for i in range(groups)])  2.89 us
    ppermute x16, waiting for transfers between devices, swap(): return lax.ppermute(part, 'sn', [(i, i ^ bit) for i in range(devices)])  2.71 us
  transfers between devices with their start and end apart: 24, of which 10 were waited for; matrix products, arithmetic and copies ran while one was open for 1% of the time, Pallas kernels for 8%

profile of v6, /device:TPU:1, one launch (start us, length us, event | category | flops | bytes accessed | tf_op | source)
XLA Modules:
  0.0 94.6 jit_solution(8166097710878560864)
XLA Ops:
  0.1 0.7 copy-done
  0.9 0.1 squeeze.4
  0.9 0.1 iota_compare_fusion
  1.0 0.1 select_reduce_fusion
  1.1 0.1 reshape.100.index_ref
  1.2 0.2 select_reduce_fusion.1
  1.4 0.8 start.1
  2.2 13.3 %all-to-all-start = ((bf16[64,16,128]{2,1,0:T(8,128)(2,1)}), bf16[64,16,128]{2,1,0:T(8,128)(2,1)S(1)}, u32[]{:S(2)}, u32[]{:S(2)}) async-start(bf16[64,16,128]{2,1,0:T(8,128)(2,1)} %start.1), calls=%async_computation | async-start | bytes 524288 | tf_op jit(solution)/shard_map/all_to_all | solution.py:223
  15.5 1.3 %collective-permute-start.2 = (bf16[3,64,1024]{2,1,0:T(8,128)(2,1)}, bf16[3,64,1024]{2,1,0:T(8,128)(2,1)S(1)}, u32[]{:S(2)}, u32[]{:S(2)}) collective-permute-start(bf16[3,64,1024]{2,1,0:T(8,128)(2,1)} %param.8), channel_id=1, source_target_pairs={{0,1},{1,0},{2,3},{3,2},{4,5},{5,4},{6,7},{7,6},{8,9},{9,8},{10,11... | collective-permute-start | bytes 1179656 | tf_op jit(solution)/shard_map/ppermute | solution.py:226
  16.8 2.9 %collective-permute-start = (bf16[1,64,1024]{2,1,0:T(8,128)(2,1)S(1)}, bf16[1,64,1024]{2,1,0:T(8,128)(2,1)}, u32[]{:S(2)}, u32[]{:S(2)}) collective-permute-start(bf16[1,64,1024]{2,1,0:T(8,128)(2,1)S(1)} %bitcast.9), channel_id=1, source_target_pairs={{0,16},{4,20},{8,24},{12,28},{16,0},{20,4},{24,8},{28,12},{32,48},... | collective-permute-start | bytes 393224 | tf_op jit(solution)/shard_map/ppermute | solution.py:229
  19.7 1.2 %collective-permute-start.1 = (bf16[1,64,1024]{2,1,0:T(8,128)(2,1)S(1)}, bf16[1,64,1024]{2,1,0:T(8,128)(2,1)S(1)}, u32[]{:S(2)}, u32[]{:S(2)}) collective-permute-start(bf16[1,64,1024]{2,1,0:T(8,128)(2,1)S(1)} %bitcast.10), channel_id=1, source_target_pairs={{0,32},{4,36},{8,40},{12,44},{16,48},{20,52},{24,56},{28,60},{32,0... | collective-permute-start | bytes 393224 | tf_op jit(solution)/shard_map/ppermute | solution.py:229
  20.9 7.8 %all-to-all-done.gathered_ref = bf16[64,16,128]{2,1,0:T(8,128)(2,1)S(1)} async-done(((bf16[64,16,128]{2,1,0:T(8,128)(2,1)}), bf16[64,16,128]{2,1,0:T(8,128)(2,1)S(1)}, u32[]{:S(2)}, u32[]{:S(2)}) %all-to-all-start) | async-done | bytes 262176 | tf_op jit(solution)/shard_map/all_to_all | solution.py:223
  28.7 1.2 %solve0.1 = (f32[32,64]{1,0:T(8,128)S(1)}, bf16[64,16,128]{2,1,0:T(8,128)(2,1)}) custom-call(bf16[64,16,128]{2,1,0:T(8,128)(2,1)S(1)} %all-to-all-done.gathered_ref, bf16[64,4096]{1,0:T(8,128)(2,1)S(1)} %copy-done.2), custom_call_target="tpu_custom_call" | custom-call | flops 20000000 | bytes 1000000 | tf_op jit(solution)/shard_map/solve0/pallas_call | solution.py:185
  29.8 0.0 collective-permute-done
  29.8 0.0 collective-permute-done.1
  29.8 0.0 collective-permute-done.2
  29.8 7.4 %all-to-all-start.1 = ((bf16[64,16,128]{2,1,0:T(8,128)(2,1)}), bf16[64,16,128]{2,1,0:T(8,128)(2,1)S(1)}, u32[]{:S(2)}, u32[]{:S(2)}) async-start(bf16[64,16,128]{2,1,0:T(8,128)(2,1)} %get-tuple-element.27), calls=%async_computation.1 | async-start | bytes 524288 | tf_op jit(solution)/shard_map/all_to_all | solution.py:223
  37.3 0.0 copy-start.7
  37.3 1.0 %pad_maximum_fusion.1.refs_0_ = bf16[3,64,1024]{2,1,0:T(8,128)(2,1)S(1)} fusion(bf16[1,64,1024]{2,1,0:T(8,128)(2,1)S(1)} %collective-permute-done.1, bf16[1,64,1024]{2,1,0:T(8,128)(2,1)} %collective-permute-done, bf16[1,64,1024]{2,1,0:T(8,128)(2,1)S(1)} %bitcast.11), kind=kLoop, calls=%fused_computation.1 | loop fusion | flops 393216 | bytes 786432 | tf_op jit(solution)/shard_map/concatenate | solution.py:274
  38.3 1.5 %collective-permute-start.4 = (bf16[3,64,1024]{2,1,0:T(8,128)(2,1)S(1)}, bf16[3,64,1024]{2,1,0:T(8,128)(2,1)}, u32[]{:S(2)}, u32[]{:S(2)}) collective-permute-start(bf16[3,64,1024]{2,1,0:T(8,128)(2,1)S(1)} %pad_maximum_fusion.1.refs_0_), channel_id=1, source_target_pairs={{0,8},{4,12},{8,0},{12,4},{16,24},{20,28},{24,16},{28,20},{32,40},... | collective-permute-start | bytes 1179656 | tf_op jit(solution)/shard_map/ppermute | solution.py:229
  39.8 2.8 %collective-permute-start.3 = (bf16[2,64,1024]{2,1,0:T(8,128)(2,1)S(1)}, bf16[2,64,1024]{2,1,0:T(8,128)(2,1)S(1)}, u32[]{:S(2)}, u32[]{:S(2)}) collective-permute-start(bf16[2,64,1024]{2,1,0:T(8,128)(2,1)S(1)} %pad_maximum_fusion.2.near_ref), channel_id=1, source_target_pairs={{0,2},{1,3},{2,0},{3,1},{4,6},{5,7},{6,4},{7,5},{8,10},{9,11},{10,... | collective-permute-start | bytes 786440 | tf_op jit(solution)/shard_map/ppermute | solution.py:226
  42.8 0.3 collective-permute-start.6
  43.1 1.2 %collective-permute-start.5 = (bf16[1,64,1024]{2,1,0:T(8,128)(2,1)}, bf16[1,64,1024]{2,1,0:T(8,128)(2,1)S(1)}, u32[]{:S(2)}, u32[]{:S(2)}) collective-permute-start(bf16[1,64,1024]{2,1,0:T(8,128)(2,1)} %collective-permute-done), channel_id=1, source_target_pairs={{0,32},{4,36},{8,40},{12,44},{16,48},{20,52},{24,56},{28,60},{32,0... | collective-permute-start | bytes 393224 | tf_op jit(solution)/shard_map/ppermute | solution.py:229
  44.3 1.5 %collective-permute-start.7 = (bf16[3,64,1024]{2,1,0:T(8,128)(2,1)S(1)}, bf16[3,64,1024]{2,1,0:T(8,128)(2,1)S(1)}, u32[]{:S(2)}, u32[]{:S(2)}) collective-permute-start(bf16[3,64,1024]{2,1,0:T(8,128)(2,1)S(1)} %pad_maximum_fusion.1.refs_0_), channel_id=1, source_target_pairs={{0,4},{4,0},{8,12},{12,8},{16,20},{20,16},{24,28},{28,24},{32,36},... | collective-permute-start | bytes 1179656 | tf_op jit(solution)/shard_map/ppermute | solution.py:229
  45.8 2.9 %collective-permute-done.3.far_ref = bf16[2,64,1024]{2,1,0:T(8,128)(2,1)S(1)} collective-permute-done((bf16[2,64,1024]{2,1,0:T(8,128)(2,1)S(1)}, bf16[2,64,1024]{2,1,0:T(8,128)(2,1)S(1)}, u32[]{:S(2)}, u32[]{:S(2)}) %collective-permute-start.3) | collective-permute-done | bytes 262176 | tf_op jit(solution)/shard_map/ppermute | solution.py:226
  48.6 1.8 %all-to-all-done.1.gathered_ref = bf16[64,16,128]{2,1,0:T(8,128)(2,1)S(1)} async-done(((bf16[64,16,128]{2,1,0:T(8,128)(2,1)}), bf16[64,16,128]{2,1,0:T(8,128)(2,1)S(1)}, u32[]{:S(2)}, u32[]{:S(2)}) %all-to-all-start.1) | async-done | bytes 262176 | tf_op jit(solution)/shard_map/all_to_all | solution.py:223
  50.4 1.2 %update1.1 = (bf16[32,16,128]{2,1,0:T(8,128)(2,1)}, bf16[32,32,128]{2,1,0:T(8,128)(2,1)S(1)}) custom-call(s32[3,32]{1,0:T(4,128)S(1)} %reshape.100.index_ref, bf16[64,16,128]{2,1,0:T(8,128)(2,1)S(1)} %all-to-all-done.1.gathered_ref, f32[4,32,64]{2,1,0:T(8,128)S(1)} %bitcast.7, bf16[2,64,1024]{2,1,0:T(8,128)(2,1)S(1)} %pad_maximum_fusion.2.near_ref, ...), custom_call_target="tpu_custom_call" | custom-call | flops 20000000 | bytes 1000000 | tf_op jit(solution)/shard_map/update1/pallas_call | solution.py:185
  51.6 0.0 collective-permute-done.5.refs_0_
  51.6 0.0 collective-permute-done.4.refs_1_
  51.6 0.8 collective-permute-start.8
  52.5 7.1 %all-to-all-start.2 = ((bf16[32,16,128]{2,1,0:T(8,128)(2,1)}), bf16[32,16,128]{2,1,0:T(8,128)(2,1)S(1)}, u32[]{:S(2)}, u32[]{:S(2)}) async-start(bf16[32,16,128]{2,1,0:T(8,128)(2,1)} %get-tuple-element.32), calls=%async_computation.2 | async-start | bytes 262144 | tf_op jit(solution)/shard_map/all_to_all | solution.py:223
  59.6 1.5 %collective-permute-start.9 = (bf16[1,64,1024]{2,1,0:T(8,128)(2,1)S(1)}, bf16[1,64,1024]{2,1,0:T(8,128)(2,1)S(1)}, u32[]{:S(2)}, u32[]{:S(2)}) collective-permute-start(bf16[1,64,1024]{2,1,0:T(8,128)(2,1)S(1)} %collective-permute-done.5.refs_0_), channel_id=1, source_target_pairs={{0,8},{4,12},{8,0},{12,4},{16,24},{20,28},{24,16},{28,20},{32,40},... | collective-permute-start | bytes 393224 | tf_op jit(solution)/shard_map/ppermute | solution.py:229
  61.1 0.0 collective-permute-done.6.far_ref
  61.1 1.0 %select.40.coupled_ref = bf16[1,64,1024]{2,1,0:T(8,128)(2,1)S(1)} custom-call(s32[1,8]{1,0:T(1,128)S(1)} %bitcast.12, bf16[4,64,1024]{2,1,0:T(8,128)(2,1)S(1)} %pad_maximum_fusion.near_ref, bf16[4,64,1024]{2,1,0:T(8,128)(2,1)S(1)} %collective-permute-done.6.far_ref), custom_call_target="tpu_custom_call" | custom-call | flops 20000000 | bytes 1000000 | tf_op jit(solution)/shard_map/select/pallas_call | solution.py:185
  62.1 0.0 copy-start.4
  62.1 0.0 collective-permute-done.7.refs_2_
  62.1 0.7 copy-done.8
  62.9 1.9 %product.1.refs_4_ = f32[1,64,1024]{2,1,0:T(8,128)S(1)} custom-call(bf16[1,64,1024]{2,1,0:T(8,128)(2,1)S(1)} %select.40.coupled_ref, bf16[3,64,1024]{2,1,0:T(8,128)(2,1)} %copy-done.6, bf16[3,64,1024]{2,1,0:T(8,128)(2,1)} %collective-permute-done.4.refs_1_, bf16[3,64,1024]{2,1,0:T(8,128)(2,1)} %copy-done.8, bf16[3,64,1024]{2,1,0:T(8,128)(2,1)} %collective-permute-done.8.refs_3_), custom_call_target="tpu_custom_call" | custom-call | flops 20000000 | bytes 1000000 | tf_op jit(solution)/shard_map/product/pallas_call | solution.py:185
  64.8 3.4 %all-to-all-done.2.gathered_ref = bf16[32,16,128]{2,1,0:T(8,128)(2,1)S(1)} async-done(((bf16[32,16,128]{2,1,0:T(8,128)(2,1)}), bf16[32,16,128]{2,1,0:T(8,128)(2,1)S(1)}, u32[]{:S(2)}, u32[]{:S(2)}) %all-to-all-start.2) | async-done | bytes 131104 | tf_op jit(solution)/shard_map/all_to_all | solution.py:223
  68.2 1.0 %solve1.1 = (f32[32,64]{1,0:T(8,128)S(1)}, bf16[32,16,128]{2,1,0:T(8,128)(2,1)}) custom-call(bf16[32,16,128]{2,1,0:T(8,128)(2,1)S(1)} %all-to-all-done.2.gathered_ref, bf16[64,2048]{1,0:T(8,128)(2,1)S(1)} %copy-done.4), custom_call_target="tpu_custom_call" | custom-call | flops 20000000 | bytes 1000000 | tf_op jit(solution)/shard_map/solve1/pallas_call | solution.py:185
  69.2 4.2 %all-to-all-start.3 = ((bf16[32,16,128]{2,1,0:T(8,128)(2,1)}), bf16[32,16,128]{2,1,0:T(8,128)(2,1)S(1)}, u32[]{:S(2)}, u32[]{:S(2)}) async-start(bf16[32,16,128]{2,1,0:T(8,128)(2,1)} %get-tuple-element.36), calls=%async_computation.3 | async-start | bytes 262144 | tf_op jit(solution)/shard_map/all_to_all | solution.py:223
  73.3 0.3 collective-permute-start.10
  73.7 0.3 collective-permute-start.11
  73.9 0.8 collective-permute-done.10.refs_2_
  74.8 0.2 collective-permute-done.11.refs_3_
  75.0 0.4 corner.1.refs_0_
  75.4 1.8 %collective-permute-start.12 = (bf16[1,64,1024]{2,1,0:T(8,128)(2,1)S(1)}, bf16[1,64,1024]{2,1,0:T(8,128)(2,1)S(1)}, u32[]{:S(2)}, u32[]{:S(2)}) collective-permute-start(bf16[1,64,1024]{2,1,0:T(8,128)(2,1)S(1)} %corner.1.refs_0_), channel_id=1, source_target_pairs={{0,8},{4,12},{8,0},{12,4},{16,24},{20,28},{24,16},{28,20},{32,40},... | collective-permute-start | bytes 393224 | tf_op jit(solution)/shard_map/ppermute | solution.py:229
  77.2 2.4 %collective-permute-start.13 = (bf16[1,64,1024]{2,1,0:T(8,128)(2,1)S(1)}, bf16[1,64,1024]{2,1,0:T(8,128)(2,1)S(1)}, u32[]{:S(2)}, u32[]{:S(2)}) collective-permute-start(bf16[1,64,1024]{2,1,0:T(8,128)(2,1)S(1)} %corner.1.refs_0_), channel_id=1, source_target_pairs={{0,16},{4,20},{8,24},{12,28},{16,0},{20,4},{24,8},{28,12},{32,48},... | collective-permute-start | bytes 393224 | tf_op jit(solution)/shard_map/ppermute | solution.py:229
  79.6 0.1 collective-permute-start.14
  79.6 2.2 %all-to-all-done.3.gathered_ref = bf16[32,16,128]{2,1,0:T(8,128)(2,1)S(1)} async-done(((bf16[32,16,128]{2,1,0:T(8,128)(2,1)}), bf16[32,16,128]{2,1,0:T(8,128)(2,1)S(1)}, u32[]{:S(2)}, u32[]{:S(2)}) %all-to-all-start.3) | async-done | bytes 131104 | tf_op jit(solution)/shard_map/all_to_all | solution.py:223
  81.9 1.3 %update2.1 = bf16[16,32,128]{2,1,0:T(8,128)(2,1)} custom-call(s32[3,32]{1,0:T(4,128)S(1)} %reshape.100.index_ref, bf16[32,16,128]{2,1,0:T(8,128)(2,1)S(1)} %all-to-all-done.3.gathered_ref, f32[4,32,64]{2,1,0:T(8,128)S(1)} %bitcast.8, bf16[4,64,1024]{2,1,0:T(8,128)(2,1)S(1)} %pad_maximum_fusion.near_ref, ...), custom_call_target="tpu_custom_call" | custom-call | flops 20000000 | bytes 1000000 | tf_op jit(solution)/shard_map/update2/pallas_call | solution.py:185
  83.2 4.0 %all-to-all-start.4 = ((bf16[16,32,128]{2,1,0:T(8,128)(2,1)}), bf16[16,32,128]{2,1,0:T(8,128)(2,1)S(1)}, u32[]{:S(2)}, u32[]{:S(2)}) async-start(bf16[16,32,128]{2,1,0:T(8,128)(2,1)} %update2.1), calls=%async_computation.4 | async-start | bytes 262144 | tf_op jit(solution)/shard_map/all_to_all | solution.py:223
  87.1 0.2 collective-permute-start.15
  87.3 0.0 collective-permute-done.12.refs_1_
  87.3 0.3 collective-permute-start.16
  87.7 0.0 collective-permute-done.13.refs_2_
  87.7 0.2 collective-permute-start.17
  87.8 0.6 collective-permute-done.14.refs_3_
  88.5 1.0 %collective-permute-start.18 = (bf16[1,64,1024]{2,1,0:T(8,128)(2,1)S(1)}, bf16[1,64,1024]{2,1,0:T(8,128)(2,1)S(1)}, u32[]{:S(2)}, u32[]{:S(2)}) collective-permute-start(bf16[1,64,1024]{2,1,0:T(8,128)(2,1)S(1)} %collective-permute-done.14.refs_3_), channel_id=1, source_target_pairs={{0,4},{4,0},{8,12},{12,8},{16,20},{20,16},{24,28},{28,24},{32,36},... | collective-permute-start | bytes 393224 | tf_op jit(solution)/shard_map/ppermute | solution.py:229
  89.5 0.0 collective-permute-done.15.refs_4_
  89.5 0.0 collective-permute-done.16.refs_5_
  89.5 1.0 %collective-permute-done.18.refs_7_ = bf16[1,64,1024]{2,1,0:T(8,128)(2,1)S(1)} collective-permute-done((bf16[1,64,1024]{2,1,0:T(8,128)(2,1)S(1)}, bf16[1,64,1024]{2,1,0:T(8,128)(2,1)S(1)}, u32[]{:S(2)}, u32[]{:S(2)}) %collective-permute-start.18) | collective-permute-done | bytes 131104 | tf_op jit(solution)/shard_map/ppermute | solution.py:229
  90.5 2.8 %all-to-all-done.4.gathered_ref = bf16[16,32,128]{2,1,0:T(8,128)(2,1)S(1)} async-done(((bf16[16,32,128]{2,1,0:T(8,128)(2,1)}), bf16[16,32,128]{2,1,0:T(8,128)(2,1)S(1)}, u32[]{:S(2)}, u32[]{:S(2)}) %all-to-all-start.4) | async-done | bytes 131104 | tf_op jit(solution)/shard_map/all_to_all | solution.py:223
  93.3 1.4 %final.1 = f32[4,32,64]{2,1,0:T(8,128)} custom-call(bf16[16,32,128]{2,1,0:T(8,128)(2,1)S(1)} %all-to-all-done.4.gathered_ref, bf16[64,1024]{1,0:T(8,128)(2,1)S(1)} %copy-done.3, bf16[64,512]{1,0:T(8,128)(2,1)S(1)} %copy-done.5, f32[32,64]{1,0:T(8,128)S(1)} %get-tuple-element.38.first_result_ref, f32[32,64]{1,0:T(8,128)S(1)} %get-tuple-element.39.second_result_ref, ...), custom_call_target="tpu_custom_call" | custom-call | flops 20000000 | bytes 1000000 | tf_op jit(solution)/shard_map/final/pallas_call | solution.py:185
  (29 shorter events, 0.2 us)
Async XLA Ops:
  0.0 0.8 copy-start
  0.0 1.4 %copy-start.1 = (f32[4,64,32]{1,2,0:T(8,128)S(1)}, f32[4,64,32]{1,2,0:T(8,128)}, u32[]{:S(2)}) copy-start(f32[4,64,32]{1,2,0:T(8,128)} %param.7) | copy-start | bytes 98308
  0.0 28.7 %copy-start.2 = (bf16[64,4096]{1,0:T(8,128)(2,1)S(1)}, bf16[64,4096]{1,0:T(8,128)(2,1)}, u32[]{:S(2)}) copy-start(bf16[64,4096]{1,0:T(8,128)(2,1)} %inverse_ref.2) | copy-start | bytes 1572868
  2.2 14.6 %copy-start.3 = (bf16[64,1024]{1,0:T(8,128)(2,1)S(1)}, bf16[64,1024]{1,0:T(8,128)(2,1)}, u32[]{:S(2)}) copy-start(bf16[64,1024]{1,0:T(8,128)(2,1)} %third_ref.1) | copy-start | bytes 393220
  2.2 26.5 %all-to-all-start = ((bf16[64,16,128]{2,1,0:T(8,128)(2,1)}), bf16[64,16,128]{2,1,0:T(8,128)(2,1)S(1)}, u32[]{:S(2)}, u32[]{:S(2)}) async-start(bf16[64,16,128]{2,1,0:T(8,128)(2,1)} %start.1), calls=%async_computation | async-start | bytes 524288 | tf_op jit(solution)/shard_map/all_to_all | solution.py:223
  15.5 14.3 %collective-permute-start.2 = (bf16[3,64,1024]{2,1,0:T(8,128)(2,1)}, bf16[3,64,1024]{2,1,0:T(8,128)(2,1)S(1)}, u32[]{:S(2)}, u32[]{:S(2)}) collective-permute-start(bf16[3,64,1024]{2,1,0:T(8,128)(2,1)} %param.8), channel_id=1, source_target_pairs={{0,1},{1,0},{2,3},{3,2},{4,5},{5,4},{6,7},{7,6},{8,9},{9,8},{10,11... | collective-permute-start | bytes 1179656 | tf_op jit(solution)/shard_map/ppermute | solution.py:226
  16.8 13.0 %collective-permute-start = (bf16[1,64,1024]{2,1,0:T(8,128)(2,1)S(1)}, bf16[1,64,1024]{2,1,0:T(8,128)(2,1)}, u32[]{:S(2)}, u32[]{:S(2)}) collective-permute-start(bf16[1,64,1024]{2,1,0:T(8,128)(2,1)S(1)} %bitcast.9), channel_id=1, source_target_pairs={{0,16},{4,20},{8,24},{12,28},{16,0},{20,4},{24,8},{28,12},{32,48},... | collective-permute-start | bytes 393224 | tf_op jit(solution)/shard_map/ppermute | solution.py:229
  19.7 10.1 %collective-permute-start.1 = (bf16[1,64,1024]{2,1,0:T(8,128)(2,1)S(1)}, bf16[1,64,1024]{2,1,0:T(8,128)(2,1)S(1)}, u32[]{:S(2)}, u32[]{:S(2)}) collective-permute-start(bf16[1,64,1024]{2,1,0:T(8,128)(2,1)S(1)} %bitcast.10), channel_id=1, source_target_pairs={{0,32},{4,36},{8,40},{12,44},{16,48},{20,52},{24,56},{28,60},{32,0... | collective-permute-start | bytes 393224 | tf_op jit(solution)/shard_map/ppermute | solution.py:229
  29.8 20.6 %all-to-all-start.1 = ((bf16[64,16,128]{2,1,0:T(8,128)(2,1)}), bf16[64,16,128]{2,1,0:T(8,128)(2,1)S(1)}, u32[]{:S(2)}, u32[]{:S(2)}) async-start(bf16[64,16,128]{2,1,0:T(8,128)(2,1)} %get-tuple-element.27), calls=%async_computation.1 | async-start | bytes 524288 | tf_op jit(solution)/shard_map/all_to_all | solution.py:223
  37.3 2.5 %copy-start.7 = (bf16[3,64,1024]{2,1,0:T(8,128)(2,1)S(1)}, bf16[3,64,1024]{2,1,0:T(8,128)(2,1)}, u32[]{:S(2)}) copy-start(bf16[3,64,1024]{2,1,0:T(8,128)(2,1)} %param.8) | copy-start | bytes 1179652
  38.3 6.0 %copy-start.6 = (bf16[3,64,1024]{2,1,0:T(8,128)(2,1)}, bf16[3,64,1024]{2,1,0:T(8,128)(2,1)S(1)}, u32[]{:S(2)}) copy-start(bf16[3,64,1024]{2,1,0:T(8,128)(2,1)S(1)} %pad_maximum_fusion.1.refs_0_) | copy-start | bytes 1179652
  38.3 13.4 %collective-permute-start.4 = (bf16[3,64,1024]{2,1,0:T(8,128)(2,1)S(1)}, bf16[3,64,1024]{2,1,0:T(8,128)(2,1)}, u32[]{:S(2)}, u32[]{:S(2)}) collective-permute-start(bf16[3,64,1024]{2,1,0:T(8,128)(2,1)S(1)} %pad_maximum_fusion.1.refs_0_), channel_id=1, source_target_pairs={{0,8},{4,12},{8,0},{12,4},{16,24},{20,28},{24,16},{28,20},{32,40},... | collective-permute-start | bytes 1179656 | tf_op jit(solution)/shard_map/ppermute | solution.py:229
  39.8 8.8 %collective-permute-start.3 = (bf16[2,64,1024]{2,1,0:T(8,128)(2,1)S(1)}, bf16[2,64,1024]{2,1,0:T(8,128)(2,1)S(1)}, u32[]{:S(2)}, u32[]{:S(2)}) collective-permute-start(bf16[2,64,1024]{2,1,0:T(8,128)(2,1)S(1)} %pad_maximum_fusion.2.near_ref), channel_id=1, source_target_pairs={{0,2},{1,3},{2,0},{3,1},{4,6},{5,7},{6,4},{7,5},{8,10},{9,11},{10,... | collective-permute-start | bytes 786440 | tf_op jit(solution)/shard_map/ppermute | solution.py:226
  42.8 18.3 %collective-permute-start.6 = (bf16[4,64,1024]{2,1,0:T(8,128)(2,1)S(1)}, bf16[4,64,1024]{2,1,0:T(8,128)(2,1)S(1)}, u32[]{:S(2)}, u32[]{:S(2)}) collective-permute-start(bf16[4,64,1024]{2,1,0:T(8,128)(2,1)S(1)} %pad_maximum_fusion.near_ref), channel_id=1, source_target_pairs={{0,2},{1,3},{2,0},{3,1},{4,6},{5,7},{6,4},{7,5},{8,10},{9,11},{10,... | collective-permute-start | bytes 1572872 | tf_op jit(solution)/shard_map/ppermute | solution.py:226
  43.1 8.6 %collective-permute-start.5 = (bf16[1,64,1024]{2,1,0:T(8,128)(2,1)}, bf16[1,64,1024]{2,1,0:T(8,128)(2,1)S(1)}, u32[]{:S(2)}, u32[]{:S(2)}) collective-permute-start(bf16[1,64,1024]{2,1,0:T(8,128)(2,1)} %collective-permute-done), channel_id=1, source_target_pairs={{0,32},{4,36},{8,40},{12,44},{16,48},{20,52},{24,56},{28,60},{32,0... | collective-permute-start | bytes 393224 | tf_op jit(solution)/shard_map/ppermute | solution.py:229
  44.3 17.8 %collective-permute-start.7 = (bf16[3,64,1024]{2,1,0:T(8,128)(2,1)S(1)}, bf16[3,64,1024]{2,1,0:T(8,128)(2,1)S(1)}, u32[]{:S(2)}, u32[]{:S(2)}) collective-permute-start(bf16[3,64,1024]{2,1,0:T(8,128)(2,1)S(1)} %pad_maximum_fusion.1.refs_0_), channel_id=1, source_target_pairs={{0,4},{4,0},{8,12},{12,8},{16,20},{20,16},{24,28},{28,24},{32,36},... | collective-permute-start | bytes 1179656 | tf_op jit(solution)/shard_map/ppermute | solution.py:229
  51.6 10.5 %collective-permute-start.8 = (bf16[3,64,1024]{2,1,0:T(8,128)(2,1)}, bf16[3,64,1024]{2,1,0:T(8,128)(2,1)}, u32[]{:S(2)}, u32[]{:S(2)}) collective-permute-start(bf16[3,64,1024]{2,1,0:T(8,128)(2,1)} %collective-permute-done.4.refs_1_), channel_id=1, source_target_pairs={{0,4},{4,0},{8,12},{12,8},{16,20},{20,16},{24,28},{28,24},{32,36},... | collective-permute-start | bytes 1179656 | tf_op jit(solution)/shard_map/ppermute | solution.py:229
  52.5 15.7 %all-to-all-start.2 = ((bf16[32,16,128]{2,1,0:T(8,128)(2,1)}), bf16[32,16,128]{2,1,0:T(8,128)(2,1)S(1)}, u32[]{:S(2)}, u32[]{:S(2)}) async-start(bf16[32,16,128]{2,1,0:T(8,128)(2,1)} %get-tuple-element.32), calls=%async_computation.2 | async-start | bytes 262144 | tf_op jit(solution)/shard_map/all_to_all | solution.py:223
  59.6 14.1 %collective-permute-start.9 = (bf16[1,64,1024]{2,1,0:T(8,128)(2,1)S(1)}, bf16[1,64,1024]{2,1,0:T(8,128)(2,1)S(1)}, u32[]{:S(2)}, u32[]{:S(2)}) collective-permute-start(bf16[1,64,1024]{2,1,0:T(8,128)(2,1)S(1)} %collective-permute-done.5.refs_0_), channel_id=1, source_target_pairs={{0,8},{4,12},{8,0},{12,4},{16,24},{20,28},{24,16},{28,20},{32,40},... | collective-permute-start | bytes 393224 | tf_op jit(solution)/shard_map/ppermute | solution.py:229
  62.1 6.1 %copy-start.4 = (bf16[64,2048]{1,0:T(8,128)(2,1)S(1)}, bf16[64,2048]{1,0:T(8,128)(2,1)}, u32[]{:S(2)}) copy-start(bf16[64,2048]{1,0:T(8,128)(2,1)} %inverse_ref.3) | copy-start | bytes 786436
  62.1 0.8 copy-start.8
  69.2 12.7 %all-to-all-start.3 = ((bf16[32,16,128]{2,1,0:T(8,128)(2,1)}), bf16[32,16,128]{2,1,0:T(8,128)(2,1)S(1)}, u32[]{:S(2)}, u32[]{:S(2)}) async-start(bf16[32,16,128]{2,1,0:T(8,128)(2,1)} %get-tuple-element.36), calls=%async_computation.3 | async-start | bytes 262144 | tf_op jit(solution)/shard_map/all_to_all | solution.py:223
  73.3 1.4 %collective-permute-start.10 = (bf16[1,64,1024]{2,1,0:T(8,128)(2,1)S(1)}, bf16[1,64,1024]{2,1,0:T(8,128)(2,1)S(1)}, u32[]{:S(2)}, u32[]{:S(2)}) collective-permute-start(bf16[1,64,1024]{2,1,0:T(8,128)(2,1)S(1)} %collective-permute-done.5.refs_0_), channel_id=1, source_target_pairs={{0,4},{4,0},{8,12},{12,8},{16,20},{20,16},{24,28},{28,24},{32,36},... | collective-permute-start | bytes 393224 | tf_op jit(solution)/shard_map/ppermute | solution.py:229
  73.7 1.3 %collective-permute-start.11 = (bf16[1,64,1024]{2,1,0:T(8,128)(2,1)S(1)}, bf16[1,64,1024]{2,1,0:T(8,128)(2,1)S(1)}, u32[]{:S(2)}, u32[]{:S(2)}) collective-permute-start(bf16[1,64,1024]{2,1,0:T(8,128)(2,1)S(1)} %collective-permute-done.9.refs_1_), channel_id=1, source_target_pairs={{0,4},{4,0},{8,12},{12,8},{16,20},{20,16},{24,28},{28,24},{32,36},... | collective-permute-start | bytes 393224 | tf_op jit(solution)/shard_map/ppermute | solution.py:229
  75.4 12.0 %collective-permute-start.12 = (bf16[1,64,1024]{2,1,0:T(8,128)(2,1)S(1)}, bf16[1,64,1024]{2,1,0:T(8,128)(2,1)S(1)}, u32[]{:S(2)}, u32[]{:S(2)}) collective-permute-start(bf16[1,64,1024]{2,1,0:T(8,128)(2,1)S(1)} %corner.1.refs_0_), channel_id=1, source_target_pairs={{0,8},{4,12},{8,0},{12,4},{16,24},{20,28},{24,16},{28,20},{32,40},... | collective-permute-start | bytes 393224 | tf_op jit(solution)/shard_map/ppermute | solution.py:229
  77.2 10.5 %collective-permute-start.13 = (bf16[1,64,1024]{2,1,0:T(8,128)(2,1)S(1)}, bf16[1,64,1024]{2,1,0:T(8,128)(2,1)S(1)}, u32[]{:S(2)}, u32[]{:S(2)}) collective-permute-start(bf16[1,64,1024]{2,1,0:T(8,128)(2,1)S(1)} %corner.1.refs_0_), channel_id=1, source_target_pairs={{0,16},{4,20},{8,24},{12,28},{16,0},{20,4},{24,8},{28,12},{32,48},... | collective-permute-start | bytes 393224 | tf_op jit(solution)/shard_map/ppermute | solution.py:229
  79.6 8.9 %collective-permute-start.14 = (bf16[1,64,1024]{2,1,0:T(8,128)(2,1)S(1)}, bf16[1,64,1024]{2,1,0:T(8,128)(2,1)S(1)}, u32[]{:S(2)}, u32[]{:S(2)}) collective-permute-start(bf16[1,64,1024]{2,1,0:T(8,128)(2,1)S(1)} %corner.1.refs_0_), channel_id=1, source_target_pairs={{0,24},{4,28},{8,16},{12,20},{16,8},{20,12},{24,0},{28,4},{32,56},... | collective-permute-start | bytes 393224 | tf_op jit(solution)/shard_map/ppermute | solution.py:229
  83.2 10.1 %copy-start.5 = (bf16[64,512]{1,0:T(8,128)(2,1)S(1)}, bf16[64,512]{1,0:T(8,128)(2,1)}, u32[]{:S(2)}) copy-start(bf16[64,512]{1,0:T(8,128)(2,1)} %fourth_ref.1) | copy-start | bytes 196612
  83.2 10.1 %all-to-all-start.4 = ((bf16[16,32,128]{2,1,0:T(8,128)(2,1)}), bf16[16,32,128]{2,1,0:T(8,128)(2,1)S(1)}, u32[]{:S(2)}, u32[]{:S(2)}) async-start(bf16[16,32,128]{2,1,0:T(8,128)(2,1)} %update2.1), calls=%async_computation.4 | async-start | bytes 262144 | tf_op jit(solution)/shard_map/all_to_all | solution.py:223
  87.1 2.3 %collective-permute-start.15 = (bf16[1,64,1024]{2,1,0:T(8,128)(2,1)S(1)}, bf16[1,64,1024]{2,1,0:T(8,128)(2,1)S(1)}, u32[]{:S(2)}, u32[]{:S(2)}) collective-permute-start(bf16[1,64,1024]{2,1,0:T(8,128)(2,1)S(1)} %corner.1.refs_0_), channel_id=1, source_target_pairs={{0,4},{4,0},{8,12},{12,8},{16,20},{20,16},{24,28},{28,24},{32,36},... | collective-permute-start | bytes 393224 | tf_op jit(solution)/shard_map/ppermute | solution.py:229
  87.3 2.2 %collective-permute-start.16 = (bf16[1,64,1024]{2,1,0:T(8,128)(2,1)S(1)}, bf16[1,64,1024]{2,1,0:T(8,128)(2,1)S(1)}, u32[]{:S(2)}, u32[]{:S(2)}) collective-permute-start(bf16[1,64,1024]{2,1,0:T(8,128)(2,1)S(1)} %collective-permute-done.12.refs_1_), channel_id=1, source_target_pairs={{0,4},{4,0},{8,12},{12,8},{16,20},{20,16},{24,28},{28,24},{32,36},... | collective-permute-start | bytes 393224 | tf_op jit(solution)/shard_map/ppermute | solution.py:229
  87.7 1.8 %collective-permute-start.17 = (bf16[1,64,1024]{2,1,0:T(8,128)(2,1)S(1)}, bf16[1,64,1024]{2,1,0:T(8,128)(2,1)S(1)}, u32[]{:S(2)}, u32[]{:S(2)}) collective-permute-start(bf16[1,64,1024]{2,1,0:T(8,128)(2,1)S(1)} %collective-permute-done.13.refs_2_), channel_id=1, source_target_pairs={{0,4},{4,0},{8,12},{12,8},{16,20},{20,16},{24,28},{28,24},{32,36},... | collective-permute-start | bytes 393224 | tf_op jit(solution)/shard_map/ppermute | solution.py:229
  88.5 2.0 %collective-permute-start.18 = (bf16[1,64,1024]{2,1,0:T(8,128)(2,1)S(1)}, bf16[1,64,1024]{2,1,0:T(8,128)(2,1)S(1)}, u32[]{:S(2)}, u32[]{:S(2)}) collective-permute-start(bf16[1,64,1024]{2,1,0:T(8,128)(2,1)S(1)} %collective-permute-done.14.refs_3_), channel_id=1, source_target_pairs={{0,4},{4,0},{8,12},{12,8},{16,20},{20,16},{24,28},{28,24},{32,36},... | collective-permute-start | bytes 393224 | tf_op jit(solution)/shard_map/ppermute | solution.py:229

commit v7 on v6

--- a/solution.py
+++ b/solution.py
@@ -17,6 +17,17 @@
     half = block.shape[0] // 2
     packed = jnp.concatenate((block[:half], block[half:]), axis=1).astype(jnp.bfloat16)
     return jnp.broadcast_to(packed[None], (copies, *packed.shape))
+
+
+def unpack_cores(mine_ref, other_ref, store):
+    core = lax.axis_index("sn") % 2
+    lanes = mine_ref.shape[2] // 2
+    for b in range(mine_ref.shape[0]):
+        one = jnp.where(core == 0, mine_ref[b], other_ref[b])
+        two = jnp.where(core == 0, other_ref[b], mine_ref[b])
+        top = jnp.concatenate((one[:, :lanes], two[:, :lanes]), axis=1)
+        low = jnp.concatenate((one[:, lanes:], two[:, lanes:]), axis=1)
+        store(b, jnp.concatenate((top, low), axis=0))
 
 
 def unpack(gathered, store):
@@ -139,7 +150,11 @@
     return found
 
 
-def update_kernel(tiers, kept, index_ref, gathered_ref, right_ref, near_ref, far_ref, *refs):
+def update_kernel(tiers, kept, parts, index_ref, gathered_ref, right_ref, *refs):
+    if kept:
+        other_ref, refs = refs[0], refs[1:]
+    below = refs[:parts] if kept else refs[:2]
+    refs = refs[len(below) :]
     known_ref, flat_ref = refs[-2], refs[-1]
     base = 0
     if not kept:
@@ -151,20 +166,22 @@
     def store(b, block):
         known_ref[base + b] = block
 
-    unpack(gathered_ref, store)
+    if kept:
+        unpack_cores(gathered_ref, other_ref, store)
+    else:
+        unpack(gathered_ref, store)
     if kept:
         refs[1][...] = known_ref[...]
     else:
         known_ref[known_ref.shape[0] - 1] = jnp.zeros(known_ref.shape[1:], known_ref.dtype)
     places = index_ref[...]
-    quarter = near_ref.shape[2] // BS
-    parts = RB // quarter
+    quarter = RB // parts
     slot = 0
     packed = []
     for t, tier in enumerate(tiers):
         total = right_ref[tier]
         for k in range(parts):
-            ref = below_part(near_ref, far_ref, k, t, len(tiers))
+            ref = below[k] if kept else below_part(*below, k, t, len(tiers))
             for p in range(quarter):
                 block = known_ref[places[tier - 1, k * quarter + p]]
                 flat_ref[slot, :, p * BS : (p + 1) * BS] = block
@@ -181,14 +198,14 @@
     return [pltpu.with_memory_space_constraint(array, pltpu.HBM) for array in arrays]
 
 
-def call(kernel, name, outs, scratch, *args):
+def call(kernel, name, outs, scratch, *args, flops=20_000_000):
     return pl.pallas_call(
         kernel,
         out_shape=outs,
         in_specs=[VMEM] * len(args),
         out_specs=[VMEM] * len(outs),
         scratch_shapes=scratch,
-        cost_estimate=pl.CostEstimate(flops=20_000_000, bytes_accessed=1_000_000, transcendentals=0),
+        cost_estimate=pl.CostEstimate(flops=flops, bytes_accessed=flops // 20, transcendentals=0),
         compiler_params=pltpu.CompilerParams(vmem_limit_bytes=16 * 2**20),
         name=name,
     )(*args)
@@ -222,6 +239,10 @@
             sets = [list(range(s, s + n)) for s in range(0, devices, n)]
         return lax.all_to_all(copies, "sn", 0, 0, axis_index_groups=sets)
 
+    def gather_core(copies):
+        sets = [[2 * k + c for k in range(devices // 2)] for c in range(2)]
+        return lax.all_to_all(copies, "sn", 0, 0, axis_index_groups=sets)
+
     def swap_group(part, bit):
         return lax.ppermute(part, "rhs", [(i, i ^ bit) for i in range(groups)])
 
@@ -250,8 +271,9 @@
     positions = jnp.sum(jnp.where(hit, turned[None, :], 0), axis=1)[None].astype(jnp.int32)
     places, positions, right_sides = barrier((places, positions, right_sides))
 
-    below = factor_below
-    below_got = swap_group(below, 1)
+    first_below, rest_below = factor_below[0], factor_below[1:]
+    first_got = [swap_group(first_below, bits) for bits in (1, 3)]
+    rest_got = swap_group(rest_below, 1)
     third = inverse_third[None]
     far, near = swap(third, y_high), swap(third, z_low)
 
@@ -260,32 +282,34 @@
     first_result, copies = call(
         solve_kernel,
         "solve0",
-        [shape((columns, rows), f32), shape((members[0], *message), bf16)],
+        [shape((columns, rows), f32), shape((devices // 2, *message), bf16)],
         [pltpu.VMEM((columns, members[0] * rows), bf16)],
         gathered,
         inverse_top,
     )
 
-    copies, (far, near), below_got = barrier((copies, (far, near), below_got))
-    first_below = jnp.stack((below[0], below_got[0]))
-    first_far = swap_group(first_below, 2)
-    rest_below = jnp.concatenate((below[1:], below_got[1:]))
+    copies, far, near, first_got, rest_got = barrier((copies, far, near, first_got, rest_got))
+    first_parts = (first_below, first_got[0], swap_group(first_below, 2), first_got[1])
+    rest_below = jnp.concatenate((rest_below, rest_got))
     rest_far = swap_group(rest_below, 2)
     third = jnp.concatenate((third, far, near))
     third_got = swap(third, y_low)
     corner = swap(far, z_low)
 
-    gathered = gather(copies)
+    gathered = gather_core(copies)
+    gathered, corner, first_parts = barrier((gathered, corner, first_parts))
+    other = swap(gathered, core)
     copies, known = call(
-        functools.partial(update_kernel, (1,), True),
+        functools.partial(update_kernel, (1,), True, groups),
         "update1",
         [shape((members[1], *message), bf16), shape((NB, columns, BS), bf16)],
         [pltpu.VMEM((NB, columns, BS), bf16), pltpu.VMEM((groups, columns, RB // groups * BS), bf16)],
         places,
         gathered,
         right_sides,
-        first_below,
-        first_far,
+        other,
+        *first_parts,
+        flops=20_000,
     )
 
     copies, third_got, corner = barrier((copies, third_got, corner))
@@ -330,7 +354,7 @@
     gathered = gather(copies)
     blocks = NB + NB // 2 + 1
     (copies,) = call(
-        functools.partial(update_kernel, (2, 3), False),
+        functools.partial(update_kernel, (2, 3), False, groups),
         "update2",
         [shape((members[2], 2 * message[0], message[1]), bf16)],
         [pltpu.VMEM((blocks, columns, BS), bf16), pltpu.VMEM((2 * groups, columns, RB // groups * BS), bf16)],

time: 95.2 us -> 91.7 us (0.963)
  other arithmetic: 1.46 us -> 0.48 us
    all_to_all x5 -> x4, starting transfers between devices: 36 us -> 25.3 us  [gather(): return lax.all_to_all(copies, 'sn', 0, 0, axis_index_groups=sets)]
    all_to_all x0 -> x1, starting transfers between devices: none -> 5.9 us  [gather_core(): return lax.all_to_all(copies, 'sn', 0, 0, axis_index_groups=sets)]
    all_to_all x5 -> x4, waiting for transfers between devices: 18 us -> 14.5 us  [gather(): return lax.all_to_all(copies, 'sn', 0, 0, axis_index_groups=sets)]
    ppermute x16 -> x17, waiting for transfers between devices: 2.71 us -> 5.74 us  [swap(): return lax.ppermute(part, 'sn', [(i, i ^ bit) for i in range(devices)])]
    ppermute x3 -> x5, starting transfers between devices: 4.44 us -> 7.26 us  [swap_group(): return lax.ppermute(part, 'rhs', [(i, i ^ bit) for i in range(groups)])]
    ppermute x3 -> x5, waiting for transfers between devices: 2.89 us -> 0.99 us  [swap_group(): return lax.ppermute(part, 'rhs', [(i, i ^ bit) for i in range(groups)])]
    all_to_all x0 -> x1, waiting for transfers between devices: none -> 1.7 us  [gather_core(): return lax.all_to_all(copies, 'sn', 0, 0, axis_index_groups=sets)]
    ppermute x16 -> x17, starting transfers between devices: 17.1 us -> 18.1 us  [swap(): return lax.ppermute(part, 'sn', [(i, i ^ bit) for i in range(devices)])]
  transfers between devices with their start and end apart: 24 -> 27, of which waited for: 10 -> 12; matrix products, arithmetic and copies ran while one was open for 1% -> 0% of each run, Pallas kernels for 8% -> 9%
where the time goes in v7:
time: 91.7 us; the launch traced here: 91.2 us
  starting transfers between devices  56.6 us (62%)
  waiting for transfers between devices  22.9 us (25%)
  Pallas kernels  9.93 us (11%)
  local copies, waits for them, and re-layouts  1 us (1%)
    all_to_all x4, starting transfers between devices, gather(): return lax.all_to_all(copies, 'sn', 0, 0, axis_index_groups=sets)  25.3 us
    ppermute x17, starting transfers between devices, swap(): return lax.ppermute(part, 'sn', [(i, i ^ bit) for i in range(devices)])  18.1 us
    all_to_all x4, waiting for transfers between devices, gather(): return lax.all_to_all(copies, 'sn', 0, 0, axis_index_groups=sets)  14.5 us
    pallas_call x9, Pallas kernels, call(): pl.pallas_call(kernel, out_shape=outs, in_specs=[VMEM] * len(args), out_s...  9.93 us
    ppermute x5, starting transfers between devices, swap_group(): return lax.ppermute(part, 'rhs', [(i, i ^ bit) for i in range(groups)])  7.26 us
    all_to_all x1, starting transfers between devices, gather_core(): return lax.all_to_all(copies, 'sn', 0, 0, axis_index_groups=sets)  5.9 us
    ppermute x17, waiting for transfers between devices, swap(): return lax.ppermute(part, 'sn', [(i, i ^ bit) for i in range(devices)])  5.74 us
  transfers between devices with their start and end apart: 27, of which 12 were waited for; matrix products, arithmetic and copies ran while one was open for 0% of the time, Pallas kernels for 9%

profile of v7, /device:TPU:1, one launch (start us, length us, event | category | flops | bytes accessed | tf_op | source)
XLA Modules:
  0.0 91.2 jit_solution(7424222441592640643)
XLA Ops:
  0.1 0.7 copy-done
  0.9 0.1 squeeze.7
  0.9 0.1 iota_compare_fusion
  1.0 0.1 select_reduce_fusion
  1.1 0.1 reshape.100.index_ref
  1.2 0.2 select_reduce_fusion.1
  1.4 0.0 copy-start.7
  1.4 0.8 start.1
  2.2 13.2 %all-to-all-start = ((bf16[64,16,128]{2,1,0:T(8,128)(2,1)}), bf16[64,16,128]{2,1,0:T(8,128)(2,1)S(1)}, u32[]{:S(2)}, u32[]{:S(2)}) async-start(bf16[64,16,128]{2,1,0:T(8,128)(2,1)} %start.1), calls=%async_computation | async-start | bytes 524288 | tf_op jit(solution)/shard_map/all_to_all | solution.py:240
  15.4 0.0 copy-start.2
  15.4 0.0 copy-start.3
  15.4 1.3 %collective-permute-start.4 = (bf16[2,64,1024]{2,1,0:T(8,128)(2,1)S(1)}, bf16[2,64,1024]{2,1,0:T(8,128)(2,1)S(1)}, u32[]{:S(2)}, u32[]{:S(2)}) collective-permute-start(bf16[2,64,1024]{2,1,0:T(8,128)(2,1)S(1)} %slice.12), channel_id=1, source_target_pairs={{0,1},{1,0},{2,3},{3,2},{4,5},{5,4},{6,7},{7,6},{8,9},{9,8},{10,11... | collective-permute-start | bytes 786440 | tf_op jit(solution)/shard_map/ppermute | solution.py:247
  16.7 0.4 collective-permute-start.2
  17.1 2.5 %collective-permute-start.3 = (bf16[64,1024]{1,0:T(8,128)(2,1)S(1)}, bf16[64,1024]{1,0:T(8,128)(2,1)S(1)}, u32[]{:S(2)}, u32[]{:S(2)}) collective-permute-start(bf16[64,1024]{1,0:T(8,128)(2,1)S(1)} %slice_bitcast_fusion.refs_1_), channel_id=1, source_target_pairs={{0,3},{1,2},{2,1},{3,0},{4,7},{5,6},{6,5},{7,4},{8,11},{9,10},{10,... | collective-permute-start | bytes 393224 | tf_op jit(solution)/shard_map/ppermute | solution.py:247
  19.6 2.9 %collective-permute-start = (bf16[1,64,1024]{2,1,0:T(8,128)(2,1)S(1)}, bf16[1,64,1024]{2,1,0:T(8,128)(2,1)S(1)}, u32[]{:S(2)}, u32[]{:S(2)}) collective-permute-start(bf16[1,64,1024]{2,1,0:T(8,128)(2,1)S(1)} %bitcast.11), channel_id=1, source_target_pairs={{0,16},{4,20},{8,24},{12,28},{16,0},{20,4},{24,8},{28,12},{32,48},... | collective-permute-start | bytes 393224 | tf_op jit(solution)/shard_map/ppermute | solution.py:250
  22.5 1.2 %collective-permute-start.1 = (bf16[1,64,1024]{2,1,0:T(8,128)(2,1)S(1)}, bf16[1,64,1024]{2,1,0:T(8,128)(2,1)S(1)}, u32[]{:S(2)}, u32[]{:S(2)}) collective-permute-start(bf16[1,64,1024]{2,1,0:T(8,128)(2,1)S(1)} %bitcast.12), channel_id=1, source_target_pairs={{0,32},{4,36},{8,40},{12,44},{16,48},{20,52},{24,56},{28,60},{32,0... | collective-permute-start | bytes 393224 | tf_op jit(solution)/shard_map/ppermute | solution.py:250
  23.6 4.9 %all-to-all-done.gathered_ref = bf16[64,16,128]{2,1,0:T(8,128)(2,1)S(1)} async-done(((bf16[64,16,128]{2,1,0:T(8,128)(2,1)}), bf16[64,16,128]{2,1,0:T(8,128)(2,1)S(1)}, u32[]{:S(2)}, u32[]{:S(2)}) %all-to-all-start) | async-done | bytes 262176 | tf_op jit(solution)/shard_map/all_to_all | solution.py:240
  28.5 1.1 %solve0.1 = (f32[32,64]{1,0:T(8,128)S(1)}, bf16[32,16,128]{2,1,0:T(8,128)(2,1)}) custom-call(bf16[64,16,128]{2,1,0:T(8,128)(2,1)S(1)} %all-to-all-done.gathered_ref, bf16[64,4096]{1,0:T(8,128)(2,1)S(1)} %copy-done.2), custom_call_target="tpu_custom_call" | custom-call | flops 20000000 | bytes 1000000 | tf_op jit(solution)/shard_map/solve0/pallas_call | solution.py:202
  29.6 0.0 collective-permute-done.3.refs_4_
  29.6 0.0 collective-permute-done
  29.6 0.0 collective-permute-done.4
  29.7 0.8 collective-permute-start.8
  30.5 5.9 %all-to-all-start.1 = ((bf16[32,16,128]{2,1,0:T(8,128)(2,1)}), bf16[32,16,128]{2,1,0:T(8,128)(2,1)S(1)}, u32[]{:S(2)}, u32[]{:S(2)}) async-start(bf16[32,16,128]{2,1,0:T(8,128)(2,1)} %get-tuple-element.35), calls=%async_computation.1 | async-start | bytes 262144 | tf_op jit(solution)/shard_map/all_to_all | solution.py:244
  36.4 2.8 %collective-permute-start.6 = (bf16[64,1024]{1,0:T(8,128)(2,1)S(1)}, bf16[64,1024]{1,0:T(8,128)(2,1)S(1)}, u32[]{:S(2)}, u32[]{:S(2)}) collective-permute-start(bf16[64,1024]{1,0:T(8,128)(2,1)S(1)} %slice_bitcast_fusion.refs_1_), channel_id=1, source_target_pairs={{0,2},{1,3},{2,0},{3,1},{4,6},{5,7},{6,4},{7,5},{8,10},{9,11},{10,... | collective-permute-start | bytes 393224 | tf_op jit(solution)/shard_map/ppermute | solution.py:247
  39.3 1.2 %collective-permute-start.5 = (bf16[1,64,1024]{2,1,0:T(8,128)(2,1)S(1)}, bf16[1,64,1024]{2,1,0:T(8,128)(2,1)S(1)}, u32[]{:S(2)}, u32[]{:S(2)}) collective-permute-start(bf16[1,64,1024]{2,1,0:T(8,128)(2,1)S(1)} %collective-permute-done), channel_id=1, source_target_pairs={{0,32},{4,36},{8,40},{12,44},{16,48},{20,52},{24,56},{28,60},{32,0... | collective-permute-start | bytes 393224 | tf_op jit(solution)/shard_map/ppermute | solution.py:250
  40.5 0.3 collective-permute-start.9
  40.9 1.0 %collective-permute-done.6.refs_3_ = bf16[64,1024]{1,0:T(8,128)(2,1)S(1)} collective-permute-done((bf16[64,1024]{1,0:T(8,128)(2,1)S(1)}, bf16[64,1024]{1,0:T(8,128)(2,1)S(1)}, u32[]{:S(2)}, u32[]{:S(2)}) %collective-permute-start.6) | collective-permute-done | bytes 131104 | tf_op jit(solution)/shard_map/ppermute | solution.py:247
  41.8 2.3 %collective-permute-done.5.refs_0_ = bf16[1,64,1024]{2,1,0:T(8,128)(2,1)S(1)} collective-permute-done((bf16[1,64,1024]{2,1,0:T(8,128)(2,1)S(1)}, bf16[1,64,1024]{2,1,0:T(8,128)(2,1)S(1)}, u32[]{:S(2)}, u32[]{:S(2)}) %collective-permute-start.5) | collective-permute-done | bytes 131104 | tf_op jit(solution)/shard_map/ppermute | solution.py:250
  44.1 1.7 %all-to-all-done.1.gathered_ref = bf16[32,16,128]{2,1,0:T(8,128)(2,1)S(1)} async-done(((bf16[32,16,128]{2,1,0:T(8,128)(2,1)}), bf16[32,16,128]{2,1,0:T(8,128)(2,1)S(1)}, u32[]{:S(2)}, u32[]{:S(2)}) %all-to-all-start.1) | async-done | bytes 131104 | tf_op jit(solution)/shard_map/all_to_all | solution.py:244
  45.8 3.5 %collective-permute-start.7 = (bf16[32,16,128]{2,1,0:T(8,128)(2,1)S(1)}, bf16[32,16,128]{2,1,0:T(8,128)(2,1)S(1)}, u32[]{:S(2)}, u32[]{:S(2)}) collective-permute-start(bf16[32,16,128]{2,1,0:T(8,128)(2,1)S(1)} %all-to-all-done.1.gathered_ref), channel_id=1, source_target_pairs={{0,4},{4,0},{8,12},{12,8},{16,20},{20,16},{24,28},{28,24},{32,36},... | collective-permute-start | bytes 393224 | tf_op jit(solution)/shard_map/ppermute | solution.py:250
  49.3 0.0 collective-permute-start.10
  49.3 1.1 %collective-permute-done.7.refs_0_ = bf16[32,16,128]{2,1,0:T(8,128)(2,1)S(1)} collective-permute-done((bf16[32,16,128]{2,1,0:T(8,128)(2,1)S(1)}, bf16[32,16,128]{2,1,0:T(8,128)(2,1)S(1)}, u32[]{:S(2)}, u32[]{:S(2)}) %collective-permute-start.7) | collective-permute-done | bytes 131104 | tf_op jit(solution)/shard_map/ppermute | solution.py:250
  50.4 1.2 %update1.1 = (bf16[32,16,128]{2,1,0:T(8,128)(2,1)}, bf16[32,32,128]{2,1,0:T(8,128)(2,1)S(1)}) custom-call(s32[3,32]{1,0:T(4,128)S(1)} %reshape.100.index_ref, bf16[32,16,128]{2,1,0:T(8,128)(2,1)S(1)} %all-to-all-done.1.gathered_ref, f32[4,32,64]{2,1,0:T(8,128)S(1)} %bitcast.9, bf16[32,16,128]{2,1,0:T(8,128)(2,1)S(1)} %collective-permute-done.7.refs_0_, ...), custom_call_target="tpu_custom_call" | custom-call | flops 20000 | bytes 1000 | tf_op jit(solution)/shard_map/update1/pallas_call | solution.py:202
  51.6 0.0 collective-permute-done.8.refs_1_
  51.6 0.4 collective-permute-start.11
  52.0 4.4 %all-to-all-start.2 = ((bf16[32,16,128]{2,1,0:T(8,128)(2,1)}), bf16[32,16,128]{2,1,0:T(8,128)(2,1)S(1)}, u32[]{:S(2)}, u32[]{:S(2)}) async-start(bf16[32,16,128]{2,1,0:T(8,128)(2,1)} %get-tuple-element.47), calls=%async_computation.2 | async-start | bytes 262144 | tf_op jit(solution)/shard_map/all_to_all | solution.py:240
  56.4 1.5 %collective-permute-start.12 = (bf16[1,64,1024]{2,1,0:T(8,128)(2,1)S(1)}, bf16[1,64,1024]{2,1,0:T(8,128)(2,1)S(1)}, u32[]{:S(2)}, u32[]{:S(2)}) collective-permute-start(bf16[1,64,1024]{2,1,0:T(8,128)(2,1)S(1)} %collective-permute-done.5.refs_0_), channel_id=1, source_target_pairs={{0,8},{4,12},{8,0},{12,4},{16,24},{20,28},{24,16},{28,20},{32,40},... | collective-permute-start | bytes 393224 | tf_op jit(solution)/shard_map/ppermute | solution.py:250
  57.9 0.0 collective-permute-done.9.far_ref.refs_1_
  57.9 1.0 %select.40.coupled_ref = bf16[1,64,1024]{2,1,0:T(8,128)(2,1)S(1)} custom-call(s32[1,8]{1,0:T(1,128)S(1)} %bitcast.14, bf16[4,64,1024]{2,1,0:T(8,128)(2,1)S(1)} %pad_maximum_fusion.near_ref.refs_0_, bf16[4,64,1024]{2,1,0:T(8,128)(2,1)S(1)} %collective-permute-done.9.far_ref.refs_1_), custom_call_target="tpu_custom_call" | custom-call | flops 20000000 | bytes 1000000 | tf_op jit(solution)/shard_map/select/pallas_call | solution.py:202
  58.9 0.0 copy-start.4
  58.9 0.0 collective-permute-done.11.refs_3_
  58.9 1.9 %product.1.refs_4_ = f32[1,64,1024]{2,1,0:T(8,128)S(1)} custom-call(bf16[1,64,1024]{2,1,0:T(8,128)(2,1)S(1)} %select.40.coupled_ref, bf16[3,64,1024]{2,1,0:T(8,128)(2,1)} %copy-done.6, bf16[3,64,1024]{2,1,0:T(8,128)(2,1)} %copy-done.8, bf16[3,64,1024]{2,1,0:T(8,128)(2,1)} %collective-permute-done.10.refs_2_, bf16[3,64,1024]{2,1,0:T(8,128)(2,1)} %collective-permute-done.11.refs_3_), custom_call_target="tpu_custom_call" | custom-call | flops 20000000 | bytes 1000000 | tf_op jit(solution)/shard_map/product/pallas_call | solution.py:202
  60.9 4.1 %all-to-all-done.2.gathered_ref = bf16[32,16,128]{2,1,0:T(8,128)(2,1)S(1)} async-done(((bf16[32,16,128]{2,1,0:T(8,128)(2,1)}), bf16[32,16,128]{2,1,0:T(8,128)(2,1)S(1)}, u32[]{:S(2)}, u32[]{:S(2)}) %all-to-all-start.2) | async-done | bytes 131104 | tf_op jit(solution)/shard_map/all_to_all | solution.py:240
  65.0 1.0 %solve1.1 = (f32[32,64]{1,0:T(8,128)S(1)}, bf16[32,16,128]{2,1,0:T(8,128)(2,1)}) custom-call(bf16[32,16,128]{2,1,0:T(8,128)(2,1)S(1)} %all-to-all-done.2.gathered_ref, bf16[64,2048]{1,0:T(8,128)(2,1)S(1)} %copy-done.4), custom_call_target="tpu_custom_call" | custom-call | flops 20000000 | bytes 1000000 | tf_op jit(solution)/shard_map/solve1/pallas_call | solution.py:202
  66.0 3.9 %all-to-all-start.3 = ((bf16[32,16,128]{2,1,0:T(8,128)(2,1)}), bf16[32,16,128]{2,1,0:T(8,128)(2,1)S(1)}, u32[]{:S(2)}, u32[]{:S(2)}) async-start(bf16[32,16,128]{2,1,0:T(8,128)(2,1)} %get-tuple-element.52), calls=%async_computation.3 | async-start | bytes 262144 | tf_op jit(solution)/shard_map/all_to_all | solution.py:240
  69.9 0.4 collective-permute-start.13
  70.3 0.3 collective-permute-start.14
  70.6 0.7 collective-permute-done.13.refs_2_
  71.3 0.4 collective-permute-done.14.refs_3_
  71.7 0.4 corner.1.refs_0_
  72.0 1.5 %collective-permute-start.15 = (bf16[1,64,1024]{2,1,0:T(8,128)(2,1)S(1)}, bf16[1,64,1024]{2,1,0:T(8,128)(2,1)S(1)}, u32[]{:S(2)}, u32[]{:S(2)}) collective-permute-start(bf16[1,64,1024]{2,1,0:T(8,128)(2,1)S(1)} %corner.1.refs_0_), channel_id=1, source_target_pairs={{0,8},{4,12},{8,0},{12,4},{16,24},{20,28},{24,16},{28,20},{32,40},... | collective-permute-start | bytes 393224 | tf_op jit(solution)/shard_map/ppermute | solution.py:250
  73.5 2.4 %collective-permute-start.16 = (bf16[1,64,1024]{2,1,0:T(8,128)(2,1)S(1)}, bf16[1,64,1024]{2,1,0:T(8,128)(2,1)S(1)}, u32[]{:S(2)}, u32[]{:S(2)}) collective-permute-start(bf16[1,64,1024]{2,1,0:T(8,128)(2,1)S(1)} %corner.1.refs_0_), channel_id=1, source_target_pairs={{0,16},{4,20},{8,24},{12,28},{16,0},{20,4},{24,8},{28,12},{32,48},... | collective-permute-start | bytes 393224 | tf_op jit(solution)/shard_map/ppermute | solution.py:250
  75.9 0.1 collective-permute-start.17
  76.0 2.5 %all-to-all-done.3.gathered_ref = bf16[32,16,128]{2,1,0:T(8,128)(2,1)S(1)} async-done(((bf16[32,16,128]{2,1,0:T(8,128)(2,1)}), bf16[32,16,128]{2,1,0:T(8,128)(2,1)S(1)}, u32[]{:S(2)}, u32[]{:S(2)}) %all-to-all-start.3) | async-done | bytes 131104 | tf_op jit(solution)/shard_map/all_to_all | solution.py:240
  78.5 1.3 %update2.1 = bf16[16,32,128]{2,1,0:T(8,128)(2,1)} custom-call(s32[3,32]{1,0:T(4,128)S(1)} %reshape.100.index_ref, bf16[32,16,128]{2,1,0:T(8,128)(2,1)S(1)} %all-to-all-done.3.gathered_ref, f32[4,32,64]{2,1,0:T(8,128)S(1)} %bitcast.10, bf16[4,64,1024]{2,1,0:T(8,128)(2,1)S(1)} %pad_maximum_fusion.near_ref.refs_0_, ...), custom_call_target="tpu_custom_call" | custom-call | flops 20000000 | bytes 1000000 | tf_op jit(solution)/shard_map/update2/pallas_call | solution.py:202
  79.8 3.9 %all-to-all-start.4 = ((bf16[16,32,128]{2,1,0:T(8,128)(2,1)}), bf16[16,32,128]{2,1,0:T(8,128)(2,1)S(1)}, u32[]{:S(2)}, u32[]{:S(2)}) async-start(bf16[16,32,128]{2,1,0:T(8,128)(2,1)} %update2.1), calls=%async_computation.4 | async-start | bytes 262144 | tf_op jit(solution)/shard_map/all_to_all | solution.py:240
  83.7 0.3 collective-permute-start.18
  83.9 0.3 collective-permute-start.19
  84.2 0.3 collective-permute-start.20
  84.4 0.3 collective-permute-done.17.refs_3_
  84.8 1.1 %collective-permute-start.21 = (bf16[1,64,1024]{2,1,0:T(8,128)(2,1)S(1)}, bf16[1,64,1024]{2,1,0:T(8,128)(2,1)S(1)}, u32[]{:S(2)}, u32[]{:S(2)}) collective-permute-start(bf16[1,64,1024]{2,1,0:T(8,128)(2,1)S(1)} %collective-permute-done.17.refs_3_), channel_id=1, source_target_pairs={{0,4},{4,0},{8,12},{12,8},{16,20},{20,16},{24,28},{28,24},{32,36},... | collective-permute-start | bytes 393224 | tf_op jit(solution)/shard_map/ppermute | solution.py:250
  85.9 1.0 %collective-permute-done.21.refs_7_ = bf16[1,64,1024]{2,1,0:T(8,128)(2,1)S(1)} collective-permute-done((bf16[1,64,1024]{2,1,0:T(8,128)(2,1)S(1)}, bf16[1,64,1024]{2,1,0:T(8,128)(2,1)S(1)}, u32[]{:S(2)}, u32[]{:S(2)}) %collective-permute-start.21) | collective-permute-done | bytes 131104 | tf_op jit(solution)/shard_map/ppermute | solution.py:250
  86.9 3.0 %all-to-all-done.4.gathered_ref = bf16[16,32,128]{2,1,0:T(8,128)(2,1)S(1)} async-done(((bf16[16,32,128]{2,1,0:T(8,128)(2,1)}), bf16[16,32,128]{2,1,0:T(8,128)(2,1)S(1)}, u32[]{:S(2)}, u32[]{:S(2)}) %all-to-all-start.4) | async-done | bytes 131104 | tf_op jit(solution)/shard_map/all_to_all | solution.py:240
  89.8 1.4 %final.1 = f32[4,32,64]{2,1,0:T(8,128)} custom-call(bf16[16,32,128]{2,1,0:T(8,128)(2,1)S(1)} %all-to-all-done.4.gathered_ref, bf16[64,1024]{1,0:T(8,128)(2,1)S(1)} %copy-done.3, bf16[64,512]{1,0:T(8,128)(2,1)S(1)} %copy-done.5, f32[32,64]{1,0:T(8,128)S(1)} %get-tuple-element.54.first_result_ref, f32[32,64]{1,0:T(8,128)S(1)} %get-tuple-element.55.second_result_ref, ...), custom_call_target="tpu_custom_call" | custom-call | flops 20000000 | bytes 1000000 | tf_op jit(solution)/shard_map/final/pallas_call | solution.py:202
  (32 shorter events, 0.2 us)
Async XLA Ops:
  0.0 0.8 copy-start
  0.0 1.4 %copy-start.1 = (f32[4,64,32]{1,2,0:T(8,128)S(1)}, f32[4,64,32]{1,2,0:T(8,128)}, u32[]{:S(2)}) copy-start(f32[4,64,32]{1,2,0:T(8,128)} %param.7) | copy-start | bytes 98308
  1.4 14.0 %copy-start.7 = (bf16[3,64,1024]{2,1,0:T(8,128)(2,1)S(1)}, bf16[3,64,1024]{2,1,0:T(8,128)(2,1)}, u32[]{:S(2)}) copy-start(bf16[3,64,1024]{2,1,0:T(8,128)(2,1)} %param.8) | copy-start | bytes 1179652
  2.2 26.3 %all-to-all-start = ((bf16[64,16,128]{2,1,0:T(8,128)(2,1)}), bf16[64,16,128]{2,1,0:T(8,128)(2,1)S(1)}, u32[]{:S(2)}, u32[]{:S(2)}) async-start(bf16[64,16,128]{2,1,0:T(8,128)(2,1)} %start.1), calls=%async_computation | async-start | bytes 524288 | tf_op jit(solution)/shard_map/all_to_all | solution.py:240
  15.4 13.2 %copy-start.2 = (bf16[64,4096]{1,0:T(8,128)(2,1)S(1)}, bf16[64,4096]{1,0:T(8,128)(2,1)}, u32[]{:S(2)}) copy-start(bf16[64,4096]{1,0:T(8,128)(2,1)} %inverse_ref.2) | copy-start | bytes 1572868
  15.4 4.1 %copy-start.3 = (bf16[64,1024]{1,0:T(8,128)(2,1)S(1)}, bf16[64,1024]{1,0:T(8,128)(2,1)}, u32[]{:S(2)}) copy-start(bf16[64,1024]{1,0:T(8,128)(2,1)} %third_ref.1) | copy-start | bytes 393220
  15.4 14.2 %collective-permute-start.4 = (bf16[2,64,1024]{2,1,0:T(8,128)(2,1)S(1)}, bf16[2,64,1024]{2,1,0:T(8,128)(2,1)S(1)}, u32[]{:S(2)}, u32[]{:S(2)}) collective-permute-start(bf16[2,64,1024]{2,1,0:T(8,128)(2,1)S(1)} %slice.12), channel_id=1, source_target_pairs={{0,1},{1,0},{2,3},{3,2},{4,5},{5,4},{6,7},{7,6},{8,9},{9,8},{10,11... | collective-permute-start | bytes 786440 | tf_op jit(solution)/shard_map/ppermute | solution.py:247
  16.7 12.9 %collective-permute-start.2 = (bf16[64,1024]{1,0:T(8,128)(2,1)S(1)}, bf16[64,1024]{1,0:T(8,128)(2,1)S(1)}, u32[]{:S(2)}, u32[]{:S(2)}) collective-permute-start(bf16[64,1024]{1,0:T(8,128)(2,1)S(1)} %slice_bitcast_fusion.refs_1_), channel_id=1, source_target_pairs={{0,1},{1,0},{2,3},{3,2},{4,5},{5,4},{6,7},{7,6},{8,9},{9,8},{10,11... | collective-permute-start | bytes 393224 | tf_op jit(solution)/shard_map/ppermute | solution.py:247
  17.1 12.5 %collective-permute-start.3 = (bf16[64,1024]{1,0:T(8,128)(2,1)S(1)}, bf16[64,1024]{1,0:T(8,128)(2,1)S(1)}, u32[]{:S(2)}, u32[]{:S(2)}) collective-permute-start(bf16[64,1024]{1,0:T(8,128)(2,1)S(1)} %slice_bitcast_fusion.refs_1_), channel_id=1, source_target_pairs={{0,3},{1,2},{2,1},{3,0},{4,7},{5,6},{6,5},{7,4},{8,11},{9,10},{10,... | collective-permute-start | bytes 393224 | tf_op jit(solution)/shard_map/ppermute | solution.py:247
  19.6 10.1 %collective-permute-start = (bf16[1,64,1024]{2,1,0:T(8,128)(2,1)S(1)}, bf16[1,64,1024]{2,1,0:T(8,128)(2,1)S(1)}, u32[]{:S(2)}, u32[]{:S(2)}) collective-permute-start(bf16[1,64,1024]{2,1,0:T(8,128)(2,1)S(1)} %bitcast.11), channel_id=1, source_target_pairs={{0,16},{4,20},{8,24},{12,28},{16,0},{20,4},{24,8},{28,12},{32,48},... | collective-permute-start | bytes 393224 | tf_op jit(solution)/shard_map/ppermute | solution.py:250
  22.5 7.2 %collective-permute-start.1 = (bf16[1,64,1024]{2,1,0:T(8,128)(2,1)S(1)}, bf16[1,64,1024]{2,1,0:T(8,128)(2,1)S(1)}, u32[]{:S(2)}, u32[]{:S(2)}) collective-permute-start(bf16[1,64,1024]{2,1,0:T(8,128)(2,1)S(1)} %bitcast.12), channel_id=1, source_target_pairs={{0,32},{4,36},{8,40},{12,44},{16,48},{20,52},{24,56},{28,60},{32,0... | collective-permute-start | bytes 393224 | tf_op jit(solution)/shard_map/ppermute | solution.py:250
  29.7 19.6 %copy-start.6 = (bf16[3,64,1024]{2,1,0:T(8,128)(2,1)}, bf16[3,64,1024]{2,1,0:T(8,128)(2,1)S(1)}, u32[]{:S(2)}) copy-start(bf16[3,64,1024]{2,1,0:T(8,128)(2,1)S(1)} %pad_maximum_fusion.1.refs_0_) | copy-start | bytes 1179652
  29.7 21.9 %collective-permute-start.8 = (bf16[3,64,1024]{2,1,0:T(8,128)(2,1)S(1)}, bf16[3,64,1024]{2,1,0:T(8,128)(2,1)S(1)}, u32[]{:S(2)}, u32[]{:S(2)}) collective-permute-start(bf16[3,64,1024]{2,1,0:T(8,128)(2,1)S(1)} %pad_maximum_fusion.1.refs_0_), channel_id=1, source_target_pairs={{0,8},{4,12},{8,0},{12,4},{16,24},{20,28},{24,16},{28,20},{32,40},... | collective-permute-start | bytes 1179656 | tf_op jit(solution)/shard_map/ppermute | solution.py:250
  30.5 15.3 %all-to-all-start.1 = ((bf16[32,16,128]{2,1,0:T(8,128)(2,1)}), bf16[32,16,128]{2,1,0:T(8,128)(2,1)S(1)}, u32[]{:S(2)}, u32[]{:S(2)}) async-start(bf16[32,16,128]{2,1,0:T(8,128)(2,1)} %get-tuple-element.35), calls=%async_computation.1 | async-start | bytes 262144 | tf_op jit(solution)/shard_map/all_to_all | solution.py:244
  36.4 5.4 %collective-permute-start.6 = (bf16[64,1024]{1,0:T(8,128)(2,1)S(1)}, bf16[64,1024]{1,0:T(8,128)(2,1)S(1)}, u32[]{:S(2)}, u32[]{:S(2)}) collective-permute-start(bf16[64,1024]{1,0:T(8,128)(2,1)S(1)} %slice_bitcast_fusion.refs_1_), channel_id=1, source_target_pairs={{0,2},{1,3},{2,0},{3,1},{4,6},{5,7},{6,4},{7,5},{8,10},{9,11},{10,... | collective-permute-start | bytes 393224 | tf_op jit(solution)/shard_map/ppermute | solution.py:247
  39.3 4.8 %collective-permute-start.5 = (bf16[1,64,1024]{2,1,0:T(8,128)(2,1)S(1)}, bf16[1,64,1024]{2,1,0:T(8,128)(2,1)S(1)}, u32[]{:S(2)}, u32[]{:S(2)}) collective-permute-start(bf16[1,64,1024]{2,1,0:T(8,128)(2,1)S(1)} %collective-permute-done), channel_id=1, source_target_pairs={{0,32},{4,36},{8,40},{12,44},{16,48},{20,52},{24,56},{28,60},{32,0... | collective-permute-start | bytes 393224 | tf_op jit(solution)/shard_map/ppermute | solution.py:250
  40.5 17.3 %collective-permute-start.9 = (bf16[4,64,1024]{2,1,0:T(8,128)(2,1)S(1)}, bf16[4,64,1024]{2,1,0:T(8,128)(2,1)S(1)}, u32[]{:S(2)}, u32[]{:S(2)}) collective-permute-start(bf16[4,64,1024]{2,1,0:T(8,128)(2,1)S(1)} %pad_maximum_fusion.near_ref.refs_0_), channel_id=1, source_target_pairs={{0,2},{1,3},{2,0},{3,1},{4,6},{5,7},{6,4},{7,5},{8,10},{9,11},{10,... | collective-permute-start | bytes 1572872 | tf_op jit(solution)/shard_map/ppermute | solution.py:247
  45.8 4.6 %collective-permute-start.7 = (bf16[32,16,128]{2,1,0:T(8,128)(2,1)S(1)}, bf16[32,16,128]{2,1,0:T(8,128)(2,1)S(1)}, u32[]{:S(2)}, u32[]{:S(2)}) collective-permute-start(bf16[32,16,128]{2,1,0:T(8,128)(2,1)S(1)} %all-to-all-done.1.gathered_ref), channel_id=1, source_target_pairs={{0,4},{4,0},{8,12},{12,8},{16,20},{20,16},{24,28},{28,24},{32,36},... | collective-permute-start | bytes 393224 | tf_op jit(solution)/shard_map/ppermute | solution.py:250
  49.3 9.6 %collective-permute-start.10 = (bf16[3,64,1024]{2,1,0:T(8,128)(2,1)S(1)}, bf16[3,64,1024]{2,1,0:T(8,128)(2,1)}, u32[]{:S(2)}, u32[]{:S(2)}) collective-permute-start(bf16[3,64,1024]{2,1,0:T(8,128)(2,1)S(1)} %pad_maximum_fusion.1.refs_0_), channel_id=1, source_target_pairs={{0,4},{4,0},{8,12},{12,8},{16,20},{20,16},{24,28},{28,24},{32,36},... | collective-permute-start | bytes 1179656 | tf_op jit(solution)/shard_map/ppermute | solution.py:250
  51.6 7.3 %copy-start.8 = (bf16[3,64,1024]{2,1,0:T(8,128)(2,1)}, bf16[3,64,1024]{2,1,0:T(8,128)(2,1)S(1)}, u32[]{:S(2)}) copy-start(bf16[3,64,1024]{2,1,0:T(8,128)(2,1)S(1)} %collective-permute-done.8.refs_1_) | copy-start | bytes 1179652
  51.6 7.3 %collective-permute-start.11 = (bf16[3,64,1024]{2,1,0:T(8,128)(2,1)S(1)}, bf16[3,64,1024]{2,1,0:T(8,128)(2,1)}, u32[]{:S(2)}, u32[]{:S(2)}) collective-permute-start(bf16[3,64,1024]{2,1,0:T(8,128)(2,1)S(1)} %collective-permute-done.8.refs_1_), channel_id=1, source_target_pairs={{0,4},{4,0},{8,12},{12,8},{16,20},{20,16},{24,28},{28,24},{32,36},... | collective-permute-start | bytes 1179656 | tf_op jit(solution)/shard_map/ppermute | solution.py:250
  52.0 13.0 %all-to-all-start.2 = ((bf16[32,16,128]{2,1,0:T(8,128)(2,1)}), bf16[32,16,128]{2,1,0:T(8,128)(2,1)S(1)}, u32[]{:S(2)}, u32[]{:S(2)}) async-start(bf16[32,16,128]{2,1,0:T(8,128)(2,1)} %get-tuple-element.47), calls=%async_computation.2 | async-start | bytes 262144 | tf_op jit(solution)/shard_map/all_to_all | solution.py:240
  56.4 13.9 %collective-permute-start.12 = (bf16[1,64,1024]{2,1,0:T(8,128)(2,1)S(1)}, bf16[1,64,1024]{2,1,0:T(8,128)(2,1)S(1)}, u32[]{:S(2)}, u32[]{:S(2)}) collective-permute-start(bf16[1,64,1024]{2,1,0:T(8,128)(2,1)S(1)} %collective-permute-done.5.refs_0_), channel_id=1, source_target_pairs={{0,8},{4,12},{8,0},{12,4},{16,24},{20,28},{24,16},{28,20},{32,40},... | collective-permute-start | bytes 393224 | tf_op jit(solution)/shard_map/ppermute | solution.py:250
  58.9 6.1 %copy-start.4 = (bf16[64,2048]{1,0:T(8,128)(2,1)S(1)}, bf16[64,2048]{1,0:T(8,128)(2,1)}, u32[]{:S(2)}) copy-start(bf16[64,2048]{1,0:T(8,128)(2,1)} %inverse_ref.3) | copy-start | bytes 786436
  66.0 12.6 %all-to-all-start.3 = ((bf16[32,16,128]{2,1,0:T(8,128)(2,1)}), bf16[32,16,128]{2,1,0:T(8,128)(2,1)S(1)}, u32[]{:S(2)}, u32[]{:S(2)}) async-start(bf16[32,16,128]{2,1,0:T(8,128)(2,1)} %get-tuple-element.52), calls=%async_computation.3 | async-start | bytes 262144 | tf_op jit(solution)/shard_map/all_to_all | solution.py:240
  69.9 1.4 %collective-permute-start.13 = (bf16[1,64,1024]{2,1,0:T(8,128)(2,1)S(1)}, bf16[1,64,1024]{2,1,0:T(8,128)(2,1)S(1)}, u32[]{:S(2)}, u32[]{:S(2)}) collective-permute-start(bf16[1,64,1024]{2,1,0:T(8,128)(2,1)S(1)} %collective-permute-done.5.refs_0_), channel_id=1, source_target_pairs={{0,4},{4,0},{8,12},{12,8},{16,20},{20,16},{24,28},{28,24},{32,36},... | collective-permute-start | bytes 393224 | tf_op jit(solution)/shard_map/ppermute | solution.py:250
  70.3 1.3 %collective-permute-start.14 = (bf16[1,64,1024]{2,1,0:T(8,128)(2,1)S(1)}, bf16[1,64,1024]{2,1,0:T(8,128)(2,1)S(1)}, u32[]{:S(2)}, u32[]{:S(2)}) collective-permute-start(bf16[1,64,1024]{2,1,0:T(8,128)(2,1)S(1)} %collective-permute-done.12.refs_1_), channel_id=1, source_target_pairs={{0,4},{4,0},{8,12},{12,8},{16,20},{20,16},{24,28},{28,24},{32,36},... | collective-permute-start | bytes 393224 | tf_op jit(solution)/shard_map/ppermute | solution.py:250
  72.0 11.9 %collective-permute-start.15 = (bf16[1,64,1024]{2,1,0:T(8,128)(2,1)S(1)}, bf16[1,64,1024]{2,1,0:T(8,128)(2,1)S(1)}, u32[]{:S(2)}, u32[]{:S(2)}) collective-permute-start(bf16[1,64,1024]{2,1,0:T(8,128)(2,1)S(1)} %corner.1.refs_0_), channel_id=1, source_target_pairs={{0,8},{4,12},{8,0},{12,4},{16,24},{20,28},{24,16},{28,20},{32,40},... | collective-permute-start | bytes 393224 | tf_op jit(solution)/shard_map/ppermute | solution.py:250
  73.5 10.7 %collective-permute-start.16 = (bf16[1,64,1024]{2,1,0:T(8,128)(2,1)S(1)}, bf16[1,64,1024]{2,1,0:T(8,128)(2,1)S(1)}, u32[]{:S(2)}, u32[]{:S(2)}) collective-permute-start(bf16[1,64,1024]{2,1,0:T(8,128)(2,1)S(1)} %corner.1.refs_0_), channel_id=1, source_target_pairs={{0,16},{4,20},{8,24},{12,28},{16,0},{20,4},{24,8},{28,12},{32,48},... | collective-permute-start | bytes 393224 | tf_op jit(solution)/shard_map/ppermute | solution.py:250
  75.9 8.8 %collective-permute-start.17 = (bf16[1,64,1024]{2,1,0:T(8,128)(2,1)S(1)}, bf16[1,64,1024]{2,1,0:T(8,128)(2,1)S(1)}, u32[]{:S(2)}, u32[]{:S(2)}) collective-permute-start(bf16[1,64,1024]{2,1,0:T(8,128)(2,1)S(1)} %corner.1.refs_0_), channel_id=1, source_target_pairs={{0,24},{4,28},{8,16},{12,20},{16,8},{20,12},{24,0},{28,4},{32,56},... | collective-permute-start | bytes 393224 | tf_op jit(solution)/shard_map/ppermute | solution.py:250
  79.8 10.0 %copy-start.5 = (bf16[64,512]{1,0:T(8,128)(2,1)S(1)}, bf16[64,512]{1,0:T(8,128)(2,1)}, u32[]{:S(2)}) copy-start(bf16[64,512]{1,0:T(8,128)(2,1)} %fourth_ref.1) | copy-start | bytes 196612
  79.8 10.0 %all-to-all-start.4 = ((bf16[16,32,128]{2,1,0:T(8,128)(2,1)}), bf16[16,32,128]{2,1,0:T(8,128)(2,1)S(1)}, u32[]{:S(2)}, u32[]{:S(2)}) async-start(bf16[16,32,128]{2,1,0:T(8,128)(2,1)} %update2.1), calls=%async_computation.4 | async-start | bytes 262144 | tf_op jit(solution)/shard_map/all_to_all | solution.py:240
  83.7 2.2 %collective-permute-start.18 = (bf16[1,64,1024]{2,1,0:T(8,128)(2,1)S(1)}, bf16[1,64,1024]{2,1,0:T(8,128)(2,1)S(1)}, u32[]{:S(2)}, u32[]{:S(2)}) collective-permute-start(bf16[1,64,1024]{2,1,0:T(8,128)(2,1)S(1)} %corner.1.refs_0_), channel_id=1, source_target_pairs={{0,4},{4,0},{8,12},{12,8},{16,20},{20,16},{24,28},{28,24},{32,36},... | collective-permute-start | bytes 393224 | tf_op jit(solution)/shard_map/ppermute | solution.py:250
  83.9 1.9 %collective-permute-start.19 = (bf16[1,64,1024]{2,1,0:T(8,128)(2,1)S(1)}, bf16[1,64,1024]{2,1,0:T(8,128)(2,1)S(1)}, u32[]{:S(2)}, u32[]{:S(2)}) collective-permute-start(bf16[1,64,1024]{2,1,0:T(8,128)(2,1)S(1)} %collective-permute-done.15.refs_1_), channel_id=1, source_target_pairs={{0,4},{4,0},{8,12},{12,8},{16,20},{20,16},{24,28},{28,24},{32,36},... | collective-permute-start | bytes 393224 | tf_op jit(solution)/shard_map/ppermute | solution.py:250
  84.2 1.7 %collective-permute-start.20 = (bf16[1,64,1024]{2,1,0:T(8,128)(2,1)S(1)}, bf16[1,64,1024]{2,1,0:T(8,128)(2,1)S(1)}, u32[]{:S(2)}, u32[]{:S(2)}) collective-permute-start(bf16[1,64,1024]{2,1,0:T(8,128)(2,1)S(1)} %collective-permute-done.16.refs_2_), channel_id=1, source_target_pairs={{0,4},{4,0},{8,12},{12,8},{16,20},{20,16},{24,28},{28,24},{32,36},... | collective-permute-start | bytes 393224 | tf_op jit(solution)/shard_map/ppermute | solution.py:250
  84.8 2.1 %collective-permute-start.21 = (bf16[1,64,1024]{2,1,0:T(8,128)(2,1)S(1)}, bf16[1,64,1024]{2,1,0:T(8,128)(2,1)S(1)}, u32[]{:S(2)}, u32[]{:S(2)}) collective-permute-start(bf16[1,64,1024]{2,1,0:T(8,128)(2,1)S(1)} %collective-permute-done.17.refs_3_), channel_id=1, source_target_pairs={{0,4},{4,0},{8,12},{12,8},{16,20},{20,16},{24,28},{28,24},{32,36},... | collective-permute-start | bytes 393224 | tf_op jit(solution)/shard_map/ppermute | solution.py:250

commit v8 on v7

--- a/solution.py
+++ b/solution.py
@@ -330,7 +330,7 @@
         *held(*third),
     )
     gathered = gather(copies)
-    gathered, coupled, partial = barrier((gathered, coupled, partial))
+    gathered, coupled, partial, corner = barrier((gathered, coupled, partial, corner))
     second_result, copies = call(
         solve_kernel,
         "solve1",

time: 91.7 us -> 93.2 us (1.016)
  waiting for transfers between devices: 22.9 us -> 25.4 us
  starting transfers between devices: 56.6 us -> 55.4 us
    all_to_all x4, waiting for transfers between devices: 14.5 us -> 18.2 us  [gather(): return lax.all_to_all(copies, 'sn', 0, 0, axis_index_groups=sets)]
    ppermute x17, starting transfers between devices: 18.1 us -> 15.6 us  [swap(): return lax.ppermute(part, 'sn', [(i, i ^ bit) for i in range(devices)])]
    all_to_all x4, starting transfers between devices: 25.3 us -> 26.6 us  [gather(): return lax.all_to_all(copies, 'sn', 0, 0, axis_index_groups=sets)]
    ppermute x17, waiting for transfers between devices: 5.74 us -> 4.52 us  [swap(): return lax.ppermute(part, 'sn', [(i, i ^ bit) for i in range(devices)])]
  transfers between devices with their start and end apart: 27 -> 27, of which waited for: 12 -> 12; matrix products, arithmetic and copies ran while one was open for 0% -> 0% of each run, Pallas kernels for 9% -> 7%
where the time goes in v8:
time: 93.2 us; the launch traced here: 92.6 us
  starting transfers between devices  55.4 us (59%)
  waiting for transfers between devices  25.4 us (27%)
  Pallas kernels  10 us (11%)
  local copies, waits for them, and re-layouts  1 us (1%)
    all_to_all x4, starting transfers between devices, gather(): return lax.all_to_all(copies, 'sn', 0, 0, axis_index_groups=sets)  26.6 us
    all_to_all x4, waiting for transfers between devices, gather(): return lax.all_to_all(copies, 'sn', 0, 0, axis_index_groups=sets)  18.2 us
    ppermute x17, starting transfers between devices, swap(): return lax.ppermute(part, 'sn', [(i, i ^ bit) for i in range(devices)])  15.6 us
    pallas_call x9, Pallas kernels, call(): pl.pallas_call(kernel, out_shape=outs, in_specs=[VMEM] * len(args), out_s...  10 us
    ppermute x5, starting transfers between devices, swap_group(): return lax.ppermute(part, 'rhs', [(i, i ^ bit) for i in range(groups)])  7.26 us
    all_to_all x1, starting transfers between devices, gather_core(): return lax.all_to_all(copies, 'sn', 0, 0, axis_index_groups=sets)  5.89 us
    ppermute x17, waiting for transfers between devices, swap(): return lax.ppermute(part, 'sn', [(i, i ^ bit) for i in range(devices)])  4.52 us
  transfers between devices with their start and end apart: 27, of which 12 were waited for; matrix products, arithmetic and copies ran while one was open for 0% of the time, Pallas kernels for 7%

profile of v8, /device:TPU:1, one launch (start us, length us, event | category | flops | bytes accessed | tf_op | source)
XLA Modules:
  0.0 92.6 jit_solution(8980242198161986307)
XLA Ops:
  0.1 0.7 copy-done
  0.9 0.1 squeeze.7
  0.9 0.1 iota_compare_fusion
  1.0 0.1 select_reduce_fusion
  1.1 0.1 reshape.100.index_ref
  1.2 0.2 select_reduce_fusion.1
  1.4 0.0 copy-start.7
  1.4 0.8 start.1
  2.2 13.2 %all-to-all-start = ((bf16[64,16,128]{2,1,0:T(8,128)(2,1)}), bf16[64,16,128]{2,1,0:T(8,128)(2,1)S(1)}, u32[]{:S(2)}, u32[]{:S(2)}) async-start(bf16[64,16,128]{2,1,0:T(8,128)(2,1)} %start.1), calls=%async_computation | async-start | bytes 524288 | tf_op jit(solution)/shard_map/all_to_all | solution.py:240
  15.4 0.0 copy-start.2
  15.4 0.0 copy-start.3
  15.4 1.3 %collective-permute-start.4 = (bf16[2,64,1024]{2,1,0:T(8,128)(2,1)S(1)}, bf16[2,64,1024]{2,1,0:T(8,128)(2,1)S(1)}, u32[]{:S(2)}, u32[]{:S(2)}) collective-permute-start(bf16[2,64,1024]{2,1,0:T(8,128)(2,1)S(1)} %slice.12), channel_id=1, source_target_pairs={{0,1},{1,0},{2,3},{3,2},{4,5},{5,4},{6,7},{7,6},{8,9},{9,8},{10,11... | collective-permute-start | bytes 786440 | tf_op jit(solution)/shard_map/ppermute | solution.py:247
  16.7 0.4 collective-permute-start.2
  17.1 2.5 %collective-permute-start.3 = (bf16[64,1024]{1,0:T(8,128)(2,1)S(1)}, bf16[64,1024]{1,0:T(8,128)(2,1)S(1)}, u32[]{:S(2)}, u32[]{:S(2)}) collective-permute-start(bf16[64,1024]{1,0:T(8,128)(2,1)S(1)} %slice_bitcast_fusion.refs_1_), channel_id=1, source_target_pairs={{0,3},{1,2},{2,1},{3,0},{4,7},{5,6},{6,5},{7,4},{8,11},{9,10},{10,... | collective-permute-start | bytes 393224 | tf_op jit(solution)/shard_map/ppermute | solution.py:247
  19.6 2.9 %collective-permute-start = (bf16[1,64,1024]{2,1,0:T(8,128)(2,1)S(1)}, bf16[1,64,1024]{2,1,0:T(8,128)(2,1)S(1)}, u32[]{:S(2)}, u32[]{:S(2)}) collective-permute-start(bf16[1,64,1024]{2,1,0:T(8,128)(2,1)S(1)} %bitcast.11), channel_id=1, source_target_pairs={{0,16},{4,20},{8,24},{12,28},{16,0},{20,4},{24,8},{28,12},{32,48},... | collective-permute-start | bytes 393224 | tf_op jit(solution)/shard_map/ppermute | solution.py:250
  22.5 1.2 %collective-permute-start.1 = (bf16[1,64,1024]{2,1,0:T(8,128)(2,1)S(1)}, bf16[1,64,1024]{2,1,0:T(8,128)(2,1)S(1)}, u32[]{:S(2)}, u32[]{:S(2)}) collective-permute-start(bf16[1,64,1024]{2,1,0:T(8,128)(2,1)S(1)} %bitcast.12), channel_id=1, source_target_pairs={{0,32},{4,36},{8,40},{12,44},{16,48},{20,52},{24,56},{28,60},{32,0... | collective-permute-start | bytes 393224 | tf_op jit(solution)/shard_map/ppermute | solution.py:250
  23.6 4.9 %all-to-all-done.gathered_ref = bf16[64,16,128]{2,1,0:T(8,128)(2,1)S(1)} async-done(((bf16[64,16,128]{2,1,0:T(8,128)(2,1)}), bf16[64,16,128]{2,1,0:T(8,128)(2,1)S(1)}, u32[]{:S(2)}, u32[]{:S(2)}) %all-to-all-start) | async-done | bytes 262176 | tf_op jit(solution)/shard_map/all_to_all | solution.py:240
  28.5 1.1 %solve0.1 = (f32[32,64]{1,0:T(8,128)S(1)}, bf16[32,16,128]{2,1,0:T(8,128)(2,1)}) custom-call(bf16[64,16,128]{2,1,0:T(8,128)(2,1)S(1)} %all-to-all-done.gathered_ref, bf16[64,4096]{1,0:T(8,128)(2,1)S(1)} %copy-done.2), custom_call_target="tpu_custom_call" | custom-call | flops 20000000 | bytes 1000000 | tf_op jit(solution)/shard_map/solve0/pallas_call | solution.py:202
  29.6 0.0 collective-permute-done.2.refs_2_
  29.6 0.0 collective-permute-done.3.refs_4_
  29.6 0.0 collective-permute-done
  29.7 0.8 collective-permute-start.8
  30.5 5.9 %all-to-all-start.1 = ((bf16[32,16,128]{2,1,0:T(8,128)(2,1)}), bf16[32,16,128]{2,1,0:T(8,128)(2,1)S(1)}, u32[]{:S(2)}, u32[]{:S(2)}) async-start(bf16[32,16,128]{2,1,0:T(8,128)(2,1)} %get-tuple-element.39), calls=%async_computation.1 | async-start | bytes 262144 | tf_op jit(solution)/shard_map/all_to_all | solution.py:244
  36.4 2.8 %collective-permute-start.6 = (bf16[64,1024]{1,0:T(8,128)(2,1)S(1)}, bf16[64,1024]{1,0:T(8,128)(2,1)S(1)}, u32[]{:S(2)}, u32[]{:S(2)}) collective-permute-start(bf16[64,1024]{1,0:T(8,128)(2,1)S(1)} %slice_bitcast_fusion.refs_1_), channel_id=1, source_target_pairs={{0,2},{1,3},{2,0},{3,1},{4,6},{5,7},{6,4},{7,5},{8,10},{9,11},{10,... | collective-permute-start | bytes 393224 | tf_op jit(solution)/shard_map/ppermute | solution.py:247
  39.3 1.2 %collective-permute-start.5 = (bf16[1,64,1024]{2,1,0:T(8,128)(2,1)S(1)}, bf16[1,64,1024]{2,1,0:T(8,128)(2,1)S(1)}, u32[]{:S(2)}, u32[]{:S(2)}) collective-permute-start(bf16[1,64,1024]{2,1,0:T(8,128)(2,1)S(1)} %collective-permute-done), channel_id=1, source_target_pairs={{0,32},{4,36},{8,40},{12,44},{16,48},{20,52},{24,56},{28,60},{32,0... | collective-permute-start | bytes 393224 | tf_op jit(solution)/shard_map/ppermute | solution.py:250
  40.5 0.3 collective-permute-start.9
  40.9 1.0 %collective-permute-done.6.refs_3_ = bf16[64,1024]{1,0:T(8,128)(2,1)S(1)} collective-permute-done((bf16[64,1024]{1,0:T(8,128)(2,1)S(1)}, bf16[64,1024]{1,0:T(8,128)(2,1)S(1)}, u32[]{:S(2)}, u32[]{:S(2)}) %collective-permute-start.6) | collective-permute-done | bytes 131104 | tf_op jit(solution)/shard_map/ppermute | solution.py:247
  41.8 2.3 %collective-permute-done.5.refs_0_ = bf16[1,64,1024]{2,1,0:T(8,128)(2,1)S(1)} collective-permute-done((bf16[1,64,1024]{2,1,0:T(8,128)(2,1)S(1)}, bf16[1,64,1024]{2,1,0:T(8,128)(2,1)S(1)}, u32[]{:S(2)}, u32[]{:S(2)}) %collective-permute-start.5) | collective-permute-done | bytes 131104 | tf_op jit(solution)/shard_map/ppermute | solution.py:250
  44.1 1.7 %all-to-all-done.1.gathered_ref = bf16[32,16,128]{2,1,0:T(8,128)(2,1)S(1)} async-done(((bf16[32,16,128]{2,1,0:T(8,128)(2,1)}), bf16[32,16,128]{2,1,0:T(8,128)(2,1)S(1)}, u32[]{:S(2)}, u32[]{:S(2)}) %all-to-all-start.1) | async-done | bytes 131104 | tf_op jit(solution)/shard_map/all_to_all | solution.py:244
  45.8 3.5 %collective-permute-start.7 = (bf16[32,16,128]{2,1,0:T(8,128)(2,1)S(1)}, bf16[32,16,128]{2,1,0:T(8,128)(2,1)S(1)}, u32[]{:S(2)}, u32[]{:S(2)}) collective-permute-start(bf16[32,16,128]{2,1,0:T(8,128)(2,1)S(1)} %all-to-all-done.1.gathered_ref), channel_id=1, source_target_pairs={{0,4},{4,0},{8,12},{12,8},{16,20},{20,16},{24,28},{28,24},{32,36},... | collective-permute-start | bytes 393224 | tf_op jit(solution)/shard_map/ppermute | solution.py:250
  49.3 0.0 collective-permute-start.10
  49.4 1.1 %collective-permute-done.7.refs_0_ = bf16[32,16,128]{2,1,0:T(8,128)(2,1)S(1)} collective-permute-done((bf16[32,16,128]{2,1,0:T(8,128)(2,1)S(1)}, bf16[32,16,128]{2,1,0:T(8,128)(2,1)S(1)}, u32[]{:S(2)}, u32[]{:S(2)}) %collective-permute-start.7) | collective-permute-done | bytes 131104 | tf_op jit(solution)/shard_map/ppermute | solution.py:250
  50.4 1.2 %update1.1 = (bf16[32,16,128]{2,1,0:T(8,128)(2,1)}, bf16[32,32,128]{2,1,0:T(8,128)(2,1)S(1)}) custom-call(s32[3,32]{1,0:T(4,128)S(1)} %reshape.100.index_ref, bf16[32,16,128]{2,1,0:T(8,128)(2,1)S(1)} %all-to-all-done.1.gathered_ref, f32[4,32,64]{2,1,0:T(8,128)S(1)} %bitcast.9, bf16[32,16,128]{2,1,0:T(8,128)(2,1)S(1)} %collective-permute-done.7.refs_0_, ...), custom_call_target="tpu_custom_call" | custom-call | flops 20000 | bytes 1000 | tf_op jit(solution)/shard_map/update1/pallas_call | solution.py:202
  51.7 0.0 collective-permute-done.8.refs_1_
  51.7 0.4 collective-permute-start.11
  52.0 5.6 %all-to-all-start.2 = ((bf16[32,16,128]{2,1,0:T(8,128)(2,1)}), bf16[32,16,128]{2,1,0:T(8,128)(2,1)S(1)}, u32[]{:S(2)}, u32[]{:S(2)}) async-start(bf16[32,16,128]{2,1,0:T(8,128)(2,1)} %get-tuple-element.51), calls=%async_computation.2 | async-start | bytes 262144 | tf_op jit(solution)/shard_map/all_to_all | solution.py:240
  57.6 0.3 collective-permute-start.13
  57.9 0.0 collective-permute-done.12.refs_1_
  57.9 0.3 collective-permute-start.14
  58.2 1.0 %select.40.coupled_ref = bf16[1,64,1024]{2,1,0:T(8,128)(2,1)S(1)} custom-call(s32[1,8]{1,0:T(1,128)S(1)} %bitcast.14, bf16[4,64,1024]{2,1,0:T(8,128)(2,1)S(1)} %pad_maximum_fusion.near_ref.refs_0_, bf16[4,64,1024]{2,1,0:T(8,128)(2,1)S(1)} %collective-permute-done.9.far_ref.refs_1_), custom_call_target="tpu_custom_call" | custom-call | flops 20000000 | bytes 1000000 | tf_op jit(solution)/shard_map/select/pallas_call | solution.py:202
  59.2 0.0 copy-start.4
  59.2 0.0 collective-permute-done.10.refs_2_
  59.2 1.9 %product.1.refs_4_ = f32[1,64,1024]{2,1,0:T(8,128)S(1)} custom-call(bf16[1,64,1024]{2,1,0:T(8,128)(2,1)S(1)} %select.40.coupled_ref, bf16[3,64,1024]{2,1,0:T(8,128)(2,1)} %copy-done.6, bf16[3,64,1024]{2,1,0:T(8,128)(2,1)} %collective-permute-done.8.refs_1_, bf16[3,64,1024]{2,1,0:T(8,128)(2,1)} %collective-permute-done.10.refs_2_, ...), custom_call_target="tpu_custom_call" | custom-call | flops 20000000 | bytes 1000000 | tf_op jit(solution)/shard_map/product/pallas_call | solution.py:202
  61.2 0.0 collective-permute-done.13.refs_2_
  61.2 5.0 %all-to-all-done.2.gathered_ref = bf16[32,16,128]{2,1,0:T(8,128)(2,1)S(1)} async-done(((bf16[32,16,128]{2,1,0:T(8,128)(2,1)}), bf16[32,16,128]{2,1,0:T(8,128)(2,1)S(1)}, u32[]{:S(2)}, u32[]{:S(2)}) %all-to-all-start.2) | async-done | bytes 131104 | tf_op jit(solution)/shard_map/all_to_all | solution.py:240
  66.2 1.0 %solve1.1 = (f32[32,64]{1,0:T(8,128)S(1)}, bf16[32,16,128]{2,1,0:T(8,128)(2,1)}) custom-call(bf16[32,16,128]{2,1,0:T(8,128)(2,1)S(1)} %all-to-all-done.2.gathered_ref, bf16[64,2048]{1,0:T(8,128)(2,1)S(1)} %copy-done.4), custom_call_target="tpu_custom_call" | custom-call | flops 20000000 | bytes 1000000 | tf_op jit(solution)/shard_map/solve1/pallas_call | solution.py:202
  67.2 4.1 %all-to-all-start.3 = ((bf16[32,16,128]{2,1,0:T(8,128)(2,1)}), bf16[32,16,128]{2,1,0:T(8,128)(2,1)S(1)}, u32[]{:S(2)}, u32[]{:S(2)}) async-start(bf16[32,16,128]{2,1,0:T(8,128)(2,1)} %get-tuple-element.57), calls=%async_computation.3 | async-start | bytes 262144 | tf_op jit(solution)/shard_map/all_to_all | solution.py:240
  71.2 0.4 corner.1.refs_0_
  71.6 1.5 %collective-permute-start.15 = (bf16[1,64,1024]{2,1,0:T(8,128)(2,1)S(1)}, bf16[1,64,1024]{2,1,0:T(8,128)(2,1)S(1)}, u32[]{:S(2)}, u32[]{:S(2)}) collective-permute-start(bf16[1,64,1024]{2,1,0:T(8,128)(2,1)S(1)} %corner.1.refs_0_), channel_id=1, source_target_pairs={{0,8},{4,12},{8,0},{12,4},{16,24},{20,28},{24,16},{28,20},{32,40},... | collective-permute-start | bytes 393224 | tf_op jit(solution)/shard_map/ppermute | solution.py:250
  73.1 2.4 %collective-permute-start.16 = (bf16[1,64,1024]{2,1,0:T(8,128)(2,1)S(1)}, bf16[1,64,1024]{2,1,0:T(8,128)(2,1)S(1)}, u32[]{:S(2)}, u32[]{:S(2)}) collective-permute-start(bf16[1,64,1024]{2,1,0:T(8,128)(2,1)S(1)} %corner.1.refs_0_), channel_id=1, source_target_pairs={{0,16},{4,20},{8,24},{12,28},{16,0},{20,4},{24,8},{28,12},{32,48},... | collective-permute-start | bytes 393224 | tf_op jit(solution)/shard_map/ppermute | solution.py:250
  75.5 0.1 collective-permute-start.17
  75.6 4.3 %all-to-all-done.3.gathered_ref = bf16[32,16,128]{2,1,0:T(8,128)(2,1)S(1)} async-done(((bf16[32,16,128]{2,1,0:T(8,128)(2,1)}), bf16[32,16,128]{2,1,0:T(8,128)(2,1)S(1)}, u32[]{:S(2)}, u32[]{:S(2)}) %all-to-all-start.3) | async-done | bytes 131104 | tf_op jit(solution)/shard_map/all_to_all | solution.py:240
  79.9 1.3 %update2.1 = bf16[16,32,128]{2,1,0:T(8,128)(2,1)} custom-call(s32[3,32]{1,0:T(4,128)S(1)} %reshape.100.index_ref, bf16[32,16,128]{2,1,0:T(8,128)(2,1)S(1)} %all-to-all-done.3.gathered_ref, f32[4,32,64]{2,1,0:T(8,128)S(1)} %bitcast.10, bf16[4,64,1024]{2,1,0:T(8,128)(2,1)S(1)} %pad_maximum_fusion.near_ref.refs_0_, ...), custom_call_target="tpu_custom_call" | custom-call | flops 20000000 | bytes 1000000 | tf_op jit(solution)/shard_map/update2/pallas_call | solution.py:202
  81.2 3.9 %all-to-all-start.4 = ((bf16[16,32,128]{2,1,0:T(8,128)(2,1)}), bf16[16,32,128]{2,1,0:T(8,128)(2,1)S(1)}, u32[]{:S(2)}, u32[]{:S(2)}) async-start(bf16[16,32,128]{2,1,0:T(8,128)(2,1)} %update2.1), calls=%async_computation.4 | async-start | bytes 262144 | tf_op jit(solution)/shard_map/all_to_all | solution.py:240
  85.0 0.3 collective-permute-start.18
  85.3 0.2 collective-permute-start.19
  85.6 0.3 collective-permute-start.20
  85.9 0.2 collective-permute-start.21
  86.1 0.3 collective-permute-done.18.refs_4_
  86.4 0.3 collective-permute-done.19.refs_5_
  86.7 0.2 collective-permute-done.20.refs_6_
  86.9 0.3 collective-permute-done.21.refs_7_
  87.2 4.0 %all-to-all-done.4.gathered_ref = bf16[16,32,128]{2,1,0:T(8,128)(2,1)S(1)} async-done(((bf16[16,32,128]{2,1,0:T(8,128)(2,1)}), bf16[16,32,128]{2,1,0:T(8,128)(2,1)S(1)}, u32[]{:S(2)}, u32[]{:S(2)}) %all-to-all-start.4) | async-done | bytes 131104 | tf_op jit(solution)/shard_map/all_to_all | solution.py:240
  91.3 1.4 %final.1 = f32[4,32,64]{2,1,0:T(8,128)} custom-call(bf16[16,32,128]{2,1,0:T(8,128)(2,1)S(1)} %all-to-all-done.4.gathered_ref, bf16[64,1024]{1,0:T(8,128)(2,1)S(1)} %copy-done.3, bf16[64,512]{1,0:T(8,128)(2,1)S(1)} %copy-done.5, f32[32,64]{1,0:T(8,128)S(1)} %get-tuple-element.59.first_result_ref, f32[32,64]{1,0:T(8,128)S(1)} %get-tuple-element.60.second_result_ref, ...), custom_call_target="tpu_custom_call" | custom-call | flops 20000000 | bytes 1000000 | tf_op jit(solution)/shard_map/final/pallas_call | solution.py:202
  (30 shorter events, 0.2 us)
Async XLA Ops:
  0.0 0.8 copy-start
  0.0 1.4 %copy-start.1 = (f32[4,64,32]{1,2,0:T(8,128)S(1)}, f32[4,64,32]{1,2,0:T(8,128)}, u32[]{:S(2)}) copy-start(f32[4,64,32]{1,2,0:T(8,128)} %param.7) | copy-start | bytes 98308
  1.4 14.0 %copy-start.7 = (bf16[3,64,1024]{2,1,0:T(8,128)(2,1)S(1)}, bf16[3,64,1024]{2,1,0:T(8,128)(2,1)}, u32[]{:S(2)}) copy-start(bf16[3,64,1024]{2,1,0:T(8,128)(2,1)} %param.8) | copy-start | bytes 1179652
  2.2 26.3 %all-to-all-start = ((bf16[64,16,128]{2,1,0:T(8,128)(2,1)}), bf16[64,16,128]{2,1,0:T(8,128)(2,1)S(1)}, u32[]{:S(2)}, u32[]{:S(2)}) async-start(bf16[64,16,128]{2,1,0:T(8,128)(2,1)} %start.1), calls=%async_computation | async-start | bytes 524288 | tf_op jit(solution)/shard_map/all_to_all | solution.py:240
  15.4 13.2 %copy-start.2 = (bf16[64,4096]{1,0:T(8,128)(2,1)S(1)}, bf16[64,4096]{1,0:T(8,128)(2,1)}, u32[]{:S(2)}) copy-start(bf16[64,4096]{1,0:T(8,128)(2,1)} %inverse_ref.2) | copy-start | bytes 1572868
  15.4 4.1 %copy-start.3 = (bf16[64,1024]{1,0:T(8,128)(2,1)S(1)}, bf16[64,1024]{1,0:T(8,128)(2,1)}, u32[]{:S(2)}) copy-start(bf16[64,1024]{1,0:T(8,128)(2,1)} %third_ref.1) | copy-start | bytes 393220
  15.4 14.2 %collective-permute-start.4 = (bf16[2,64,1024]{2,1,0:T(8,128)(2,1)S(1)}, bf16[2,64,1024]{2,1,0:T(8,128)(2,1)S(1)}, u32[]{:S(2)}, u32[]{:S(2)}) collective-permute-start(bf16[2,64,1024]{2,1,0:T(8,128)(2,1)S(1)} %slice.12), channel_id=1, source_target_pairs={{0,1},{1,0},{2,3},{3,2},{4,5},{5,4},{6,7},{7,6},{8,9},{9,8},{10,11... | collective-permute-start | bytes 786440 | tf_op jit(solution)/shard_map/ppermute | solution.py:247
  16.7 12.9 %collective-permute-start.2 = (bf16[64,1024]{1,0:T(8,128)(2,1)S(1)}, bf16[64,1024]{1,0:T(8,128)(2,1)S(1)}, u32[]{:S(2)}, u32[]{:S(2)}) collective-permute-start(bf16[64,1024]{1,0:T(8,128)(2,1)S(1)} %slice_bitcast_fusion.refs_1_), channel_id=1, source_target_pairs={{0,1},{1,0},{2,3},{3,2},{4,5},{5,4},{6,7},{7,6},{8,9},{9,8},{10,11... | collective-permute-start | bytes 393224 | tf_op jit(solution)/shard_map/ppermute | solution.py:247
  17.1 12.5 %collective-permute-start.3 = (bf16[64,1024]{1,0:T(8,128)(2,1)S(1)}, bf16[64,1024]{1,0:T(8,128)(2,1)S(1)}, u32[]{:S(2)}, u32[]{:S(2)}) collective-permute-start(bf16[64,1024]{1,0:T(8,128)(2,1)S(1)} %slice_bitcast_fusion.refs_1_), channel_id=1, source_target_pairs={{0,3},{1,2},{2,1},{3,0},{4,7},{5,6},{6,5},{7,4},{8,11},{9,10},{10,... | collective-permute-start | bytes 393224 | tf_op jit(solution)/shard_map/ppermute | solution.py:247
  19.6 10.1 %collective-permute-start = (bf16[1,64,1024]{2,1,0:T(8,128)(2,1)S(1)}, bf16[1,64,1024]{2,1,0:T(8,128)(2,1)S(1)}, u32[]{:S(2)}, u32[]{:S(2)}) collective-permute-start(bf16[1,64,1024]{2,1,0:T(8,128)(2,1)S(1)} %bitcast.11), channel_id=1, source_target_pairs={{0,16},{4,20},{8,24},{12,28},{16,0},{20,4},{24,8},{28,12},{32,48},... | collective-permute-start | bytes 393224 | tf_op jit(solution)/shard_map/ppermute | solution.py:250
  22.5 7.2 %collective-permute-start.1 = (bf16[1,64,1024]{2,1,0:T(8,128)(2,1)S(1)}, bf16[1,64,1024]{2,1,0:T(8,128)(2,1)S(1)}, u32[]{:S(2)}, u32[]{:S(2)}) collective-permute-start(bf16[1,64,1024]{2,1,0:T(8,128)(2,1)S(1)} %bitcast.12), channel_id=1, source_target_pairs={{0,32},{4,36},{8,40},{12,44},{16,48},{20,52},{24,56},{28,60},{32,0... | collective-permute-start | bytes 393224 | tf_op jit(solution)/shard_map/ppermute | solution.py:250
  29.7 19.6 %copy-start.6 = (bf16[3,64,1024]{2,1,0:T(8,128)(2,1)}, bf16[3,64,1024]{2,1,0:T(8,128)(2,1)S(1)}, u32[]{:S(2)}) copy-start(bf16[3,64,1024]{2,1,0:T(8,128)(2,1)S(1)} %pad_maximum_fusion.1.refs_0_) | copy-start | bytes 1179652
  29.7 21.9 %collective-permute-start.8 = (bf16[3,64,1024]{2,1,0:T(8,128)(2,1)S(1)}, bf16[3,64,1024]{2,1,0:T(8,128)(2,1)}, u32[]{:S(2)}, u32[]{:S(2)}) collective-permute-start(bf16[3,64,1024]{2,1,0:T(8,128)(2,1)S(1)} %pad_maximum_fusion.1.refs_0_), channel_id=1, source_target_pairs={{0,8},{4,12},{8,0},{12,4},{16,24},{20,28},{24,16},{28,20},{32,40},... | collective-permute-start | bytes 1179656 | tf_op jit(solution)/shard_map/ppermute | solution.py:250
  30.5 15.3 %all-to-all-start.1 = ((bf16[32,16,128]{2,1,0:T(8,128)(2,1)}), bf16[32,16,128]{2,1,0:T(8,128)(2,1)S(1)}, u32[]{:S(2)}, u32[]{:S(2)}) async-start(bf16[32,16,128]{2,1,0:T(8,128)(2,1)} %get-tuple-element.39), calls=%async_computation.1 | async-start | bytes 262144 | tf_op jit(solution)/shard_map/all_to_all | solution.py:244
  36.4 5.4 %collective-permute-start.6 = (bf16[64,1024]{1,0:T(8,128)(2,1)S(1)}, bf16[64,1024]{1,0:T(8,128)(2,1)S(1)}, u32[]{:S(2)}, u32[]{:S(2)}) collective-permute-start(bf16[64,1024]{1,0:T(8,128)(2,1)S(1)} %slice_bitcast_fusion.refs_1_), channel_id=1, source_target_pairs={{0,2},{1,3},{2,0},{3,1},{4,6},{5,7},{6,4},{7,5},{8,10},{9,11},{10,... | collective-permute-start | bytes 393224 | tf_op jit(solution)/shard_map/ppermute | solution.py:247
  39.3 4.8 %collective-permute-start.5 = (bf16[1,64,1024]{2,1,0:T(8,128)(2,1)S(1)}, bf16[1,64,1024]{2,1,0:T(8,128)(2,1)S(1)}, u32[]{:S(2)}, u32[]{:S(2)}) collective-permute-start(bf16[1,64,1024]{2,1,0:T(8,128)(2,1)S(1)} %collective-permute-done), channel_id=1, source_target_pairs={{0,32},{4,36},{8,40},{12,44},{16,48},{20,52},{24,56},{28,60},{32,0... | collective-permute-start | bytes 393224 | tf_op jit(solution)/shard_map/ppermute | solution.py:250
  40.5 17.7 %collective-permute-start.9 = (bf16[4,64,1024]{2,1,0:T(8,128)(2,1)S(1)}, bf16[4,64,1024]{2,1,0:T(8,128)(2,1)S(1)}, u32[]{:S(2)}, u32[]{:S(2)}) collective-permute-start(bf16[4,64,1024]{2,1,0:T(8,128)(2,1)S(1)} %pad_maximum_fusion.near_ref.refs_0_), channel_id=1, source_target_pairs={{0,2},{1,3},{2,0},{3,1},{4,6},{5,7},{6,4},{7,5},{8,10},{9,11},{10,... | collective-permute-start | bytes 1572872 | tf_op jit(solution)/shard_map/ppermute | solution.py:247
  45.8 4.6 %collective-permute-start.7 = (bf16[32,16,128]{2,1,0:T(8,128)(2,1)S(1)}, bf16[32,16,128]{2,1,0:T(8,128)(2,1)S(1)}, u32[]{:S(2)}, u32[]{:S(2)}) collective-permute-start(bf16[32,16,128]{2,1,0:T(8,128)(2,1)S(1)} %all-to-all-done.1.gathered_ref), channel_id=1, source_target_pairs={{0,4},{4,0},{8,12},{12,8},{16,20},{20,16},{24,28},{28,24},{32,36},... | collective-permute-start | bytes 393224 | tf_op jit(solution)/shard_map/ppermute | solution.py:250
  49.3 9.9 %collective-permute-start.10 = (bf16[3,64,1024]{2,1,0:T(8,128)(2,1)S(1)}, bf16[3,64,1024]{2,1,0:T(8,128)(2,1)}, u32[]{:S(2)}, u32[]{:S(2)}) collective-permute-start(bf16[3,64,1024]{2,1,0:T(8,128)(2,1)S(1)} %pad_maximum_fusion.1.refs_0_), channel_id=1, source_target_pairs={{0,4},{4,0},{8,12},{12,8},{16,20},{20,16},{24,28},{28,24},{32,36},... | collective-permute-start | bytes 1179656 | tf_op jit(solution)/shard_map/ppermute | solution.py:250
  51.7 7.6 %collective-permute-start.11 = (bf16[3,64,1024]{2,1,0:T(8,128)(2,1)}, bf16[3,64,1024]{2,1,0:T(8,128)(2,1)}, u32[]{:S(2)}, u32[]{:S(2)}) collective-permute-start(bf16[3,64,1024]{2,1,0:T(8,128)(2,1)} %collective-permute-done.8.refs_1_), channel_id=1, source_target_pairs={{0,4},{4,0},{8,12},{12,8},{16,20},{20,16},{24,28},{28,24},{32,36},... | collective-permute-start | bytes 1179656 | tf_op jit(solution)/shard_map/ppermute | solution.py:250
  52.0 5.9 %collective-permute-start.12 = (bf16[1,64,1024]{2,1,0:T(8,128)(2,1)S(1)}, bf16[1,64,1024]{2,1,0:T(8,128)(2,1)S(1)}, u32[]{:S(2)}, u32[]{:S(2)}) collective-permute-start(bf16[1,64,1024]{2,1,0:T(8,128)(2,1)S(1)} %collective-permute-done.5.refs_0_), channel_id=1, source_target_pairs={{0,8},{4,12},{8,0},{12,4},{16,24},{20,28},{24,16},{28,20},{32,40},... | collective-permute-start | bytes 393224 | tf_op jit(solution)/shard_map/ppermute | solution.py:250
  52.0 14.1 %all-to-all-start.2 = ((bf16[32,16,128]{2,1,0:T(8,128)(2,1)}), bf16[32,16,128]{2,1,0:T(8,128)(2,1)S(1)}, u32[]{:S(2)}, u32[]{:S(2)}) async-start(bf16[32,16,128]{2,1,0:T(8,128)(2,1)} %get-tuple-element.51), calls=%async_computation.2 | async-start | bytes 262144 | tf_op jit(solution)/shard_map/all_to_all | solution.py:240
  57.6 3.6 %collective-permute-start.13 = (bf16[1,64,1024]{2,1,0:T(8,128)(2,1)S(1)}, bf16[1,64,1024]{2,1,0:T(8,128)(2,1)S(1)}, u32[]{:S(2)}, u32[]{:S(2)}) collective-permute-start(bf16[1,64,1024]{2,1,0:T(8,128)(2,1)S(1)} %collective-permute-done.5.refs_0_), channel_id=1, source_target_pairs={{0,4},{4,0},{8,12},{12,8},{16,20},{20,16},{24,28},{28,24},{32,36},... | collective-permute-start | bytes 393224 | tf_op jit(solution)/shard_map/ppermute | solution.py:250
  57.9 8.2 %collective-permute-start.14 = (bf16[1,64,1024]{2,1,0:T(8,128)(2,1)S(1)}, bf16[1,64,1024]{2,1,0:T(8,128)(2,1)S(1)}, u32[]{:S(2)}, u32[]{:S(2)}) collective-permute-start(bf16[1,64,1024]{2,1,0:T(8,128)(2,1)S(1)} %collective-permute-done.12.refs_1_), channel_id=1, source_target_pairs={{0,4},{4,0},{8,12},{12,8},{16,20},{20,16},{24,28},{28,24},{32,36},... | collective-permute-start | bytes 393224 | tf_op jit(solution)/shard_map/ppermute | solution.py:250
  59.2 6.9 %copy-start.4 = (bf16[64,2048]{1,0:T(8,128)(2,1)S(1)}, bf16[64,2048]{1,0:T(8,128)(2,1)}, u32[]{:S(2)}) copy-start(bf16[64,2048]{1,0:T(8,128)(2,1)} %inverse_ref.3) | copy-start | bytes 786436
  67.2 12.8 %all-to-all-start.3 = ((bf16[32,16,128]{2,1,0:T(8,128)(2,1)}), bf16[32,16,128]{2,1,0:T(8,128)(2,1)S(1)}, u32[]{:S(2)}, u32[]{:S(2)}) async-start(bf16[32,16,128]{2,1,0:T(8,128)(2,1)} %get-tuple-element.57), calls=%async_computation.3 | async-start | bytes 262144 | tf_op jit(solution)/shard_map/all_to_all | solution.py:240
  71.6 13.7 %collective-permute-start.15 = (bf16[1,64,1024]{2,1,0:T(8,128)(2,1)S(1)}, bf16[1,64,1024]{2,1,0:T(8,128)(2,1)S(1)}, u32[]{:S(2)}, u32[]{:S(2)}) collective-permute-start(bf16[1,64,1024]{2,1,0:T(8,128)(2,1)S(1)} %corner.1.refs_0_), channel_id=1, source_target_pairs={{0,8},{4,12},{8,0},{12,4},{16,24},{20,28},{24,16},{28,20},{32,40},... | collective-permute-start | bytes 393224 | tf_op jit(solution)/shard_map/ppermute | solution.py:250
  73.1 12.5 %collective-permute-start.16 = (bf16[1,64,1024]{2,1,0:T(8,128)(2,1)S(1)}, bf16[1,64,1024]{2,1,0:T(8,128)(2,1)S(1)}, u32[]{:S(2)}, u32[]{:S(2)}) collective-permute-start(bf16[1,64,1024]{2,1,0:T(8,128)(2,1)S(1)} %corner.1.refs_0_), channel_id=1, source_target_pairs={{0,16},{4,20},{8,24},{12,28},{16,0},{20,4},{24,8},{28,12},{32,48},... | collective-permute-start | bytes 393224 | tf_op jit(solution)/shard_map/ppermute | solution.py:250
  75.5 10.4 %collective-permute-start.17 = (bf16[1,64,1024]{2,1,0:T(8,128)(2,1)S(1)}, bf16[1,64,1024]{2,1,0:T(8,128)(2,1)S(1)}, u32[]{:S(2)}, u32[]{:S(2)}) collective-permute-start(bf16[1,64,1024]{2,1,0:T(8,128)(2,1)S(1)} %corner.1.refs_0_), channel_id=1, source_target_pairs={{0,24},{4,28},{8,16},{12,20},{16,8},{20,12},{24,0},{28,4},{32,56},... | collective-permute-start | bytes 393224 | tf_op jit(solution)/shard_map/ppermute | solution.py:250
  81.2 10.1 %copy-start.5 = (bf16[64,512]{1,0:T(8,128)(2,1)S(1)}, bf16[64,512]{1,0:T(8,128)(2,1)}, u32[]{:S(2)}) copy-start(bf16[64,512]{1,0:T(8,128)(2,1)} %fourth_ref.1) | copy-start | bytes 196612
  81.2 10.1 %all-to-all-start.4 = ((bf16[16,32,128]{2,1,0:T(8,128)(2,1)}), bf16[16,32,128]{2,1,0:T(8,128)(2,1)S(1)}, u32[]{:S(2)}, u32[]{:S(2)}) async-start(bf16[16,32,128]{2,1,0:T(8,128)(2,1)} %update2.1), calls=%async_computation.4 | async-start | bytes 262144 | tf_op jit(solution)/shard_map/all_to_all | solution.py:240
  85.0 1.4 %collective-permute-start.18 = (bf16[1,64,1024]{2,1,0:T(8,128)(2,1)S(1)}, bf16[1,64,1024]{2,1,0:T(8,128)(2,1)S(1)}, u32[]{:S(2)}, u32[]{:S(2)}) collective-permute-start(bf16[1,64,1024]{2,1,0:T(8,128)(2,1)S(1)} %corner.1.refs_0_), channel_id=1, source_target_pairs={{0,4},{4,0},{8,12},{12,8},{16,20},{20,16},{24,28},{28,24},{32,36},... | collective-permute-start | bytes 393224 | tf_op jit(solution)/shard_map/ppermute | solution.py:250
  85.3 1.3 %collective-permute-start.19 = (bf16[1,64,1024]{2,1,0:T(8,128)(2,1)S(1)}, bf16[1,64,1024]{2,1,0:T(8,128)(2,1)S(1)}, u32[]{:S(2)}, u32[]{:S(2)}) collective-permute-start(bf16[1,64,1024]{2,1,0:T(8,128)(2,1)S(1)} %collective-permute-done.15.refs_1_), channel_id=1, source_target_pairs={{0,4},{4,0},{8,12},{12,8},{16,20},{20,16},{24,28},{28,24},{32,36},... | collective-permute-start | bytes 393224 | tf_op jit(solution)/shard_map/ppermute | solution.py:250
  85.6 1.3 %collective-permute-start.20 = (bf16[1,64,1024]{2,1,0:T(8,128)(2,1)S(1)}, bf16[1,64,1024]{2,1,0:T(8,128)(2,1)S(1)}, u32[]{:S(2)}, u32[]{:S(2)}) collective-permute-start(bf16[1,64,1024]{2,1,0:T(8,128)(2,1)S(1)} %collective-permute-done.16.refs_2_), channel_id=1, source_target_pairs={{0,4},{4,0},{8,12},{12,8},{16,20},{20,16},{24,28},{28,24},{32,36},... | collective-permute-start | bytes 393224 | tf_op jit(solution)/shard_map/ppermute | solution.py:250
  85.9 1.3 %collective-permute-start.21 = (bf16[1,64,1024]{2,1,0:T(8,128)(2,1)S(1)}, bf16[1,64,1024]{2,1,0:T(8,128)(2,1)S(1)}, u32[]{:S(2)}, u32[]{:S(2)}) collective-permute-start(bf16[1,64,1024]{2,1,0:T(8,128)(2,1)S(1)} %collective-permute-done.17.refs_3_), channel_id=1, source_target_pairs={{0,4},{4,0},{8,12},{12,8},{16,20},{20,16},{24,28},{28,24},{32,36},... | collective-permute-start | bytes 393224 | tf_op jit(solution)/shard_map/ppermute | solution.py:250
